TPU v7x, 32 devices: a whole 2x2x4 slice. The times are simulated.
32 devices in a mesh: group: 2 (over x), wide: 4 (over y, core), narrow: 4 (over z).
Axes of the slice: x: 2, y: 2, z: 4, core: 2. Of those that a mesh axis runs over, the one named last changes fastest.
Arguments:
- right_side: float32 [128, 256, 256], P(('group', 'wide'), 'narrow'), parts along dimension 0, may hold values from -4 to 4
- conduct_half: bfloat16 [128, 256, 256], P(('group', 'wide'), 'narrow'), parts along dimension 0, may hold values from 0.59765625 to 1.59375
- reaction_half: bfloat16 [128, 256, 256], P(('group', 'wide'), 'narrow'), parts along dimension 0, may hold values from 1 to 4
Outputs:
- solution: float32 [128, 256, 256], P(('group', 'wide'), 'narrow'), parts along dimension 0
- residual: float32 [128, 256, 256], P(('group', 'wide'), 'narrow'), parts along dimension 0
There are 2 independent parts, one for each index of `group`. A program takes and returns all parts, laid end to end along the dimension named above; each array names one. Nothing has to cross between parts.
All inputs are finite; a program needn't handle non-finite values.
Results may differ from a plain program's by a relative error of at most 0.02.
Values may be sent and summed in bfloat16 or wider, within the bound.
No kernel may reach another device: no remote copies, remote signals or barrier semaphores. Data moves between devices by JAX's collectives and lax.ppermute only.
A program may use at most 128 MiB of HBM per device.

v0:
```python
import jax
import jax.numpy as jnp
from jax import lax
from jax.experimental import pallas as pl
from jax.experimental.pallas import tpu as pltpu
from jax.sharding import PartitionSpec as P

S = 4
OUTER = 2
STEPS = S * OUTER

SCALE = 16.0
CENTER = 13.0
RATIO = CENTER / SCALE

LANES = 128
AXES = ("wide", "narrow")
VMEM = pl.BlockSpec(memory_space=pltpu.VMEM)
LIMIT = 56 * 1024 * 1024


def two_sum(a, b):
    total = a + b
    part = total - a
    return total, (a - (total - part)) + (b - part)


def fast_two_sum(a, b):
    total = a + b
    return total, b - (total - a)


def split(a):
    big = a * 4097.0
    high = big - (big - a)
    return high, a - high


def two_product(a, b):
    product = a * b
    a_high, a_low = split(a)
    b_high, b_low = split(b)
    error = ((a_high * b_high - product) + a_high * b_low + a_low * b_high) + a_low * b_low
    return product, error


def pair_add(a, b):
    total, error = two_sum(a[0], b[0])
    return fast_two_sum(total, error + (a[1] + b[1]))


def pair_scale(a, factor):
    product, error = two_product(a[0], factor)
    return fast_two_sum(product, error + a[1] * factor)


def send_kernel(b_ref, c_ref, r_ref, wm, wp, nm, np_, cmm, cmp, cpm, cpp):
    rows, columns = b_ref.shape[:2]
    h = STEPS

    def plane(i):
        field = b_ref[i]
        packed = r_ref[i].astype(jnp.float32) + c_ref[i].astype(jnp.float32) * (1.0 / 256.0)
        return (field, packed)

    def low(i, _):
        for k, value in enumerate(plane(i)):
            wm[k, i] = value
            nm[k, i] = value[:h]
            np_[k, i] = value[columns - h :]
            cmm[k, i] = value[:h]
            cmp[k, i] = value[columns - h :]
        return 0

    def middle(i, _):
        for k, value in enumerate(plane(i)):
            nm[k, i] = value[:h]
            np_[k, i] = value[columns - h :]
        return 0

    def high(i, _):
        at = i - (rows - h)
        for k, value in enumerate(plane(i)):
            wp[k, at] = value
            nm[k, i] = value[:h]
            np_[k, i] = value[columns - h :]
            cpm[k, at] = value[:h]
            cpp[k, at] = value[columns - h :]
        return 0

    lax.fori_loop(0, h, low, 0)
    lax.fori_loop(h, rows - h, middle, 0)
    lax.fori_loop(rows - h, rows, high, 0)


def messages(b, c, r):
    rows, columns, depth = b.shape
    h = STEPS
    shapes = (
        [(2, h, columns, depth)] * 2 + [(2, rows, h, depth)] * 2 + [(2, h, h, depth)] * 4
    )
    return pl.pallas_call(
        send_kernel,
        out_shape=[jax.ShapeDtypeStruct(s, jnp.float32) for s in shapes],
        in_specs=[VMEM] * 3,
        out_specs=[VMEM] * 8,
        compiler_params=pltpu.CompilerParams(vmem_limit_bytes=LIMIT),
    )(b, c, r)


def exchange(sent):
    wides, narrows = lax.axis_size("wide"), lax.axis_size("narrow")

    def moved(array, down, across):
        pairs = []
        for w in range(wides):
            for n in range(narrows):
                if 0 <= w + down < wides and 0 <= n + across < narrows:
                    pairs.append((w * narrows + n, (w + down) * narrows + n + across))
        return lax.ppermute(array, AXES, pairs)

    ways = [(-1, 0), (1, 0), (0, -1), (0, 1), (-1, -1), (-1, 1), (1, -1), (1, 1)]
    return [moved(array, *way) for array, way in zip(sent, ways)]


def basis_kernel(
    b_ref, c_ref, r_ref, wm, wp, nm, np_, cmm, cmp, cpm, cpp, f_ref, m_ref, u_even, u_odd, diag, coef
):
    rows, columns, depth = b_ref.shape
    h = STEPS
    tiles = (columns + 2 * h) // 8

    def place_u(buffer, i, y, value):
        count = value.shape[0]
        for half in range(2):
            buffer[i, half, pl.ds(8 + y, count), :] = value[:, half * LANES : (half + 1) * LANES]

    def outside(i, y, field, packed):
        count = field.shape[0]
        reaction = jnp.floor(packed * 128.0) * (1.0 / 128.0)
        conduct = (packed - reaction) * 256.0
        square = conduct * conduct
        place_u(u_even, i, y, conduct * field * 0.25)
        coef[i, pl.ds(y, count), :] = square * (1.0 / SCALE)
        diag[i, pl.ds(y, count), :] = ((reaction - CENTER) + 6.0 * square) * (1.0 / SCALE)

    def fill_low(i, _):
        outside(i, 0, cpp[0, i], cpp[1, i])
        outside(i, h, wp[0, i], wp[1, i])
        outside(i, h + columns, cpm[0, i], cpm[1, i])
        return 0

    def fill_high(i, _):
        at = i + h + rows
        outside(at, 0, cmp[0, i], cmp[1, i])
        outside(at, h, wm[0, i], wm[1, i])
        outside(at, h + columns, cmm[0, i], cmm[1, i])
        return 0

    def fill_middle(i, total):
        at = i + h
        outside(at, 0, np_[0, i], np_[1, i])
        outside(at, h + columns, nm[0, i], nm[1, i])
        field = b_ref[i]
        conduct = c_ref[i].astype(jnp.float32)
        reaction = r_ref[i].astype(jnp.float32)
        root = conduct * 0.25
        place_u(u_even, at, h, root * field)
        coef[at, pl.ds(h, columns), :] = root
        diag[at, pl.ds(h, columns), :] = (
            (reaction - CENTER) + 6.0 * (conduct * conduct)
        ) * (1.0 / SCALE)
        return total + tile_sum(field * field)

    def tile_sum(value):
        parts = [
            value[t * 8 : t * 8 + 8, half * LANES : (half + 1) * LANES]
            for t in range(value.shape[0] // 8)
            for half in range(value.shape[1] // LANES)
        ]
        return tree(parts)

    def tree(parts):
        while len(parts) > 1:
            parts = [sum(parts[k : k + 2][1:], parts[k]) for k in range(0, len(parts), 2)]
        return parts[0]

    zero = jnp.zeros((8, LANES), jnp.float32)
    lax.fori_loop(0, h, fill_low, 0)
    lax.fori_loop(0, h, fill_high, 0)
    moments = [lax.fori_loop(0, rows, fill_middle, zero)]

    lane = lax.broadcasted_iota(jnp.int32, (8, LANES), 1)
    first, last = lane == 0, lane == LANES - 1

    def neighbours(source, i, t):
        here = pl.ds(8 + 8 * t, 8)
        left, right = source[i, 0, here, :], source[i, 1, here, :]
        left_up, left_down = pltpu.roll(left, 1, 1), pltpu.roll(left, LANES - 1, 1)
        right_up, right_down = pltpu.roll(right, 1, 1), pltpu.roll(right, LANES - 1, 1)
        along = (
            jnp.where(first, 0.0, left_up) + jnp.where(last, right_down, left_down),
            jnp.where(first, left_up, right_up) + jnp.where(last, 0.0, right_down),
        )
        out = []
        for half in range(2):
            beside = source[i, half, pl.ds(7 + 8 * t, 8), :] + source[i, half, pl.ds(9 + 8 * t, 8), :]
            above = source[i - 1, half, here, :] + source[i + 1, half, here, :]
            out.append((along[half] + beside) + above)
        return (left, right), out

    for step in range(1, STEPS + 1):
        source, target = (u_even, u_odd) if step % 2 else (u_odd, u_even)

        def halo_tile(i, t, source=source, target=target):
            center, around = neighbours(source, i, t)
            for half in range(2):
                at = (i, pl.ds(8 * t, 8), pl.ds(half * LANES, LANES))
                target[i, half, pl.ds(8 + 8 * t, 8), :] = diag[at] * center[half] - coef[at] * around[half]

        def halo_plane(i, _):
            for t in range(tiles):
                halo_tile(i, t)
            return 0

        def inner_plane(i, carry, step=step, source=source, target=target):
            if step < STEPS:
                halo_tile(i, 0)
                halo_tile(i, tiles - 1)
            cross, own = [], []
            for t in range(1, tiles - 1):
                _, around = neighbours(source, i, t)
                for half in range(2):
                    lanes = pl.ds(half * LANES, LANES)
                    at = (i, pl.ds(8 * t, 8), lanes)
                    inside = (i - h, pl.ds(8 * t - h, 8), lanes)
                    before = b_ref[inside] if step == 1 else f_ref[(step - 2,) + inside]
                    root = coef[at]
                    value = diag[at] * before - root * around[half]
                    f_ref[(step - 1,) + inside] = value
                    if step < STEPS:
                        target[i, half, pl.ds(8 + 8 * t, 8), :] = root * value
                        own.append(value * value)
                    cross.append(value * before)
            total = carry[0] + tree(cross)
            return (total, carry[1] + tree(own) if own else carry[1])

        lax.fori_loop(step, h, halo_plane, 0)
        cross, own = lax.fori_loop(h, h + rows, inner_plane, (zero, zero))
        lax.fori_loop(h + rows, rows + 2 * h - step, halo_plane, 0)
        moments.append(cross)
        if step < STEPS:
            moments.append(own)

    def folded(high, low, shift, axis):
        total, error = two_sum(high, pltpu.roll(high, shift, axis))
        return total, (low + pltpu.roll(low, shift, axis)) + error

    sublane = lax.broadcasted_iota(jnp.int32, (8, LANES), 0)
    packed = []
    for group in range(2):
        highs, lows = zero, zero
        for k in range(8):
            high, low = moments[group * 8 + k], zero
            for shift in (4, 2, 1):
                high, low = folded(high, low, shift, 0)
            highs = jnp.where(sublane == k, high, highs)
            lows = jnp.where(sublane == k, low, lows)
        for shift in (64, 32, 16, 8, 4, 2, 1):
            highs, lows = folded(highs, lows, shift, 1)
        packed += [highs, lows]
    quarter = LANES // 4
    message = jnp.where(
        lane < quarter,
        packed[0],
        jnp.where(lane < 2 * quarter, packed[1], jnp.where(lane < 3 * quarter, packed[2], packed[3])),
    )
    for k in range(m_ref.shape[0]):
        m_ref[k] = message


def basis(b, c, r, received, peers):
    rows, columns, depth = b.shape
    h = STEPS
    wide, narrow = rows + 2 * h, columns + 2 * h
    return pl.pallas_call(
        basis_kernel,
        out_shape=[
            jax.ShapeDtypeStruct((STEPS, rows, columns, depth), jnp.float32),
            jax.ShapeDtypeStruct((peers, 8, LANES), jnp.float32),
        ],
        in_specs=[VMEM] * 11,
        out_specs=[VMEM] * 2,
        scratch_shapes=[
            pltpu.VMEM((wide, 2, narrow + 16, LANES), jnp.float32),
            pltpu.VMEM((wide, 2, narrow + 16, LANES), jnp.float32),
            pltpu.VMEM((wide, narrow, depth), jnp.float32),
            pltpu.VMEM((wide, narrow, depth), jnp.float32),
        ],
        compiler_params=pltpu.CompilerParams(vmem_limit_bytes=LIMIT),
    )(b, c, r, *received)


def coordinates(moment):
    shape = moment[0].shape
    count = shape[0]
    row = lax.broadcasted_iota(jnp.int32, shape, 0)

    def later(v):
        return jnp.where(row == count - 1, 0.0, pltpu.roll(v, count - 1, 0))

    def raised(v):
        return jnp.where(row == 0, 0.0, pltpu.roll(v, 1, 0))

    def spread(v):
        return jnp.broadcast_to(v, shape)

    residual = search = moment
    resid_coord = jnp.where(row == 0, 1.0, 0.0)
    search_coord = resid_coord
    sol_coord = jnp.zeros(shape, jnp.float32)
    ratio = jnp.full(shape, RATIO, jnp.float32)
    for i in range(STEPS):
        mapped = pair_add((later(search[0]), later(search[1])), pair_scale(search, ratio))
        old = residual[0][i : i + 1]
        length = old / mapped[0][i : i + 1]
        lengths = spread(length)
        residual = pair_add(residual, pair_scale(mapped, -lengths))
        grown = spread(-length * residual[0][i + 1 : i + 2] / old)
        search = pair_add(residual, pair_scale(search, grown))
        sol_coord = sol_coord + (lengths * (1.0 / SCALE)) * search_coord
        resid_coord = resid_coord - lengths * (raised(search_coord) + RATIO * search_coord)
        search_coord = resid_coord + grown * search_coord
    return sol_coord, resid_coord


def combine_kernel(m_ref, b_ref, f_ref, x_ref, r_ref, coord):
    @pl.when(pl.program_id(0) == 0)
    def _():
        total, error = m_ref[0], jnp.zeros((8, LANES), jnp.float32)
        for k in range(1, m_ref.shape[0]):
            total, lost = two_sum(total, m_ref[k])
            error = error + lost

        def lane(v, k):
            return jnp.broadcast_to(v[:, k * LANES // 4 : k * LANES // 4 + 1], (8, LANES))

        high = jnp.concatenate([lane(total, 0), lane(total, 2)], axis=0)
        low = jnp.concatenate(
            [lane(error, 0) + lane(total, 1), lane(error, 2) + lane(total, 3)], axis=0
        )
        sol_coord, resid_coord = coordinates(fast_two_sum(high, low))
        coord[0] = sol_coord
        coord[1] = resid_coord

    sol = [jnp.broadcast_to(coord[0, k : k + 1], (8, LANES)) for k in range(STEPS)]
    res = [jnp.broadcast_to(coord[1, k : k + 1], (8, LANES)) for k in range(STEPS + 1)]

    def plane(i, _):
        for t in range(b_ref.shape[1] // 8):
            for half in range(b_ref.shape[2] // LANES):
                at = (i, pl.ds(8 * t, 8), pl.ds(half * LANES, LANES))
                fields = [b_ref[at]] + [f_ref[(k,) + at] for k in range(STEPS)]
                x, r = sol[0] * fields[0], res[0] * fields[0]
                for k in range(1, STEPS + 1):
                    if k < STEPS:
                        x = x + sol[k] * fields[k]
                    r = r + res[k] * fields[k]
                x_ref[at] = x
                r_ref[at] = r
        return 0

    lax.fori_loop(0, b_ref.shape[0], plane, 0)


def combine(gathered, b, fields):
    rows, columns, depth = b.shape
    chunk = rows // 4
    block = pl.BlockSpec((chunk, columns, depth), lambda i: (i, 0, 0))
    return pl.pallas_call(
        combine_kernel,
        grid=(rows // chunk,),
        out_shape=[jax.ShapeDtypeStruct(b.shape, jnp.float32)] * 2,
        in_specs=[
            pl.BlockSpec(gathered.shape, lambda i: (0, 0, 0)),
            block,
            pl.BlockSpec((STEPS, chunk, columns, depth), lambda i: (0, i, 0, 0)),
        ],
        out_specs=[block, block],
        scratch_shapes=[pltpu.VMEM((2, 16, LANES), jnp.float32)],
        compiler_params=pltpu.CompilerParams(vmem_limit_bytes=LIMIT),
    )(gathered, b, fields)


def on_device(right_side, conduct_half, reaction_half):
    peers = lax.axis_size("wide") * lax.axis_size("narrow")
    received = exchange(messages(right_side, conduct_half, reaction_half))
    fields, moments = basis(right_side, conduct_half, reaction_half, received, peers)
    gathered = lax.all_to_all(moments, AXES, 0, 0, tiled=True)
    solution, residual = combine(gathered, right_side, fields)
    return (solution, residual)


def solution(mesh):
    placed = P(("group", "wide"), "narrow", None)
    return jax.shard_map(
        on_device,
        mesh=mesh,
        in_specs=(placed, placed, placed),
        out_specs=(placed, placed),
        check_vma=False,
    )
```

profile of v0, /device:TPU:0, one launch (start us, length us, event | category | flops | bytes accessed | tf_op | source)
XLA Modules:
  0.0 82.7 jit_solution(10776951738911171645)
XLA Ops:
  0.6 3.4 %shard_map.50 = (f32[2,8,64,256]{3,2,1,0:T(8,128)}, f32[2,8,64,256]{3,2,1,0:T(8,128)}, f32[2,16,8,256]{3,2,1,0:T(8,128)}, f32[2,16,8,256]{3,2,1,0:T(8,128)}, f32...) custom-call(f32[16,64,256]{2,1,0:T(8,128)} %b_ref.5, ...), custom_call_target="tpu_custom_call" | custom-call | tf_op jit(solution)/shard_map/pallas_call | solution.py:102
  4.1 1.3 %collective-permute-start = (f32[2,8,64,256]{3,2,1,0:T(8,128)}, f32[2,8,64,256]{3,2,1,0:T(8,128)S(1)}, u32[]{:S(2)}, u32[]{:S(2)}) collective-permute-start(f32[2,8,64,256]{3,2,1,0:T(8,128)} %get-tuple-element.12), channel_id=1, source_target_pairs={{4,0},{5,1},{6,2},{7,3},{8,4},{9,5},{10,6},{11,7},{12,8},{13,9},{1... | collective-permute-start | bytes 3145736 | tf_op jit(solution)/shard_map/ppermute | solution.py:120
  5.3 3.1 %collective-permute-start.1 = (f32[2,8,64,256]{3,2,1,0:T(8,128)}, f32[2,8,64,256]{3,2,1,0:T(8,128)S(1)}, u32[]{:S(2)}, u32[]{:S(2)}) collective-permute-start(f32[2,8,64,256]{3,2,1,0:T(8,128)} %get-tuple-element.13), channel_id=1, source_target_pairs={{0,4},{1,5},{2,6},{3,7},{4,8},{5,9},{6,10},{7,11},{8,12},{9,13},{1... | collective-permute-start | bytes 3145736 | tf_op jit(solution)/shard_map/ppermute | solution.py:120
  8.5 1.3 %collective-permute-start.4 = (f32[2,8,8,256]{3,2,1,0:T(8,128)}, f32[2,8,8,256]{3,2,1,0:T(8,128)S(1)}, u32[]{:S(2)}, u32[]{:S(2)}) collective-permute-start(f32[2,8,8,256]{3,2,1,0:T(8,128)} %get-tuple-element.16), channel_id=1, source_target_pairs={{5,0},{6,1},{7,2},{9,4},{10,5},{11,6},{13,8},{14,9},{15,10},{21,16... | collective-permute-start | bytes 393224 | tf_op jit(solution)/shard_map/ppermute | solution.py:120
  9.8 0.7 collective-permute-start.5
  10.4 0.7 collective-permute-start.6
  11.1 5.8 %collective-permute-done.4.cmm = f32[2,8,8,256]{3,2,1,0:T(8,128)S(1)} collective-permute-done((f32[2,8,8,256]{3,2,1,0:T(8,128)}, f32[2,8,8,256]{3,2,1,0:T(8,128)S(1)}, u32[]{:S(2)}, u32[]{:S(2)}) %collective-permute-start.4) | collective-permute-done | bytes 131104 | tf_op jit(solution)/shard_map/ppermute | solution.py:120
  16.9 1.3 %collective-permute-start.2 = (f32[2,16,8,256]{3,2,1,0:T(8,128)}, f32[2,16,8,256]{3,2,1,0:T(8,128)S(1)}, u32[]{:S(2)}, u32[]{:S(2)}) collective-permute-start(f32[2,16,8,256]{3,2,1,0:T(8,128)} %get-tuple-element.14), channel_id=1, source_target_pairs={{1,0},{2,1},{3,2},{5,4},{6,5},{7,6},{9,8},{10,9},{11,10},{13,12},{... | collective-permute-start | bytes 786440 | tf_op jit(solution)/shard_map/ppermute | solution.py:120
  18.2 0.0 collective-permute-done.5.cmp
  18.2 0.0 copy-start.5
  18.2 4.6 %collective-permute-start.3 = (f32[2,16,8,256]{3,2,1,0:T(8,128)}, f32[2,16,8,256]{3,2,1,0:T(8,128)S(1)}, u32[]{:S(2)}, u32[]{:S(2)}) collective-permute-start(f32[2,16,8,256]{3,2,1,0:T(8,128)} %get-tuple-element.15), channel_id=1, source_target_pairs={{0,1},{1,2},{2,3},{4,5},{5,6},{6,7},{8,9},{9,10},{10,11},{12,13},{... | collective-permute-start | bytes 786440 | tf_op jit(solution)/shard_map/ppermute | solution.py:120
  22.8 0.0 collective-permute-done.6.cpm
  22.8 0.0 copy-start.6
  22.8 5.1 %collective-permute-start.7 = (f32[2,8,8,256]{3,2,1,0:T(8,128)}, f32[2,8,8,256]{3,2,1,0:T(8,128)S(1)}, u32[]{:S(2)}, u32[]{:S(2)}) collective-permute-start(f32[2,8,8,256]{3,2,1,0:T(8,128)} %get-tuple-element.19), channel_id=1, source_target_pairs={{0,5},{1,6},{2,7},{4,9},{5,10},{6,11},{8,13},{9,14},{10,15},{16,21... | collective-permute-start | bytes 393224 | tf_op jit(solution)/shard_map/ppermute | solution.py:120
  27.9 4.2 %collective-permute-done.7.cpp = f32[2,8,8,256]{3,2,1,0:T(8,128)S(1)} collective-permute-done((f32[2,8,8,256]{3,2,1,0:T(8,128)}, f32[2,8,8,256]{3,2,1,0:T(8,128)S(1)}, u32[]{:S(2)}, u32[]{:S(2)}) %collective-permute-start.7) | collective-permute-done | bytes 131104 | tf_op jit(solution)/shard_map/ppermute | solution.py:120
  32.1 0.0 collective-permute-done.2.nm
  32.2 0.0 collective-permute-done.3.np_
  32.2 0.0 copy-start.3
  32.2 0.0 collective-permute-done.wm
  32.2 0.0 copy-start
  32.2 0.0 collective-permute-done.1.wp
  32.2 0.0 copy-done.4
  32.2 0.0 copy-done.5
  32.2 0.0 copy-done.6
  32.2 0.6 copy-done.7
  32.8 0.1 copy-done.2
  32.9 0.1 copy-done.3
  33.0 0.3 copy-done
  33.3 1.0 %copy-done.1 = f32[2,8,64,256]{3,2,1,0:T(8,128)} copy-done((f32[2,8,64,256]{3,2,1,0:T(8,128)}, f32[2,8,64,256]{3,2,1,0:T(8,128)S(1)}, u32[]{:S(2)}) %copy-start.1) | copy-done | bytes 1048600
  34.3 28.1 %shard_map.51 = (f32[8,16,64,256]{3,2,1,0:T(8,128)}, f32[16,8,128]{2,1,0:T(8,128)}) custom-call(f32[16,64,256]{2,1,0:T(8,128)} %b_ref.5, bf16[16,64,256]{2,1,0:T(8,128)(2,1)} %c_ref.3, bf16[16,64,256]{2,1,0:T(8,128)(2,1)} %r_ref.3, f32[2,8,64,256]{3,2,1,0:T(8,128)} %copy-done, f32[2,8,64,256]{3,2,1,0:T(8,128)} %copy-done.1, f32[2,16,8,256]{3,2,1,0:T(8,128)} %copy-done.2, ...), custom_call_target="tpu_custom_call" | custom-call | tf_op jit(solution)/shard_map/pallas_call | solution.py:286
  62.4 13.8 %all_to_all.5.m_ref = f32[16,8,128]{2,1,0:T(8,128)} all-to-all(f32[16,8,128]{2,1,0:T(8,128)} %get-tuple-element.20), channel_id=1, replica_groups=mesh['group'=2,'wide'=4,'narrow'=4] {'wide','narrow'}, dimensions={0} | all-to-all | bytes 131072 | tf_op jit(solution)/shard_map/all_to_all | solution.py:399
  76.2 6.5 %shard_map.52 = (f32[16,64,256]{2,1,0:T(8,128)}, f32[16,64,256]{2,1,0:T(8,128)}) custom-call(f32[16,8,128]{2,1,0:T(8,128)} %all_to_all.5.m_ref, f32[16,64,256]{2,1,0:T(8,128)} %b_ref.5, f32[8,16,64,256]{3,2,1,0:T(8,128)} %get-tuple-element.21.f_ref), custom_call_target="tpu_custom_call" | custom-call | tf_op jit(solution)/shard_map/pallas_call | solution.py:380
  (4 shorter events, 0.0 us)
Async XLA Ops:
  4.1 28.1 %collective-permute-start = (f32[2,8,64,256]{3,2,1,0:T(8,128)}, f32[2,8,64,256]{3,2,1,0:T(8,128)S(1)}, u32[]{:S(2)}, u32[]{:S(2)}) collective-permute-start(f32[2,8,64,256]{3,2,1,0:T(8,128)} %get-tuple-element.12), channel_id=1, source_target_pairs={{4,0},{5,1},{6,2},{7,3},{8,4},{9,5},{10,6},{11,7},{12,8},{13,9},{1... | collective-permute-start | bytes 3145736 | tf_op jit(solution)/shard_map/ppermute | solution.py:120
  5.3 26.8 %collective-permute-start.1 = (f32[2,8,64,256]{3,2,1,0:T(8,128)}, f32[2,8,64,256]{3,2,1,0:T(8,128)S(1)}, u32[]{:S(2)}, u32[]{:S(2)}) collective-permute-start(f32[2,8,64,256]{3,2,1,0:T(8,128)} %get-tuple-element.13), channel_id=1, source_target_pairs={{0,4},{1,5},{2,6},{3,7},{4,8},{5,9},{6,10},{7,11},{8,12},{9,13},{1... | collective-permute-start | bytes 3145736 | tf_op jit(solution)/shard_map/ppermute | solution.py:120
  8.5 8.5 %collective-permute-start.4 = (f32[2,8,8,256]{3,2,1,0:T(8,128)}, f32[2,8,8,256]{3,2,1,0:T(8,128)S(1)}, u32[]{:S(2)}, u32[]{:S(2)}) collective-permute-start(f32[2,8,8,256]{3,2,1,0:T(8,128)} %get-tuple-element.16), channel_id=1, source_target_pairs={{5,0},{6,1},{7,2},{9,4},{10,5},{11,6},{13,8},{14,9},{15,10},{21,16... | collective-permute-start | bytes 393224 | tf_op jit(solution)/shard_map/ppermute | solution.py:120
  9.8 8.5 %collective-permute-start.5 = (f32[2,8,8,256]{3,2,1,0:T(8,128)}, f32[2,8,8,256]{3,2,1,0:T(8,128)S(1)}, u32[]{:S(2)}, u32[]{:S(2)}) collective-permute-start(f32[2,8,8,256]{3,2,1,0:T(8,128)} %get-tuple-element.17), channel_id=1, source_target_pairs={{4,1},{5,2},{6,3},{8,5},{9,6},{10,7},{12,9},{13,10},{14,11},{20,17... | collective-permute-start | bytes 393224 | tf_op jit(solution)/shard_map/ppermute | solution.py:120
  10.4 12.4 %collective-permute-start.6 = (f32[2,8,8,256]{3,2,1,0:T(8,128)}, f32[2,8,8,256]{3,2,1,0:T(8,128)S(1)}, u32[]{:S(2)}, u32[]{:S(2)}) collective-permute-start(f32[2,8,8,256]{3,2,1,0:T(8,128)} %get-tuple-element.18), channel_id=1, source_target_pairs={{1,4},{2,5},{3,6},{5,8},{6,9},{7,10},{9,12},{10,13},{11,14},{17,20... | collective-permute-start | bytes 393224 | tf_op jit(solution)/shard_map/ppermute | solution.py:120
  16.9 15.3 %copy-start.4 = (f32[2,8,8,256]{3,2,1,0:T(8,128)}, f32[2,8,8,256]{3,2,1,0:T(8,128)S(1)}, u32[]{:S(2)}) copy-start(f32[2,8,8,256]{3,2,1,0:T(8,128)S(1)} %collective-permute-done.4.cmm) | copy-start | bytes 393220
  16.9 15.2 %collective-permute-start.2 = (f32[2,16,8,256]{3,2,1,0:T(8,128)}, f32[2,16,8,256]{3,2,1,0:T(8,128)S(1)}, u32[]{:S(2)}, u32[]{:S(2)}) collective-permute-start(f32[2,16,8,256]{3,2,1,0:T(8,128)} %get-tuple-element.14), channel_id=1, source_target_pairs={{1,0},{2,1},{3,2},{5,4},{6,5},{7,6},{9,8},{10,9},{11,10},{13,12},{... | collective-permute-start | bytes 786440 | tf_op jit(solution)/shard_map/ppermute | solution.py:120
  18.2 14.0 %copy-start.5 = (f32[2,8,8,256]{3,2,1,0:T(8,128)}, f32[2,8,8,256]{3,2,1,0:T(8,128)S(1)}, u32[]{:S(2)}) copy-start(f32[2,8,8,256]{3,2,1,0:T(8,128)S(1)} %collective-permute-done.5.cmp) | copy-start | bytes 393220
  18.2 13.9 %collective-permute-start.3 = (f32[2,16,8,256]{3,2,1,0:T(8,128)}, f32[2,16,8,256]{3,2,1,0:T(8,128)S(1)}, u32[]{:S(2)}, u32[]{:S(2)}) collective-permute-start(f32[2,16,8,256]{3,2,1,0:T(8,128)} %get-tuple-element.15), channel_id=1, source_target_pairs={{0,1},{1,2},{2,3},{4,5},{5,6},{6,7},{8,9},{9,10},{10,11},{12,13},{... | collective-permute-start | bytes 786440 | tf_op jit(solution)/shard_map/ppermute | solution.py:120
  22.8 9.4 %copy-start.6 = (f32[2,8,8,256]{3,2,1,0:T(8,128)}, f32[2,8,8,256]{3,2,1,0:T(8,128)S(1)}, u32[]{:S(2)}) copy-start(f32[2,8,8,256]{3,2,1,0:T(8,128)S(1)} %collective-permute-done.6.cpm) | copy-start | bytes 393220
  22.8 9.3 %collective-permute-start.7 = (f32[2,8,8,256]{3,2,1,0:T(8,128)}, f32[2,8,8,256]{3,2,1,0:T(8,128)S(1)}, u32[]{:S(2)}, u32[]{:S(2)}) collective-permute-start(f32[2,8,8,256]{3,2,1,0:T(8,128)} %get-tuple-element.19), channel_id=1, source_target_pairs={{0,5},{1,6},{2,7},{4,9},{5,10},{6,11},{8,13},{9,14},{10,15},{16,21... | collective-permute-start | bytes 393224 | tf_op jit(solution)/shard_map/ppermute | solution.py:120
  32.1 0.7 copy-start.7
  32.1 0.8 copy-start.2
  32.2 0.9 %copy-start.3 = (f32[2,16,8,256]{3,2,1,0:T(8,128)}, f32[2,16,8,256]{3,2,1,0:T(8,128)S(1)}, u32[]{:S(2)}) copy-start(f32[2,16,8,256]{3,2,1,0:T(8,128)S(1)} %collective-permute-done.3.np_) | copy-start | bytes 786436
  32.2 1.1 %copy-start = (f32[2,8,64,256]{3,2,1,0:T(8,128)}, f32[2,8,64,256]{3,2,1,0:T(8,128)S(1)}, u32[]{:S(2)}) copy-start(f32[2,8,64,256]{3,2,1,0:T(8,128)S(1)} %collective-permute-done.wm) | copy-start | bytes 3145732
  33.3 1.0 %copy-start.1 = (f32[2,8,64,256]{3,2,1,0:T(8,128)}, f32[2,8,64,256]{3,2,1,0:T(8,128)S(1)}, u32[]{:S(2)}) copy-start(f32[2,8,64,256]{3,2,1,0:T(8,128)S(1)} %collective-permute-done.1.wp) | copy-start | bytes 3145732
where the time goes:
time: 83.2 us; the launch traced here: 82.7 us
  Pallas kernels  38.1 us (46%)
  starting transfers between devices  17.9 us (22%)
  blocking collectives  13.8 us (17%)
  waiting for transfers between devices  10.1 us (12%)
  local copies, waits for them, and re-layouts  2.09 us (3%)
    pallas_call x1, Pallas kernels, basis(): pl.pallas_call(basis_kernel, out_shape=[jax.ShapeDtypeStruct((STEPS, rows...  28.1 us
    ppermute x8, starting transfers between devices, moved(): return lax.ppermute(array, AXES, pairs)  17.9 us
    all_to_all x1, blocking collectives, on_device(): gathered = lax.all_to_all(moments, AXES, 0, 0, tiled=True)  13.8 us
    ppermute x8, waiting for transfers between devices, moved(): return lax.ppermute(array, AXES, pairs)  10.1 us
    pallas_call x1, Pallas kernels, combine(): pl.pallas_call(combine_kernel, grid=(rows // chunk,), out_shape=[jax.Shap...  6.55 us
    pallas_call x1, Pallas kernels, messages(): pl.pallas_call(send_kernel, out_shape=[jax.ShapeDtypeStruct(s, jnp.float3...  3.43 us
    unnamed x16, local copies, waits for them, and re-layouts  2.09 us
  transfers between devices with their start and end apart: 8, of which 2 were waited for; matrix products, arithmetic and copies ran while one was open for 0% of the time, Pallas kernels for 0%

commit v1 on v0

v1 whole, which is shorter than its diff:
```python
import jax
import jax.numpy as jnp
from jax import lax
from jax.experimental import pallas as pl
from jax.experimental.pallas import tpu as pltpu
from jax.sharding import PartitionSpec as P

S = 4
OUTER = 2
STEPS = S * OUTER

SCALE = 13.0
CENTER = SCALE
ROOT = SCALE**-0.5

LANES = 128
AXES = ("wide", "narrow")
VMEM = pl.BlockSpec(memory_space=pltpu.VMEM)
ANY = pl.BlockSpec(memory_space=pl.ANY)
MIB = 1024 * 1024


def two_sum(a, b):
    total = a + b
    part = total - a
    return total, (a - (total - part)) + (b - part)


def fast_two_sum(a, b):
    total = a + b
    return total, b - (total - a)


def split(a):
    big = a * 4097.0
    high = big - (big - a)
    return high, a - high


def two_product(a, b):
    product = a * b
    a_high, a_low = split(a)
    b_high, b_low = split(b)
    error = ((a_high * b_high - product) + a_high * b_low + a_low * b_high) + a_low * b_low
    return product, error


def pair_add(a, b):
    total, error = two_sum(a[0], b[0])
    return fast_two_sum(total, error + (a[1] + b[1]))


def pair_scale(a, factor):
    product, error = two_product(a[0], factor)
    return fast_two_sum(product, error + a[1] * factor)


def sides():
    out = []
    for axis in AXES:
        even = lax.rem(lax.axis_index(axis), 2) == 0
        out.append((even, jnp.logical_not(even)))
    return out


def send_kernel(b_ref, c_ref, r_ref, *refs):
    (w_out, n_out, c_out), pack = (refs[:2], refs[2:4], refs[4:8]), refs[8]
    rows, columns = b_ref.shape[:2]
    h = STEPS
    wide, narrow = sides()
    top = [jnp.where(up, rows - h, 0) for up in wide]
    left = [pl.multiple_of(jnp.where(up, columns - h, 0), 8) for up in narrow]

    def code(i, _):
        pack[i] = r_ref[i].astype(jnp.float32) + c_ref[i].astype(jnp.float32) * (1.0 / 256.0)
        return 0

    def edges(i, _):
        for k, source in enumerate((b_ref, pack)):
            for side in range(2):
                n_out[side][k, i] = source[i, pl.ds(left[side], h), :]
        return 0

    def layers(i, _):
        for k, source in enumerate((b_ref, pack)):
            for a in range(2):
                w_out[a][k, i] = source[top[a] + i]
                for side in range(2):
                    c_out[2 * a + side][k, i] = source[top[a] + i, pl.ds(left[side], h), :]
        return 0

    lax.fori_loop(0, rows, code, 0)
    lax.fori_loop(0, rows, edges, 0)
    lax.fori_loop(0, h, layers, 0)


def messages(b, c, r):
    rows, columns, depth = b.shape
    h = STEPS
    shapes = (
        [(2, h, columns, depth)] * 2 + [(2, rows, h, depth)] * 2 + [(2, h, h, depth)] * 4
    )
    return pl.pallas_call(
        send_kernel,
        out_shape=[jax.ShapeDtypeStruct(s, jnp.float32) for s in shapes],
        in_specs=[VMEM] * 3,
        out_specs=[VMEM] * 8,
        scratch_shapes=[pltpu.VMEM(b.shape, jnp.float32)],
        compiler_params=pltpu.CompilerParams(vmem_limit_bytes=16 * MIB),
    )(b, c, r)


def exchange(sent):
    wides, narrows = lax.axis_size("wide"), lax.axis_size("narrow")

    def partner(index, pairing):
        return index if pairing is None else index + (1 if index % 2 == pairing else -1)

    def swapped(array, across, along):
        pairs = []
        for w in range(wides):
            for n in range(narrows):
                to_w, to_n = partner(w, across), partner(n, along)
                if 0 <= to_w < wides and 0 <= to_n < narrows:
                    pairs.append((w * narrows + n, to_w * narrows + to_n))
        return lax.ppermute(array, AXES, pairs)

    ways = [(0, None), (1, None), (None, 0), (None, 1), (0, 0), (0, 1), (1, 0), (1, 1)]
    return [swapped(array, *way) for array, way in zip(sent, ways)]


def basis_kernel(b_ref, c_ref, r_ref, *refs):
    (w_in, n_in, c_in), refs = (refs[:2], refs[2:4], refs[4:8]), refs[8:]
    out, m_ref, refs = refs[:STEPS], refs[STEPS], refs[STEPS + 1 :]
    field, (u_even, u_odd, diag, coef, done) = refs[:STEPS], refs[STEPS:]
    rows, columns, depth = b_ref.shape
    h = STEPS
    tiles = (columns + 2 * h) // 8
    wide, narrow = sides()
    top = [jnp.where(up, rows + h, 0) for up in wide]
    left = [pl.multiple_of(jnp.where(up, columns + h, 0), 8) for up in narrow]

    def place_u(buffer, i, y, value):
        count = value.shape[0]
        for half in range(2):
            buffer[i, half, pl.ds(y + 8, count), :] = value[:, half * LANES : (half + 1) * LANES]

    def outside(i, y, value, packed):
        count = value.shape[0]
        reaction = jnp.floor(packed * 128.0) * (1.0 / 128.0)
        conduct = (packed - reaction) * 256.0
        root = conduct * ROOT
        place_u(u_even, i, y, root * value)
        coef[i, pl.ds(y, count), :] = root * root
        diag[i, pl.ds(y, count), :] = ((reaction - CENTER) + 6.0 * (conduct * conduct)) * (1.0 / SCALE)

    def fill_outer(i, _):
        for a in range(2):
            at = top[a] + i
            outside(at, h, w_in[a][0, i], w_in[a][1, i])
            for side in range(2):
                corner = c_in[2 * a + side]
                outside(at, left[side], corner[0, i], corner[1, i])
        return 0

    def fill_middle(i, total):
        at = i + h
        for side in range(2):
            outside(at, left[side], n_in[side][0, i], n_in[side][1, i])
        value = b_ref[i]
        conduct = c_ref[i].astype(jnp.float32)
        reaction = r_ref[i].astype(jnp.float32)
        root = conduct * ROOT
        place_u(u_even, at, h, root * value)
        coef[at, pl.ds(h, columns), :] = root
        diag[at, pl.ds(h, columns), :] = (
            (reaction - CENTER) + 6.0 * (conduct * conduct)
        ) * (1.0 / SCALE)
        square = value * value
        return total + tree(
            [
                square[t * 8 : t * 8 + 8, half * LANES : (half + 1) * LANES]
                for t in range(columns // 8)
                for half in range(2)
            ]
        )

    def tree(parts):
        while len(parts) > 1:
            parts = [
                parts[k] + parts[k + 1] if k + 1 < len(parts) else parts[k]
                for k in range(0, len(parts), 2)
            ]
        return parts[0]

    zero = jnp.zeros((8, LANES), jnp.float32)
    lax.fori_loop(0, h, fill_outer, 0)
    moments = [lax.fori_loop(0, rows, fill_middle, zero)]

    lane = lax.broadcasted_iota(jnp.int32, (8, LANES), 1)
    first, last = lane == 0, lane == LANES - 1

    def advance(step, base, inner, halo, carry):
        source, target = (u_even, u_odd) if step % 2 else (u_odd, u_even)
        before = b_ref if step == 1 else field[step - 2]
        now = field[step - 1]
        planes = [(base, d, True) for d in range(inner)] + [(i, 0, False) for i in halo]
        cross, own = [], []
        for t in range(tiles):
            edge = t in (0, tiles - 1)
            loaded = {}

            def load(start, d, half):
                key = (id(start), d, half)
                if key not in loaded:
                    loaded[key] = source[start + d, half, pl.ds(8 * t + 8, 8), :]
                return loaded[key]

            for start, d, inside in planes:
                if edge and step == STEPS:
                    continue
                i = start + d
                left_half, right_half = load(start, d, 0), load(start, d, 1)
                left_up, left_down = pltpu.roll(left_half, 1, 1), pltpu.roll(left_half, LANES - 1, 1)
                right_up, right_down = pltpu.roll(right_half, 1, 1), pltpu.roll(right_half, LANES - 1, 1)
                along = (
                    jnp.where(first, 0.0, left_up) + jnp.where(last, right_down, left_down),
                    jnp.where(first, left_up, right_up) + jnp.where(last, 0.0, right_down),
                )
                for half in range(2):
                    beside = (
                        source[i, half, pl.ds(8 * t + 7, 8), :]
                        + source[i, half, pl.ds(8 * t + 9, 8), :]
                    )
                    across = load(start, d - 1, half) + load(start, d + 1, half)
                    around = (beside + across) + along[half]
                    lanes = pl.ds(half * LANES, LANES)
                    at = (i, pl.ds(8 * t, 8), lanes)
                    if inside and not edge:
                        here = (i - h, pl.ds(8 * t - h, 8), lanes)
                        old = before[here]
                        root = coef[at]
                        value = diag[at] * old - root * around
                        now[here] = value
                        cross.append(value * old)
                        if step < STEPS:
                            target[i, half, pl.ds(8 * t + 8, 8), :] = root * value
                            own.append(value * value)
                    else:
                        center = (left_half, right_half)[half]
                        target[i, half, pl.ds(8 * t + 8, 8), :] = diag[at] * center - coef[at] * around
        first_sum, second_sum = carry
        return first_sum + tree(cross), (second_sum + tree(own) if own else second_sum)

    copies = []
    for step in range(1, STEPS + 1):
        outer = h - step
        quads, rest = divmod(rows - 2 * outer, 4)

        def mixed(m, carry, step=step):
            return advance(step, 2 * m + h, 2, (m + step, m + h + rows), carry)

        def plain(m, carry, step=step, outer=outer):
            return advance(step, 4 * m + h + 2 * outer, 4, (), carry)

        carry = lax.fori_loop(0, outer, mixed, (zero, zero))
        carry = lax.fori_loop(0, quads, plain, carry)
        if rest:
            carry = advance(step, h + rows - rest, rest, (), carry)
        moments += carry if step < STEPS else carry[:1]
        copy = pltpu.make_async_copy(field[step - 1], out[step - 1], done.at[step - 1])
        copy.start()
        copies.append(copy)

    def folded(high, low, shift, axis):
        total, error = two_sum(high, pltpu.roll(high, shift, axis))
        return total, (low + pltpu.roll(low, shift, axis)) + error

    sublane = lax.broadcasted_iota(jnp.int32, (8, LANES), 0)
    packed = []
    for group in range(2):
        highs, lows = zero, zero
        for k in range(8):
            high, low = moments[group * 8 + k], zero
            for shift in (4, 2, 1):
                high, low = folded(high, low, shift, 0)
            highs = jnp.where(sublane == k, high, highs)
            lows = jnp.where(sublane == k, low, lows)
        for shift in (64, 32, 16, 8, 4, 2, 1):
            highs, lows = folded(highs, lows, shift, 1)
        packed += [highs, lows]
    quarter = LANES // 4
    message = jnp.where(
        lane < quarter,
        packed[0],
        jnp.where(lane < 2 * quarter, packed[1], jnp.where(lane < 3 * quarter, packed[2], packed[3])),
    )
    for k in range(m_ref.shape[0]):
        m_ref[k] = message
    for copy in copies:
        copy.wait()


def basis(b, c, r, received, peers):
    rows, columns, depth = b.shape
    h = STEPS
    wide, narrow = rows + 2 * h, columns + 2 * h
    outs = pl.pallas_call(
        basis_kernel,
        out_shape=[jax.ShapeDtypeStruct(b.shape, jnp.float32)] * STEPS
        + [jax.ShapeDtypeStruct((peers, 8, LANES), jnp.float32)],
        in_specs=[VMEM] * 11,
        out_specs=[ANY] * STEPS + [VMEM],
        scratch_shapes=[pltpu.VMEM(b.shape, jnp.float32)] * STEPS
        + [pltpu.VMEM((wide, 2, narrow + 16, LANES), jnp.float32)] * 2
        + [pltpu.VMEM((wide, narrow, depth), jnp.float32)] * 2
        + [pltpu.SemaphoreType.DMA((STEPS,))],
        compiler_params=pltpu.CompilerParams(vmem_limit_bytes=34 * MIB),
    )(b, c, r, *received)
    return outs[:STEPS], outs[STEPS]


def coordinates(moment):
    shape = moment[0].shape
    count = shape[0]
    row = lax.broadcasted_iota(jnp.int32, shape, 0)

    def later(v):
        return jnp.where(row == count - 1, 0.0, pltpu.roll(v, count - 1, 0))

    def raised(v):
        return jnp.where(row == 0, 0.0, pltpu.roll(v, 1, 0))

    def spread(v):
        return jnp.broadcast_to(v, shape)

    residual = search = moment
    resid_coord = jnp.where(row == 0, 1.0, 0.0)
    search_coord = resid_coord
    sol_coord = jnp.zeros(shape, jnp.float32)
    for i in range(STEPS):
        mapped = pair_add((later(search[0]), later(search[1])), search)
        old = residual[0][i : i + 1]
        length = old / mapped[0][i : i + 1]
        lengths = spread(length)
        residual = pair_add(residual, pair_scale(mapped, -lengths))
        grown = spread(-length * residual[0][i + 1 : i + 2] / old)
        search = pair_add(residual, pair_scale(search, grown))
        sol_coord = sol_coord + (lengths * (1.0 / SCALE)) * search_coord
        resid_coord = resid_coord - lengths * (raised(search_coord) + search_coord)
        search_coord = resid_coord + grown * search_coord
    return sol_coord, resid_coord


def combine_kernel(m_ref, b_ref, *refs):
    sources, (x_ref, r_ref), refs = refs[:STEPS], refs[STEPS : STEPS + 2], refs[STEPS + 2 :]
    field, done = refs[:STEPS], refs[STEPS]
    copies = []
    for k in range(STEPS):
        copies.append(pltpu.make_async_copy(sources[k], field[k], done.at[k]))
        copies[k].start()

    total, error = m_ref[0], jnp.zeros((8, LANES), jnp.float32)
    for k in range(1, m_ref.shape[0]):
        total, lost = two_sum(total, m_ref[k])
        error = error + lost

    def lane(v, k):
        return jnp.broadcast_to(v[:, k * LANES // 4 : k * LANES // 4 + 1], (8, LANES))

    high = jnp.concatenate([lane(total, 0), lane(total, 2)], axis=0)
    low = jnp.concatenate(
        [lane(error, 0) + lane(total, 1), lane(error, 2) + lane(total, 3)], axis=0
    )
    sol_coord, resid_coord = coordinates(fast_two_sum(high, low))
    sol = [jnp.broadcast_to(sol_coord[k : k + 1], (8, LANES)) for k in range(STEPS)]
    res = [jnp.broadcast_to(resid_coord[k : k + 1], (8, LANES)) for k in range(STEPS + 1)]
    for copy in copies:
        copy.wait()

    def plane(i, _):
        for t in range(b_ref.shape[1] // 8):
            for half in range(b_ref.shape[2] // LANES):
                at = (i, pl.ds(8 * t, 8), pl.ds(half * LANES, LANES))
                fields = [b_ref[at]] + [f[at] for f in field]
                x, r = sol[0] * fields[0], res[0] * fields[0]
                for k in range(1, STEPS + 1):
                    if k < STEPS:
                        x = x + sol[k] * fields[k]
                    r = r + res[k] * fields[k]
                x_ref[at] = x
                r_ref[at] = r
        return 0

    lax.fori_loop(0, b_ref.shape[0], plane, 0)


def combine(gathered, b, fields):
    return pl.pallas_call(
        combine_kernel,
        out_shape=[jax.ShapeDtypeStruct(b.shape, jnp.float32)] * 2,
        in_specs=[VMEM] * 2 + [ANY] * STEPS,
        out_specs=[VMEM] * 2,
        scratch_shapes=[pltpu.VMEM(b.shape, jnp.float32)] * STEPS
        + [pltpu.SemaphoreType.DMA((STEPS,))],
        compiler_params=pltpu.CompilerParams(vmem_limit_bytes=20 * MIB),
    )(gathered, b, *fields)


def on_device(right_side, conduct_half, reaction_half):
    peers = lax.axis_size("wide") * lax.axis_size("narrow")
    received = exchange(messages(right_side, conduct_half, reaction_half))
    fields, moments = basis(right_side, conduct_half, reaction_half, received, peers)
    gathered = lax.all_to_all(moments, AXES, 0, 0, tiled=True)
    solution, residual = combine(gathered, right_side, fields)
    return (solution, residual)


def solution(mesh):
    placed = P(("group", "wide"), "narrow", None)
    return jax.shard_map(
        on_device,
        mesh=mesh,
        in_specs=(placed, placed, placed),
        out_specs=(placed, placed),
        check_vma=False,
    )
```

time: 83.2 us -> 57.6 us (0.69)
  Pallas kernels: 38.1 us -> 17.9 us
  starting transfers between devices: 17.9 us -> 9.88 us
  blocking collectives: 13.8 us -> 17.5 us
  waiting for transfers between devices: 10.1 us -> 7.92 us
  local copies, waits for them, and re-layouts: 2.09 us -> 3.31 us
    pallas_call x2, Pallas kernels: 34.7 us -> 17.3 us  [the longest x1 13.7 us: basis(): pl.pallas_call(basis_kernel, out_shape=[jax.ShapeDtypeStruct(b.shape, jnp...]
    ppermute x8, starting transfers between devices: 17.9 us -> 9.88 us  [swapped(): return lax.ppermute(array, AXES, pairs)]
    all_to_all x1, blocking collectives: 13.8 us -> 17.5 us  [on_device(): gathered = lax.all_to_all(moments, AXES, 0, 0, tiled=True)]
    pallas_call x1, Pallas kernels: 3.43 us -> 0.56 us  [messages(): pl.pallas_call(send_kernel, out_shape=[jax.ShapeDtypeStruct(s, jnp.float3...]
    ppermute x8, waiting for transfers between devices: 10.1 us -> 7.92 us  [swapped(): return lax.ppermute(array, AXES, pairs)]
    unnamed x16 -> x12, local copies, waits for them, and re-layouts: 2.09 us -> 3.31 us
where the time goes in v1:
time: 57.6 us; the launch traced here: 57.2 us
  Pallas kernels  17.9 us (31%)
  blocking collectives  17.5 us (30%)
  starting transfers between devices  9.88 us (17%)
  waiting for transfers between devices  7.92 us (14%)
  local copies, waits for them, and re-layouts  3.31 us (6%)
  between operations  0.75 us (1%)
    all_to_all x1, blocking collectives, on_device(): gathered = lax.all_to_all(moments, AXES, 0, 0, tiled=True)  17.5 us
    pallas_call x1, Pallas kernels, basis(): pl.pallas_call(basis_kernel, out_shape=[jax.ShapeDtypeStruct(b.shape, jnp...  13.7 us
    ppermute x8, starting transfers between devices, swapped(): return lax.ppermute(array, AXES, pairs)  9.88 us
    ppermute x8, waiting for transfers between devices, swapped(): return lax.ppermute(array, AXES, pairs)  7.92 us
    pallas_call x1, Pallas kernels, combine(): pl.pallas_call(combine_kernel, out_shape=[jax.ShapeDtypeStruct(b.shape, j...  3.67 us
    unnamed x12, local copies, waits for them, and re-layouts  3.31 us
  transfers between devices with their start and end apart: 8, of which 2 were waited for; matrix products, arithmetic and copies ran while one was open for 0% of the time, Pallas kernels for 0%

profile of v1, /device:TPU:0, one launch (start us, length us, event | category | flops | bytes accessed | tf_op | source)
XLA Modules:
  0.0 57.2 jit_solution(6021936634065004200)
XLA Ops:
  0.6 0.0 copy-start
  0.6 1.2 %copy-done = f32[16,64,256]{2,1,0:T(8,128)S(1)} copy-done((f32[16,64,256]{2,1,0:T(8,128)S(1)}, f32[16,64,256]{2,1,0:T(8,128)}, u32[]{:S(2)}) %copy-start) | copy-done | bytes 1048600
  1.9 0.0 copy-start.2
  1.9 1.0 %copy-done.2 = bf16[16,64,256]{2,1,0:T(8,128)(2,1)S(1)} copy-done((bf16[16,64,256]{2,1,0:T(8,128)(2,1)S(1)}, bf16[16,64,256]{2,1,0:T(8,128)(2,1)}, u32[]{:S(2)}) %copy-start.2) | copy-done | bytes 524312
  2.9 0.0 copy-start.4
  2.9 1.0 %copy-done.4 = bf16[16,64,256]{2,1,0:T(8,128)(2,1)S(1)} copy-done((bf16[16,64,256]{2,1,0:T(8,128)(2,1)S(1)}, bf16[16,64,256]{2,1,0:T(8,128)(2,1)}, u32[]{:S(2)}) %copy-start.4) | copy-done | bytes 524312
  3.9 0.0 copy-start.1
  3.9 0.0 copy-start.3
  3.9 0.0 copy-start.5
  3.9 0.6 shard_map.50
  4.5 0.5 collective-permute-start
  5.0 0.7 %collective-permute-start.1 = (f32[2,8,64,256]{3,2,1,0:T(8,128)S(1)}, f32[2,8,64,256]{3,2,1,0:T(8,128)S(1)}, u32[]{:S(2)}, u32[]{:S(2)}) collective-permute-start(f32[2,8,64,256]{3,2,1,0:T(8,128)S(1)} %get-tuple-element.20), channel_id=1, source_target_pairs={{4,8},{5,9},{6,10},{7,11},{8,4},{9,5},{10,6},{11,7},{20,24},{21,25... | collective-permute-start | bytes 3145736 | tf_op jit(solution)/shard_map/ppermute | solution.py:126
  5.8 5.1 %collective-permute-start.4 = (f32[2,8,8,256]{3,2,1,0:T(8,128)S(1)}, f32[2,8,8,256]{3,2,1,0:T(8,128)S(1)}, u32[]{:S(2)}, u32[]{:S(2)}) collective-permute-start(f32[2,8,8,256]{3,2,1,0:T(8,128)S(1)} %get-tuple-element.23), channel_id=1, source_target_pairs={{0,5},{1,4},{2,7},{3,6},{4,1},{5,0},{6,3},{7,2},{8,13},{9,12},{10,... | collective-permute-start | bytes 393224 | tf_op jit(solution)/shard_map/ppermute | solution.py:126
  10.8 0.7 %collective-permute-start.5 = (f32[2,8,8,256]{3,2,1,0:T(8,128)S(1)}, f32[2,8,8,256]{3,2,1,0:T(8,128)S(1)}, u32[]{:S(2)}, u32[]{:S(2)}) collective-permute-start(f32[2,8,8,256]{3,2,1,0:T(8,128)S(1)} %get-tuple-element.24), channel_id=1, source_target_pairs={{1,6},{2,5},{5,2},{6,1},{9,14},{10,13},{13,10},{14,9},{17,22},{18,... | collective-permute-start | bytes 393224 | tf_op jit(solution)/shard_map/ppermute | solution.py:126
  11.5 0.7 %collective-permute-start.6 = (f32[2,8,8,256]{3,2,1,0:T(8,128)S(1)}, f32[2,8,8,256]{3,2,1,0:T(8,128)S(1)}, u32[]{:S(2)}, u32[]{:S(2)}) collective-permute-start(f32[2,8,8,256]{3,2,1,0:T(8,128)S(1)} %get-tuple-element.25), channel_id=1, source_target_pairs={{4,9},{5,8},{6,11},{7,10},{8,5},{9,4},{10,7},{11,6},{20,25},{21,24... | collective-permute-start | bytes 393224 | tf_op jit(solution)/shard_map/ppermute | solution.py:126
  12.2 2.0 %collective-permute-done.4.refs_4_ = f32[2,8,8,256]{3,2,1,0:T(8,128)S(1)} collective-permute-done((f32[2,8,8,256]{3,2,1,0:T(8,128)S(1)}, f32[2,8,8,256]{3,2,1,0:T(8,128)S(1)}, u32[]{:S(2)}, u32[]{:S(2)}) %collective-permute-start.4) | collective-permute-done | bytes 131104 | tf_op jit(solution)/shard_map/ppermute | solution.py:126
  14.2 0.9 %collective-permute-start.2 = (f32[2,16,8,256]{3,2,1,0:T(8,128)S(1)}, f32[2,16,8,256]{3,2,1,0:T(8,128)S(1)}, u32[]{:S(2)}, u32[]{:S(2)}) collective-permute-start(f32[2,16,8,256]{3,2,1,0:T(8,128)S(1)} %get-tuple-element.21), channel_id=1, source_target_pairs={{0,1},{1,0},{2,3},{3,2},{4,5},{5,4},{6,7},{7,6},{8,9},{9,8},{10,11... | collective-permute-start | bytes 786440 | tf_op jit(solution)/shard_map/ppermute | solution.py:126
  15.1 0.0 collective-permute-done.5.refs_5_
  15.1 0.7 %collective-permute-start.3 = (f32[2,16,8,256]{3,2,1,0:T(8,128)S(1)}, f32[2,16,8,256]{3,2,1,0:T(8,128)S(1)}, u32[]{:S(2)}, u32[]{:S(2)}) collective-permute-start(f32[2,16,8,256]{3,2,1,0:T(8,128)S(1)} %get-tuple-element.22), channel_id=1, source_target_pairs={{1,2},{2,1},{5,6},{6,5},{9,10},{10,9},{13,14},{14,13},{17,18},{18,... | collective-permute-start | bytes 786440 | tf_op jit(solution)/shard_map/ppermute | solution.py:126
  15.8 0.0 collective-permute-done.6.refs_6_
  15.8 0.7 %collective-permute-start.7 = (f32[2,8,8,256]{3,2,1,0:T(8,128)S(1)}, f32[2,8,8,256]{3,2,1,0:T(8,128)S(1)}, u32[]{:S(2)}, u32[]{:S(2)}) collective-permute-start(f32[2,8,8,256]{3,2,1,0:T(8,128)S(1)} %get-tuple-element.26), channel_id=1, source_target_pairs={{5,10},{6,9},{9,6},{10,5},{21,26},{22,25},{25,22},{26,21}} | collective-permute-start | bytes 393224 | tf_op jit(solution)/shard_map/ppermute | solution.py:126
  16.5 0.0 collective-permute-done.7.refs_7_
  16.5 5.9 %collective-permute-done.2.refs_2_ = f32[2,16,8,256]{3,2,1,0:T(8,128)S(1)} collective-permute-done((f32[2,16,8,256]{3,2,1,0:T(8,128)S(1)}, f32[2,16,8,256]{3,2,1,0:T(8,128)S(1)}, u32[]{:S(2)}, u32[]{:S(2)}) %collective-permute-start.2) | collective-permute-done | bytes 262176 | tf_op jit(solution)/shard_map/ppermute | solution.py:126
  22.4 0.0 collective-permute-done.3.refs_3_
  22.4 0.0 collective-permute-done.refs_0_
  22.4 0.0 collective-permute-done.1.refs_1_
  22.4 0.0 copy-done.1
  22.4 0.0 copy-done.3
  22.4 0.0 copy-done.5
  22.4 13.7 %shard_map.51 = (f32[16,64,256]{2,1,0:T(8,128)S(1)}, f32[16,64,256]{2,1,0:T(8,128)S(1)}, f32[16,64,256]{2,1,0:T(8,128)S(1)}, f32[16,64,256]{2,1,0:T(8,128)S(1)},...) custom-call(f32[16,64,256]{2,1,0:T(8,128)S(1)} %copy-done.1, ...), custom_call_target="tpu_custom_call" | custom-call | tf_op jit(solution)/shard_map/pallas_call | solution.py:308
  36.1 17.5 %all_to_all.5.m_ref = f32[16,8,128]{2,1,0:T(8,128)S(1)} all-to-all(f32[16,8,128]{2,1,0:T(8,128)S(1)} %get-tuple-element.27), channel_id=1, replica_groups=mesh['group'=2,'wide'=4,'narrow'=4] {'wide','narrow'}, dimensions={0} | all-to-all | bytes 131072 | tf_op jit(solution)/shard_map/all_to_all | solution.py:414
  53.6 3.7 %shard_map.52 = (f32[16,64,256]{2,1,0:T(8,128)}, f32[16,64,256]{2,1,0:T(8,128)}) custom-call(f32[16,8,128]{2,1,0:T(8,128)S(1)} %all_to_all.5.m_ref, f32[16,64,256]{2,1,0:T(8,128)S(1)} %copy-done.1, f32[16,64,256]{2,1,0:T(8,128)S(1)} %get-tuple-element.28.refs_0_, f32[16,64,256]{2,1,0:T(8,128)S(1)} %get-tuple-element.29.refs_1_, ...), custom_call_target="tpu_custom_call" | custom-call | tf_op jit(solution)/shard_map/pallas_call | solution.py:399
Async XLA Ops:
  0.6 1.2 %copy-start = (f32[16,64,256]{2,1,0:T(8,128)S(1)}, f32[16,64,256]{2,1,0:T(8,128)}, u32[]{:S(2)}) copy-start(f32[16,64,256]{2,1,0:T(8,128)} %b_ref.5) | copy-start | bytes 3145732
  1.9 1.0 %copy-start.2 = (bf16[16,64,256]{2,1,0:T(8,128)(2,1)S(1)}, bf16[16,64,256]{2,1,0:T(8,128)(2,1)}, u32[]{:S(2)}) copy-start(bf16[16,64,256]{2,1,0:T(8,128)(2,1)} %c_ref.3) | copy-start | bytes 1572868
  2.9 1.0 %copy-start.4 = (bf16[16,64,256]{2,1,0:T(8,128)(2,1)S(1)}, bf16[16,64,256]{2,1,0:T(8,128)(2,1)}, u32[]{:S(2)}) copy-start(bf16[16,64,256]{2,1,0:T(8,128)(2,1)} %r_ref.3) | copy-start | bytes 1572868
  3.9 18.4 %copy-start.1 = (f32[16,64,256]{2,1,0:T(8,128)S(1)}, f32[16,64,256]{2,1,0:T(8,128)}, u32[]{:S(2)}) copy-start(f32[16,64,256]{2,1,0:T(8,128)} %b_ref.5) | copy-start | bytes 3145732
  3.9 18.4 %copy-start.3 = (bf16[16,64,256]{2,1,0:T(8,128)(2,1)S(1)}, bf16[16,64,256]{2,1,0:T(8,128)(2,1)}, u32[]{:S(2)}) copy-start(bf16[16,64,256]{2,1,0:T(8,128)(2,1)} %c_ref.3) | copy-start | bytes 1572868
  3.9 18.5 %copy-start.5 = (bf16[16,64,256]{2,1,0:T(8,128)(2,1)S(1)}, bf16[16,64,256]{2,1,0:T(8,128)(2,1)}, u32[]{:S(2)}) copy-start(bf16[16,64,256]{2,1,0:T(8,128)(2,1)} %r_ref.3) | copy-start | bytes 1572868
  4.5 17.9 %collective-permute-start = (f32[2,8,64,256]{3,2,1,0:T(8,128)S(1)}, f32[2,8,64,256]{3,2,1,0:T(8,128)S(1)}, u32[]{:S(2)}, u32[]{:S(2)}) collective-permute-start(f32[2,8,64,256]{3,2,1,0:T(8,128)S(1)} %get-tuple-element.19), channel_id=1, source_target_pairs={{0,4},{1,5},{2,6},{3,7},{4,0},{5,1},{6,2},{7,3},{8,12},{9,13},{10,... | collective-permute-start | bytes 3145736 | tf_op jit(solution)/shard_map/ppermute | solution.py:126
  5.0 17.3 %collective-permute-start.1 = (f32[2,8,64,256]{3,2,1,0:T(8,128)S(1)}, f32[2,8,64,256]{3,2,1,0:T(8,128)S(1)}, u32[]{:S(2)}, u32[]{:S(2)}) collective-permute-start(f32[2,8,64,256]{3,2,1,0:T(8,128)S(1)} %get-tuple-element.20), channel_id=1, source_target_pairs={{4,8},{5,9},{6,10},{7,11},{8,4},{9,5},{10,6},{11,7},{20,24},{21,25... | collective-permute-start | bytes 3145736 | tf_op jit(solution)/shard_map/ppermute | solution.py:126
  5.8 8.4 %collective-permute-start.4 = (f32[2,8,8,256]{3,2,1,0:T(8,128)S(1)}, f32[2,8,8,256]{3,2,1,0:T(8,128)S(1)}, u32[]{:S(2)}, u32[]{:S(2)}) collective-permute-start(f32[2,8,8,256]{3,2,1,0:T(8,128)S(1)} %get-tuple-element.23), channel_id=1, source_target_pairs={{0,5},{1,4},{2,7},{3,6},{4,1},{5,0},{6,3},{7,2},{8,13},{9,12},{10,... | collective-permute-start | bytes 393224 | tf_op jit(solution)/shard_map/ppermute | solution.py:126
  10.8 4.3 %collective-permute-start.5 = (f32[2,8,8,256]{3,2,1,0:T(8,128)S(1)}, f32[2,8,8,256]{3,2,1,0:T(8,128)S(1)}, u32[]{:S(2)}, u32[]{:S(2)}) collective-permute-start(f32[2,8,8,256]{3,2,1,0:T(8,128)S(1)} %get-tuple-element.24), channel_id=1, source_target_pairs={{1,6},{2,5},{5,2},{6,1},{9,14},{10,13},{13,10},{14,9},{17,22},{18,... | collective-permute-start | bytes 393224 | tf_op jit(solution)/shard_map/ppermute | solution.py:126
  11.5 4.3 %collective-permute-start.6 = (f32[2,8,8,256]{3,2,1,0:T(8,128)S(1)}, f32[2,8,8,256]{3,2,1,0:T(8,128)S(1)}, u32[]{:S(2)}, u32[]{:S(2)}) collective-permute-start(f32[2,8,8,256]{3,2,1,0:T(8,128)S(1)} %get-tuple-element.25), channel_id=1, source_target_pairs={{4,9},{5,8},{6,11},{7,10},{8,5},{9,4},{10,7},{11,6},{20,25},{21,24... | collective-permute-start | bytes 393224 | tf_op jit(solution)/shard_map/ppermute | solution.py:126
  14.2 8.2 %collective-permute-start.2 = (f32[2,16,8,256]{3,2,1,0:T(8,128)S(1)}, f32[2,16,8,256]{3,2,1,0:T(8,128)S(1)}, u32[]{:S(2)}, u32[]{:S(2)}) collective-permute-start(f32[2,16,8,256]{3,2,1,0:T(8,128)S(1)} %get-tuple-element.21), channel_id=1, source_target_pairs={{0,1},{1,0},{2,3},{3,2},{4,5},{5,4},{6,7},{7,6},{8,9},{9,8},{10,11... | collective-permute-start | bytes 786440 | tf_op jit(solution)/shard_map/ppermute | solution.py:126
  15.1 7.3 %collective-permute-start.3 = (f32[2,16,8,256]{3,2,1,0:T(8,128)S(1)}, f32[2,16,8,256]{3,2,1,0:T(8,128)S(1)}, u32[]{:S(2)}, u32[]{:S(2)}) collective-permute-start(f32[2,16,8,256]{3,2,1,0:T(8,128)S(1)} %get-tuple-element.22), channel_id=1, source_target_pairs={{1,2},{2,1},{5,6},{6,5},{9,10},{10,9},{13,14},{14,13},{17,18},{18,... | collective-permute-start | bytes 786440 | tf_op jit(solution)/shard_map/ppermute | solution.py:126
  15.8 0.7 %collective-permute-start.7 = (f32[2,8,8,256]{3,2,1,0:T(8,128)S(1)}, f32[2,8,8,256]{3,2,1,0:T(8,128)S(1)}, u32[]{:S(2)}, u32[]{:S(2)}) collective-permute-start(f32[2,8,8,256]{3,2,1,0:T(8,128)S(1)} %get-tuple-element.26), channel_id=1, source_target_pairs={{5,10},{6,9},{9,6},{10,5},{21,26},{22,25},{25,22},{26,21}} | collective-permute-start | bytes 393224 | tf_op jit(solution)/shard_map/ppermute | solution.py:126

commit v2 on v1

--- a/solution.py
+++ b/solution.py
@@ -16,7 +16,7 @@
 LANES = 128
 AXES = ("wide", "narrow")
 VMEM = pl.BlockSpec(memory_space=pltpu.VMEM)
-ANY = pl.BlockSpec(memory_space=pl.ANY)
+HBM = pl.BlockSpec(memory_space=pltpu.HBM)
 MIB = 1024 * 1024
 
 
@@ -63,10 +63,16 @@
     return out
 
 
-def send_kernel(b_ref, c_ref, r_ref, *refs):
-    (w_out, n_out, c_out), pack = (refs[:2], refs[2:4], refs[4:8]), refs[8]
+def send_kernel(*refs):
+    args, (w_out, n_out), refs = refs[:3], (refs[3:5], refs[5:7]), refs[7:]
+    (b_ref, c_ref, r_ref), (pack, done) = refs[:3], refs[3:]
     rows, columns = b_ref.shape[:2]
     h = STEPS
+    copies = [pltpu.make_async_copy(args[k], refs[k], done.at[k]) for k in range(3)]
+    for copy in copies:
+        copy.start()
+    for copy in copies:
+        copy.wait()
     wide, narrow = sides()
     top = [jnp.where(up, rows - h, 0) for up in wide]
     left = [pl.multiple_of(jnp.where(up, columns - h, 0), 8) for up in narrow]
@@ -85,8 +91,6 @@
         for k, source in enumerate((b_ref, pack)):
             for a in range(2):
                 w_out[a][k, i] = source[top[a] + i]
-                for side in range(2):
-                    c_out[2 * a + side][k, i] = source[top[a] + i, pl.ds(left[side], h), :]
         return 0
 
     lax.fori_loop(0, rows, code, 0)
@@ -97,42 +101,63 @@
 def messages(b, c, r):
     rows, columns, depth = b.shape
     h = STEPS
-    shapes = (
-        [(2, h, columns, depth)] * 2 + [(2, rows, h, depth)] * 2 + [(2, h, h, depth)] * 4
-    )
+    shapes = [(2, h, columns, depth)] * 2 + [(2, rows, h, depth)] * 2
     return pl.pallas_call(
         send_kernel,
         out_shape=[jax.ShapeDtypeStruct(s, jnp.float32) for s in shapes],
-        in_specs=[VMEM] * 3,
-        out_specs=[VMEM] * 8,
-        scratch_shapes=[pltpu.VMEM(b.shape, jnp.float32)],
+        in_specs=[HBM] * 3,
+        out_specs=[VMEM] * 4,
+        scratch_shapes=[pltpu.VMEM(a.shape, a.dtype) for a in (b, c, r)]
+        + [pltpu.VMEM(b.shape, jnp.float32), pltpu.SemaphoreType.DMA((3,))],
         compiler_params=pltpu.CompilerParams(vmem_limit_bytes=16 * MIB),
-    )(b, c, r)
-
-
-def exchange(sent):
+    )(*[pltpu.with_memory_space_constraint(a, pltpu.HBM) for a in (b, c, r)])
+
+
+def corner_kernel(*refs):
+    n_in, c_out = refs[:2], refs[2:]
+    rows = n_in[0].shape[1]
+    top = [jnp.where(up, rows - STEPS, 0) for up in sides()[0]]
+
+    def layers(i, _):
+        for k in range(2):
+            for a in range(2):
+                for side in range(2):
+                    c_out[a][k, i, side] = n_in[side][k, top[a] + i]
+        return 0
+
+    lax.fori_loop(0, STEPS, layers, 0)
+
+
+def corners(narrow_halos):
+    depth = narrow_halos[0].shape[-1]
+    shape = jax.ShapeDtypeStruct((2, STEPS, 2, STEPS, depth), jnp.float32)
+    return pl.pallas_call(
+        corner_kernel,
+        out_shape=[shape] * 2,
+        in_specs=[VMEM] * 2,
+        out_specs=[VMEM] * 2,
+        compiler_params=pltpu.CompilerParams(vmem_limit_bytes=8 * MIB),
+    )(*narrow_halos)
+
+
+def swapped(array, across, along):
     wides, narrows = lax.axis_size("wide"), lax.axis_size("narrow")
 
     def partner(index, pairing):
         return index if pairing is None else index + (1 if index % 2 == pairing else -1)
 
-    def swapped(array, across, along):
-        pairs = []
-        for w in range(wides):
-            for n in range(narrows):
-                to_w, to_n = partner(w, across), partner(n, along)
-                if 0 <= to_w < wides and 0 <= to_n < narrows:
-                    pairs.append((w * narrows + n, to_w * narrows + to_n))
-        return lax.ppermute(array, AXES, pairs)
-
-    ways = [(0, None), (1, None), (None, 0), (None, 1), (0, 0), (0, 1), (1, 0), (1, 1)]
-    return [swapped(array, *way) for array, way in zip(sent, ways)]
+    pairs = []
+    for w in range(wides):
+        for n in range(narrows):
+            to_w, to_n = partner(w, across), partner(n, along)
+            if 0 <= to_w < wides and 0 <= to_n < narrows:
+                pairs.append((w * narrows + n, to_w * narrows + to_n))
+    return lax.ppermute(array, AXES, pairs)
 
 
 def basis_kernel(b_ref, c_ref, r_ref, *refs):
-    (w_in, n_in, c_in), refs = (refs[:2], refs[2:4], refs[4:8]), refs[8:]
-    out, m_ref, refs = refs[:STEPS], refs[STEPS], refs[STEPS + 1 :]
-    field, (u_even, u_odd, diag, coef, done) = refs[:STEPS], refs[STEPS:]
+    (w_in, n_in, c_in), refs = (refs[:2], refs[2:4], refs[4:6]), refs[6:]
+    field, m_ref, (u_even, u_odd, diag, coef) = refs[:STEPS], refs[STEPS], refs[STEPS + 1 :]
     rows, columns, depth = b_ref.shape
     h = STEPS
     tiles = (columns + 2 * h) // 8
@@ -159,8 +184,7 @@
             at = top[a] + i
             outside(at, h, w_in[a][0, i], w_in[a][1, i])
             for side in range(2):
-                corner = c_in[2 * a + side]
-                outside(at, left[side], corner[0, i], corner[1, i])
+                outside(at, left[side], c_in[a][0, i, side], c_in[a][1, i, side])
         return 0
 
     def fill_middle(i, total):
@@ -252,7 +276,6 @@
         first_sum, second_sum = carry
         return first_sum + tree(cross), (second_sum + tree(own) if own else second_sum)
 
-    copies = []
     for step in range(1, STEPS + 1):
         outer = h - step
         quads, rest = divmod(rows - 2 * outer, 4)
@@ -268,9 +291,6 @@
         if rest:
             carry = advance(step, h + rows - rest, rest, (), carry)
         moments += carry if step < STEPS else carry[:1]
-        copy = pltpu.make_async_copy(field[step - 1], out[step - 1], done.at[step - 1])
-        copy.start()
-        copies.append(copy)
 
     def folded(high, low, shift, axis):
         total, error = two_sum(high, pltpu.roll(high, shift, axis))
@@ -297,8 +317,6 @@
     )
     for k in range(m_ref.shape[0]):
         m_ref[k] = message
-    for copy in copies:
-        copy.wait()
 
 
 def basis(b, c, r, received, peers):
@@ -309,13 +327,11 @@
         basis_kernel,
         out_shape=[jax.ShapeDtypeStruct(b.shape, jnp.float32)] * STEPS
         + [jax.ShapeDtypeStruct((peers, 8, LANES), jnp.float32)],
-        in_specs=[VMEM] * 11,
-        out_specs=[ANY] * STEPS + [VMEM],
-        scratch_shapes=[pltpu.VMEM(b.shape, jnp.float32)] * STEPS
-        + [pltpu.VMEM((wide, 2, narrow + 16, LANES), jnp.float32)] * 2
-        + [pltpu.VMEM((wide, narrow, depth), jnp.float32)] * 2
-        + [pltpu.SemaphoreType.DMA((STEPS,))],
-        compiler_params=pltpu.CompilerParams(vmem_limit_bytes=34 * MIB),
+        in_specs=[VMEM] * 9,
+        out_specs=[VMEM] * (STEPS + 1),
+        scratch_shapes=[pltpu.VMEM((wide, 2, narrow + 16, LANES), jnp.float32)] * 2
+        + [pltpu.VMEM((wide, narrow, depth), jnp.float32)] * 2,
+        compiler_params=pltpu.CompilerParams(vmem_limit_bytes=30 * MIB),
     )(b, c, r, *received)
     return outs[:STEPS], outs[STEPS]
 
@@ -353,13 +369,7 @@
 
 
 def combine_kernel(m_ref, b_ref, *refs):
-    sources, (x_ref, r_ref), refs = refs[:STEPS], refs[STEPS : STEPS + 2], refs[STEPS + 2 :]
-    field, done = refs[:STEPS], refs[STEPS]
-    copies = []
-    for k in range(STEPS):
-        copies.append(pltpu.make_async_copy(sources[k], field[k], done.at[k]))
-        copies[k].start()
-
+    field, (x_ref, r_ref) = refs[:STEPS], refs[STEPS:]
     total, error = m_ref[0], jnp.zeros((8, LANES), jnp.float32)
     for k in range(1, m_ref.shape[0]):
         total, lost = two_sum(total, m_ref[k])
@@ -375,8 +385,6 @@
     sol_coord, resid_coord = coordinates(fast_two_sum(high, low))
     sol = [jnp.broadcast_to(sol_coord[k : k + 1], (8, LANES)) for k in range(STEPS)]
     res = [jnp.broadcast_to(resid_coord[k : k + 1], (8, LANES)) for k in range(STEPS + 1)]
-    for copy in copies:
-        copy.wait()
 
     def plane(i, _):
         for t in range(b_ref.shape[1] // 8):
@@ -399,17 +407,19 @@
     return pl.pallas_call(
         combine_kernel,
         out_shape=[jax.ShapeDtypeStruct(b.shape, jnp.float32)] * 2,
-        in_specs=[VMEM] * 2 + [ANY] * STEPS,
+        in_specs=[VMEM] * (STEPS + 2),
         out_specs=[VMEM] * 2,
-        scratch_shapes=[pltpu.VMEM(b.shape, jnp.float32)] * STEPS
-        + [pltpu.SemaphoreType.DMA((STEPS,))],
         compiler_params=pltpu.CompilerParams(vmem_limit_bytes=20 * MIB),
     )(gathered, b, *fields)
 
 
 def on_device(right_side, conduct_half, reaction_half):
     peers = lax.axis_size("wide") * lax.axis_size("narrow")
-    received = exchange(messages(right_side, conduct_half, reaction_half))
+    sent = messages(right_side, conduct_half, reaction_half)
+    halos = [swapped(sent[k], k, None) for k in range(2)]
+    narrow_halos = [swapped(sent[2 + k], None, k) for k in range(2)]
+    diagonal = [swapped(block, k, None) for k, block in enumerate(corners(narrow_halos))]
+    received = halos + narrow_halos + diagonal
     fields, moments = basis(right_side, conduct_half, reaction_half, received, peers)
     gathered = lax.all_to_all(moments, AXES, 0, 0, tiled=True)
     solution, residual = combine(gathered, right_side, fields)

time: 57.6 us -> 52.5 us (0.911)
  blocking collectives: 17.5 us -> 21.1 us
  local copies, waits for them, and re-layouts: 3.31 us -> 0.01 us
  waiting for transfers between devices: 7.92 us -> 4.63 us
  starting transfers between devices: 9.88 us -> 7.6 us
    all_to_all x1, blocking collectives: 17.5 us -> 21.1 us  [on_device(): gathered = lax.all_to_all(moments, AXES, 0, 0, tiled=True)]
    unnamed x12 -> x6, local copies, waits for them, and re-layouts: 3.31 us -> 0.01 us
    ppermute x8 -> x6, waiting for transfers between devices: 7.92 us -> 4.63 us  [swapped(): return lax.ppermute(array, AXES, pairs)]
    ppermute x8 -> x6, starting transfers between devices: 9.88 us -> 7.6 us  [swapped(): return lax.ppermute(array, AXES, pairs)]
    pallas_call x1, Pallas kernels: 0.56 us -> 2.16 us  [messages(): pl.pallas_call(send_kernel, out_shape=[jax.ShapeDtypeStruct(s, jnp.float3...]
    pallas_call x1, Pallas kernels: 13.7 us -> 13 us  [basis(): pl.pallas_call(basis_kernel, out_shape=[jax.ShapeDtypeStruct(b.shape, jnp...]
    pallas_call x1, Pallas kernels: 3.67 us -> 3.02 us  [combine(): pl.pallas_call(combine_kernel, out_shape=[jax.ShapeDtypeStruct(b.shape, j...]
  transfers between devices with their start and end apart: 8 -> 6, of which waited for: 2 -> 2; matrix products, arithmetic and copies ran while one was open for 0% -> 0% of each run, Pallas kernels for 0% -> 0%
where the time goes in v2:
time: 52.5 us; the launch traced here: 52.3 us
  blocking collectives  21.1 us (40%)
  Pallas kernels  18.2 us (35%)
  starting transfers between devices  7.6 us (14%)
  waiting for transfers between devices  4.63 us (9%)
  between operations  0.72 us (1%)
    all_to_all x1, blocking collectives, on_device(): gathered = lax.all_to_all(moments, AXES, 0, 0, tiled=True)  21.1 us
    pallas_call x1, Pallas kernels, basis(): pl.pallas_call(basis_kernel, out_shape=[jax.ShapeDtypeStruct(b.shape, jnp...  13 us
    ppermute x6, starting transfers between devices, swapped(): return lax.ppermute(array, AXES, pairs)  7.6 us
    ppermute x6, waiting for transfers between devices, swapped(): return lax.ppermute(array, AXES, pairs)  4.63 us
    pallas_call x1, Pallas kernels, combine(): pl.pallas_call(combine_kernel, out_shape=[jax.ShapeDtypeStruct(b.shape, j...  3.02 us
    pallas_call x1, Pallas kernels, messages(): pl.pallas_call(send_kernel, out_shape=[jax.ShapeDtypeStruct(s, jnp.float3...  2.16 us
  transfers between devices with their start and end apart: 6, of which 2 were waited for; matrix products, arithmetic and copies ran while one was open for 0% of the time, Pallas kernels for 0%

profile of v2, /device:TPU:0, one launch (start us, length us, event | category | flops | bytes accessed | tf_op | source)
XLA Modules:
  0.0 52.3 jit_solution(13615277487538207010)
XLA Ops:
  0.6 0.0 copy-start
  0.6 0.0 copy-start.2
  0.6 2.2 %shard_map.50 = (f32[2,8,64,256]{3,2,1,0:T(8,128)S(1)}, f32[2,8,64,256]{3,2,1,0:T(8,128)S(1)}, f32[2,16,8,256]{3,2,1,0:T(8,128)S(1)}, f32[2,16,8,256]{3,2,1,0:T(8,128)S(1)}) custom-call(f32[16,64,256]{2,1,0:T(8,128)} %b_ref.3, bf16[16,64,256]{2,1,0:T(8,128)(2,1)} %c_ref.1, bf16[16,64,256]{2,1,0:T(8,128)(2,1)} %r_ref.1), custom_call_target="tpu_custom_call" | custom-call | tf_op jit(solution)/shard_map/pallas_call | solution.py:105
  2.8 0.0 copy-start.1
  2.8 0.5 collective-permute-start
  3.4 0.7 %collective-permute-start.1 = (f32[2,8,64,256]{3,2,1,0:T(8,128)S(1)}, f32[2,8,64,256]{3,2,1,0:T(8,128)S(1)}, u32[]{:S(2)}, u32[]{:S(2)}) collective-permute-start(f32[2,8,64,256]{3,2,1,0:T(8,128)S(1)} %get-tuple-element.18), channel_id=1, source_target_pairs={{4,8},{5,9},{6,10},{7,11},{8,4},{9,5},{10,6},{11,7},{20,24},{21,25... | collective-permute-start | bytes 3145736 | tf_op jit(solution)/shard_map/ppermute | solution.py:155
  4.1 2.8 %collective-permute-start.2 = (f32[2,16,8,256]{3,2,1,0:T(8,128)S(1)}, f32[2,16,8,256]{3,2,1,0:T(8,128)S(1)}, u32[]{:S(2)}, u32[]{:S(2)}) collective-permute-start(f32[2,16,8,256]{3,2,1,0:T(8,128)S(1)} %get-tuple-element.19), channel_id=1, source_target_pairs={{0,1},{1,0},{2,3},{3,2},{4,5},{5,4},{6,7},{7,6},{8,9},{9,8},{10,11... | collective-permute-start | bytes 786440 | tf_op jit(solution)/shard_map/ppermute | solution.py:155
  6.9 0.7 %collective-permute-start.3 = (f32[2,16,8,256]{3,2,1,0:T(8,128)S(1)}, f32[2,16,8,256]{3,2,1,0:T(8,128)S(1)}, u32[]{:S(2)}, u32[]{:S(2)}) collective-permute-start(f32[2,16,8,256]{3,2,1,0:T(8,128)S(1)} %get-tuple-element.20), channel_id=1, source_target_pairs={{1,2},{2,1},{5,6},{6,5},{9,10},{10,9},{13,14},{14,13},{17,18},{18,... | collective-permute-start | bytes 786440 | tf_op jit(solution)/shard_map/ppermute | solution.py:155
  7.5 4.1 %collective-permute-done.2.refs_0_.refs_2_ = f32[2,16,8,256]{3,2,1,0:T(8,128)S(1)} collective-permute-done((f32[2,16,8,256]{3,2,1,0:T(8,128)S(1)}, f32[2,16,8,256]{3,2,1,0:T(8,128)S(1)}, u32[]{:S(2)}, u32[]{:S(2)}) %collective-permute-start.2) | collective-permute-done | bytes 262176 | tf_op jit(solution)/shard_map/ppermute | solution.py:155
  11.7 0.0 collective-permute-done.3.refs_1_.refs_3_
  11.7 0.1 shard_map.51
  11.7 2.2 %collective-permute-start.4 = (f32[2,8,2,8,256]{4,3,2,1,0:T(8,128)S(1)}, f32[2,8,2,8,256]{4,3,2,1,0:T(8,128)S(1)}, u32[]{:S(2)}, u32[]{:S(2)}) collective-permute-start(f32[2,8,2,8,256]{4,3,2,1,0:T(8,128)S(1)} %get-tuple-element.21), channel_id=1, source_target_pairs={{0,4},{1,5},{2,6},{3,7},{4,0},{5,1},{6,2},{7,3},{8,12},{9,13},{10,... | collective-permute-start | bytes 786440 | tf_op jit(solution)/shard_map/ppermute | solution.py:155
  14.0 0.7 %collective-permute-start.5 = (f32[2,8,2,8,256]{4,3,2,1,0:T(8,128)S(1)}, f32[2,8,2,8,256]{4,3,2,1,0:T(8,128)S(1)}, u32[]{:S(2)}, u32[]{:S(2)}) collective-permute-start(f32[2,8,2,8,256]{4,3,2,1,0:T(8,128)S(1)} %get-tuple-element.22), channel_id=1, source_target_pairs={{4,8},{5,9},{6,10},{7,11},{8,4},{9,5},{10,6},{11,7},{20,24},{21,25... | collective-permute-start | bytes 786440 | tf_op jit(solution)/shard_map/ppermute | solution.py:155
  14.7 0.5 collective-permute-done.4.refs_4_
  15.1 0.0 collective-permute-done.5.refs_5_
  15.2 0.0 collective-permute-done.refs_0_
  15.2 0.0 collective-permute-done.1.refs_1_
  15.2 0.0 copy-done
  15.2 0.0 copy-done.2
  15.2 0.0 copy-done.1
  15.2 13.0 %shard_map.52 = (f32[16,64,256]{2,1,0:T(8,128)S(1)}, f32[16,64,256]{2,1,0:T(8,128)S(1)}, f32[16,64,256]{2,1,0:T(8,128)S(1)}, f32[16,64,256]{2,1,0:T(8,128)S(1)},...) custom-call(f32[16,64,256]{2,1,0:T(8,128)S(1)} %copy-done, ...), custom_call_target="tpu_custom_call" | custom-call | tf_op jit(solution)/shard_map/pallas_call | solution.py:326
  28.2 21.1 %all_to_all.5.m_ref = f32[16,8,128]{2,1,0:T(8,128)S(1)} all-to-all(f32[16,8,128]{2,1,0:T(8,128)S(1)} %get-tuple-element.23), channel_id=1, replica_groups=mesh['group'=2,'wide'=4,'narrow'=4] {'wide','narrow'}, dimensions={0} | all-to-all | bytes 131072 | tf_op jit(solution)/shard_map/all_to_all | solution.py:424
  49.2 3.0 %shard_map.53 = (f32[16,64,256]{2,1,0:T(8,128)}, f32[16,64,256]{2,1,0:T(8,128)}) custom-call(f32[16,8,128]{2,1,0:T(8,128)S(1)} %all_to_all.5.m_ref, f32[16,64,256]{2,1,0:T(8,128)S(1)} %copy-done, f32[16,64,256]{2,1,0:T(8,128)S(1)} %get-tuple-element.24.refs_0_, f32[16,64,256]{2,1,0:T(8,128)S(1)} %get-tuple-element.25.refs_1_, ...), custom_call_target="tpu_custom_call" | custom-call | tf_op jit(solution)/shard_map/pallas_call | solution.py:407
Async XLA Ops:
  0.6 14.5 %copy-start = (f32[16,64,256]{2,1,0:T(8,128)S(1)}, f32[16,64,256]{2,1,0:T(8,128)}, u32[]{:S(2)}) copy-start(f32[16,64,256]{2,1,0:T(8,128)} %b_ref.3) | copy-start | bytes 3145732
  0.6 14.5 %copy-start.2 = (bf16[16,64,256]{2,1,0:T(8,128)(2,1)S(1)}, bf16[16,64,256]{2,1,0:T(8,128)(2,1)}, u32[]{:S(2)}) copy-start(bf16[16,64,256]{2,1,0:T(8,128)(2,1)} %r_ref.1) | copy-start | bytes 1572868
  2.8 12.4 %copy-start.1 = (bf16[16,64,256]{2,1,0:T(8,128)(2,1)S(1)}, bf16[16,64,256]{2,1,0:T(8,128)(2,1)}, u32[]{:S(2)}) copy-start(bf16[16,64,256]{2,1,0:T(8,128)(2,1)} %c_ref.1) | copy-start | bytes 1572868
  2.8 12.3 %collective-permute-start = (f32[2,8,64,256]{3,2,1,0:T(8,128)S(1)}, f32[2,8,64,256]{3,2,1,0:T(8,128)S(1)}, u32[]{:S(2)}, u32[]{:S(2)}) collective-permute-start(f32[2,8,64,256]{3,2,1,0:T(8,128)S(1)} %get-tuple-element.17), channel_id=1, source_target_pairs={{0,4},{1,5},{2,6},{3,7},{4,0},{5,1},{6,2},{7,3},{8,12},{9,13},{10,... | collective-permute-start | bytes 3145736 | tf_op jit(solution)/shard_map/ppermute | solution.py:155
  3.4 11.8 %collective-permute-start.1 = (f32[2,8,64,256]{3,2,1,0:T(8,128)S(1)}, f32[2,8,64,256]{3,2,1,0:T(8,128)S(1)}, u32[]{:S(2)}, u32[]{:S(2)}) collective-permute-start(f32[2,8,64,256]{3,2,1,0:T(8,128)S(1)} %get-tuple-element.18), channel_id=1, source_target_pairs={{4,8},{5,9},{6,10},{7,11},{8,4},{9,5},{10,6},{11,7},{20,24},{21,25... | collective-permute-start | bytes 3145736 | tf_op jit(solution)/shard_map/ppermute | solution.py:155
  4.1 7.6 %collective-permute-start.2 = (f32[2,16,8,256]{3,2,1,0:T(8,128)S(1)}, f32[2,16,8,256]{3,2,1,0:T(8,128)S(1)}, u32[]{:S(2)}, u32[]{:S(2)}) collective-permute-start(f32[2,16,8,256]{3,2,1,0:T(8,128)S(1)} %get-tuple-element.19), channel_id=1, source_target_pairs={{0,1},{1,0},{2,3},{3,2},{4,5},{5,4},{6,7},{7,6},{8,9},{9,8},{10,11... | collective-permute-start | bytes 786440 | tf_op jit(solution)/shard_map/ppermute | solution.py:155
  6.9 4.8 %collective-permute-start.3 = (f32[2,16,8,256]{3,2,1,0:T(8,128)S(1)}, f32[2,16,8,256]{3,2,1,0:T(8,128)S(1)}, u32[]{:S(2)}, u32[]{:S(2)}) collective-permute-start(f32[2,16,8,256]{3,2,1,0:T(8,128)S(1)} %get-tuple-element.20), channel_id=1, source_target_pairs={{1,2},{2,1},{5,6},{6,5},{9,10},{10,9},{13,14},{14,13},{17,18},{18,... | collective-permute-start | bytes 786440 | tf_op jit(solution)/shard_map/ppermute | solution.py:155
  11.7 3.4 %collective-permute-start.4 = (f32[2,8,2,8,256]{4,3,2,1,0:T(8,128)S(1)}, f32[2,8,2,8,256]{4,3,2,1,0:T(8,128)S(1)}, u32[]{:S(2)}, u32[]{:S(2)}) collective-permute-start(f32[2,8,2,8,256]{4,3,2,1,0:T(8,128)S(1)} %get-tuple-element.21), channel_id=1, source_target_pairs={{0,4},{1,5},{2,6},{3,7},{4,0},{5,1},{6,2},{7,3},{8,12},{9,13},{10,... | collective-permute-start | bytes 786440 | tf_op jit(solution)/shard_map/ppermute | solution.py:155
  14.0 1.2 %collective-permute-start.5 = (f32[2,8,2,8,256]{4,3,2,1,0:T(8,128)S(1)}, f32[2,8,2,8,256]{4,3,2,1,0:T(8,128)S(1)}, u32[]{:S(2)}, u32[]{:S(2)}) collective-permute-start(f32[2,8,2,8,256]{4,3,2,1,0:T(8,128)S(1)} %get-tuple-element.22), channel_id=1, source_target_pairs={{4,8},{5,9},{6,10},{7,11},{8,4},{9,5},{10,6},{11,7},{20,24},{21,25... | collective-permute-start | bytes 786440 | tf_op jit(solution)/shard_map/ppermute | solution.py:155

commit v3 on v2

v3 whole, which is shorter than its diff:
```python
import jax
import jax.numpy as jnp
from jax import lax
from jax.experimental import pallas as pl
from jax.experimental.pallas import tpu as pltpu
from jax.sharding import PartitionSpec as P

S = 4
OUTER = 2
STEPS = S * OUTER

SCALE = 13.0
CENTER = SCALE
ROOT = SCALE**-0.5

LANES = 128
AXES = ("wide", "narrow")
VMEM = pl.BlockSpec(memory_space=pltpu.VMEM)
HBM = pl.BlockSpec(memory_space=pltpu.HBM)
MIB = 1024 * 1024


def two_sum(a, b):
    total = a + b
    part = total - a
    return total, (a - (total - part)) + (b - part)


def fast_two_sum(a, b):
    total = a + b
    return total, b - (total - a)


def split(a):
    big = a * 4097.0
    high = big - (big - a)
    return high, a - high


def two_product(a, b):
    product = a * b
    a_high, a_low = split(a)
    b_high, b_low = split(b)
    error = ((a_high * b_high - product) + a_high * b_low + a_low * b_high) + a_low * b_low
    return product, error


def pair_add(a, b):
    total, error = two_sum(a[0], b[0])
    return fast_two_sum(total, error + (a[1] + b[1]))


def pair_scale(a, factor):
    product, error = two_product(a[0], factor)
    return fast_two_sum(product, error + a[1] * factor)


def sides():
    out = []
    for axis in AXES:
        even = lax.rem(lax.axis_index(axis), 2) == 0
        out.append((even, jnp.logical_not(even)))
    return out


def edge_layer(up, count, d):
    return jnp.where(up, count - d, d - 1)


def send_kernel(*refs):
    args, (w_out, n_out), refs = refs[:3], (refs[3:5], refs[5:7]), refs[7:]
    (b_ref, c_ref, r_ref), (pack, done) = refs[:3], refs[3:]
    rows, columns = b_ref.shape[:2]
    h = STEPS
    copies = [pltpu.make_async_copy(args[k], refs[k], done.at[k]) for k in range(3)]
    for copy in copies:
        copy.start()
    for copy in copies:
        copy.wait()
    wide, narrow = sides()
    left = [pl.multiple_of(jnp.where(up, columns - h, 0), 8) for up in narrow]

    def code(i, _):
        pack[i] = r_ref[i].astype(jnp.float32) + c_ref[i].astype(jnp.float32) * (1.0 / 256.0)
        return 0

    def edges(i, _):
        for k, source in enumerate((b_ref, pack)):
            for side in range(2):
                n_out[side][k, i] = source[i, pl.ds(left[side], h), :]
        return 0

    def layers(d, _):
        for a in range(2):
            at = edge_layer(wide[a], rows, d)
            w_out[a][d - 1] = b_ref[at]
            w_out[a][h + d - 1] = pack[at]
        return 0

    lax.fori_loop(0, rows, code, 0)
    lax.fori_loop(0, rows, edges, 0)
    lax.fori_loop(1, h, layers, 0)
    for a in range(2):
        at = edge_layer(wide[a], rows, h)
        w_out[a][h - 1] = c_ref[at].astype(jnp.float32) * ROOT * b_ref[at]


def messages(b, c, r):
    rows, columns, depth = b.shape
    h = STEPS
    shapes = [(2 * h - 1, columns, depth)] * 2 + [(2, rows, h, depth)] * 2
    return pl.pallas_call(
        send_kernel,
        out_shape=[jax.ShapeDtypeStruct(s, jnp.float32) for s in shapes],
        in_specs=[HBM] * 3,
        out_specs=[VMEM] * 4,
        scratch_shapes=[pltpu.VMEM(a.shape, a.dtype) for a in (b, c, r)]
        + [pltpu.VMEM(b.shape, jnp.float32), pltpu.SemaphoreType.DMA((3,))],
        compiler_params=pltpu.CompilerParams(vmem_limit_bytes=16 * MIB),
    )(*[pltpu.with_memory_space_constraint(a, pltpu.HBM) for a in (b, c, r)])


PAIRS = [(d, STEPS - d) for d in range(1, STEPS // 2 + 1)]


def corner_kernel(*refs):
    n_in, c_out = refs[:2], refs[2:]
    rows = n_in[0].shape[1]
    wide, narrow = sides()
    sub = lax.broadcasted_iota(jnp.int32, n_in[0].shape[2:], 0)
    for a in range(2):
        for side in range(2):
            up = narrow[side]
            for p, (d, other) in enumerate(PAIRS):
                shift = jnp.where(up, STEPS - d, d)
                mine = jnp.where(up, sub, STEPS - 1 - sub) < STEPS - d
                for k in range(2):
                    near = n_in[side][k, edge_layer(wide[a], rows, d)]
                    far = n_in[side][k, edge_layer(wide[a], rows, other)]
                    c_out[a][k, p, side] = jnp.where(mine, near, pltpu.roll(far, shift, 0))


def corners(narrow_halos):
    depth = narrow_halos[0].shape[-1]
    shape = jax.ShapeDtypeStruct((2, len(PAIRS), 2, STEPS, depth), jnp.float32)
    return pl.pallas_call(
        corner_kernel,
        out_shape=[shape] * 2,
        in_specs=[VMEM] * 2,
        out_specs=[VMEM] * 2,
        compiler_params=pltpu.CompilerParams(vmem_limit_bytes=8 * MIB),
    )(*narrow_halos)


def swapped(array, across, along):
    wides, narrows = lax.axis_size("wide"), lax.axis_size("narrow")

    def partner(index, pairing):
        return index if pairing is None else index + (1 if index % 2 == pairing else -1)

    pairs = []
    for w in range(wides):
        for n in range(narrows):
            to_w, to_n = partner(w, across), partner(n, along)
            if 0 <= to_w < wides and 0 <= to_n < narrows:
                pairs.append((w * narrows + n, to_w * narrows + to_n))
    return lax.ppermute(array, AXES, pairs)


def tree(parts):
    while len(parts) > 1:
        parts = [
            parts[k] + parts[k + 1] if k + 1 < len(parts) else parts[k]
            for k in range(0, len(parts), 2)
        ]
    return parts[0]


def place_u(buffer, i, y, value):
    count = value.shape[0]
    for half in range(2):
        buffer[i, half, pl.ds(y + 8, count), :] = value[:, half * LANES : (half + 1) * LANES]


def diagonal_of(conduct, reaction):
    return ((reaction - CENTER) + 6.0 * (conduct * conduct)) * (1.0 / SCALE)


def outside(u_even, diag, coef, i, y, value, packed):
    count = value.shape[0]
    reaction = jnp.floor(packed * 128.0) * (1.0 / 128.0)
    conduct = (packed - reaction) * 256.0
    root = conduct * ROOT
    place_u(u_even, i, y, root * value)
    coef[i, pl.ds(y, count), :] = root * root
    diag[i, pl.ds(y, count), :] = diagonal_of(conduct, reaction)


def advance(step, runs, refs, carry):
    b_ref, field, u_even, u_odd, diag, coef = refs
    h = STEPS
    tiles = diag.shape[1] // 8
    lane = lax.broadcasted_iota(jnp.int32, (8, LANES), 1)
    first, last = lane == 0, lane == LANES - 1
    source, target = (u_even, u_odd) if step % 2 else (u_odd, u_even)
    before = b_ref if step == 1 else field[step - 2]
    now = field[step - 1]
    cross, own = [], []
    for t in range(tiles):
        edge = t in (0, tiles - 1)
        if edge and step == STEPS:
            continue
        rows = pl.ds(8 * t + 8, 8)
        for start, count, inside in runs:
            layers = [
                [source[start + d, half, rows, :] for half in range(2)]
                for d in range(-1, count + 1)
            ]
            for d in range(count):
                i = start + d
                left, right = layers[d + 1]
                left_up, left_down = pltpu.roll(left, 1, 1), pltpu.roll(left, LANES - 1, 1)
                right_up, right_down = pltpu.roll(right, 1, 1), pltpu.roll(right, LANES - 1, 1)
                along = (
                    jnp.where(first, 0.0, left_up) + jnp.where(last, right_down, left_down),
                    jnp.where(first, left_up, right_up) + jnp.where(last, 0.0, right_down),
                )
                for half in range(2):
                    beside = (
                        source[i, half, pl.ds(8 * t + 7, 8), :]
                        + source[i, half, pl.ds(8 * t + 9, 8), :]
                    )
                    across = layers[d][half] + layers[d + 2][half]
                    around = (beside + across) + along[half]
                    lanes = pl.ds(half * LANES, LANES)
                    at = (i, pl.ds(8 * t, 8), lanes)
                    if inside and not edge:
                        here = (i - h, pl.ds(8 * t - h, 8), lanes)
                        old = before[here]
                        root = coef[at]
                        value = diag[at] * old - root * around
                        now[here] = value
                        cross.append(value * old)
                        if step < STEPS:
                            target[i, half, rows, :] = root * value
                            own.append(value * value)
                    else:
                        target[i, half, rows, :] = (
                            diag[at] * layers[d + 1][half] - coef[at] * around
                        )
    if not cross:
        return carry
    return carry[0] + tree(cross), (carry[1] + tree(own) if own else carry[1])


def inner_kernel(b_ref, c_ref, r_ref, *refs):
    n_in, field, (u_even, u_odd, diag, coef, m_ref) = refs[:2], refs[2 : 2 + STEPS], refs[2 + STEPS :]
    rows, columns, depth = b_ref.shape
    h = STEPS
    left = [pl.multiple_of(jnp.where(up, columns + h, 0), 8) for up in sides()[1]]
    everything = (b_ref, field, u_even, u_odd, diag, coef)

    def fill(i, total):
        at = i + h
        for side in range(2):
            outside(u_even, diag, coef, at, left[side], n_in[side][0, i], n_in[side][1, i])
        value = b_ref[i]
        conduct = c_ref[i].astype(jnp.float32)
        root = conduct * ROOT
        place_u(u_even, at, h, root * value)
        coef[at, pl.ds(h, columns), :] = root
        diag[at, pl.ds(h, columns), :] = diagonal_of(conduct, r_ref[i].astype(jnp.float32))
        square = value * value
        return total + tree(
            [
                square[t * 8 : t * 8 + 8, half * LANES : (half + 1) * LANES]
                for t in range(columns // 8)
                for half in range(2)
            ]
        )

    zero = jnp.zeros((8, LANES), jnp.float32)
    m_ref[0] = lax.fori_loop(0, rows, fill, zero)
    for step in range(1, STEPS + 1):
        quads, rest = divmod(max(rows - 2 * step, 0), 4)

        def body(m, carry, step=step):
            return advance(step, [(4 * m + h + step, 4, True)], everything, carry)

        carry = lax.fori_loop(0, quads, body, (zero, zero))
        if rest:
            carry = advance(step, [(h + rows - step - rest, rest, True)], everything, carry)
        m_ref[2 * step - 1] = carry[0]
        if step < STEPS:
            m_ref[2 * step] = carry[1]


def outer_kernel(b_ref, m_in, *refs):
    (w_in, c_in), refs = (refs[:2], refs[2:4]), refs[4 + STEPS + 4 :]
    field, (u_even, u_odd, diag, coef, m_out) = refs[:STEPS], refs[STEPS:]
    rows, columns, depth = b_ref.shape
    h = STEPS
    wide, narrow = sides()
    left = [pl.multiple_of(jnp.where(up, columns + h, 0), 8) for up in narrow]
    everything = (b_ref, field, u_even, u_odd, diag, coef)

    def halo_layer(a, d):
        return jnp.where(wide[a], rows + h - 1 + d, h - d)

    def fill(d, _):
        for a in range(2):
            outside(u_even, diag, coef, halo_layer(a, d), h, w_in[a][d - 1], w_in[a][h + d - 1])
        return 0

    lax.fori_loop(1, h, fill, 0)
    for a in range(2):
        place_u(u_even, halo_layer(a, h), h, w_in[a][h - 1])
        for side in range(2):
            for p, (d, other) in enumerate(PAIRS):
                near = [c_in[a][k, p, side] for k in range(2)]
                outside(u_even, diag, coef, halo_layer(a, d), left[side], *near)
                if other != d:
                    shift = jnp.where(narrow[side], d, h - d)
                    far = [pltpu.roll(block, shift, 0) for block in near]
                    outside(u_even, diag, coef, halo_layer(a, other), left[side], *far)

    zero = jnp.zeros((8, LANES), jnp.float32)
    moments = [m_in[0]]
    for step in range(1, STEPS + 1):
        halo = (step, rows + h)
        inner = (h, rows + h - step)

        def halo_body(m, carry, step=step, halo=halo):
            advance(step, [(2 * m + first, 2, False) for first in halo], everything, None)
            return carry

        def inner_body(m, carry, step=step, inner=inner):
            return advance(step, [(2 * m + first, 2, True) for first in inner], everything, carry)

        carry = (m_in[2 * step - 1], m_in[2 * step] if step < STEPS else zero)
        lax.fori_loop(0, (h - step) // 2, halo_body, 0)
        carry = lax.fori_loop(0, step // 2, inner_body, carry)
        if step % 2:
            runs = [(first + step - 1, 1, True) for first in inner]
            runs += [(first + h - step - 1, 1, False) for first in halo]
            carry = advance(step, runs, everything, carry)
        moments += carry if step < STEPS else carry[:1]

    def folded(high, low, shift, axis):
        total, error = two_sum(high, pltpu.roll(high, shift, axis))
        return total, (low + pltpu.roll(low, shift, axis)) + error

    sublane = lax.broadcasted_iota(jnp.int32, (8, LANES), 0)
    lane = lax.broadcasted_iota(jnp.int32, (8, LANES), 1)
    packed = []
    for group in range(2):
        highs, lows = zero, zero
        for k in range(8):
            high, low = moments[group * 8 + k], zero
            for shift in (4, 2, 1):
                high, low = folded(high, low, shift, 0)
            highs = jnp.where(sublane == k, high, highs)
            lows = jnp.where(sublane == k, low, lows)
        for shift in (64, 32, 16, 8, 4, 2, 1):
            highs, lows = folded(highs, lows, shift, 1)
        packed += [highs, lows]
    quarter = LANES // 4
    message = jnp.where(
        lane < quarter,
        packed[0],
        jnp.where(lane < 2 * quarter, packed[1], jnp.where(lane < 3 * quarter, packed[2], packed[3])),
    )
    for k in range(m_out.shape[0]):
        m_out[k] = message


def state_shapes(b):
    rows, columns, depth = b.shape
    wide, narrow = rows + 2 * STEPS, columns + 2 * STEPS
    shapes = [b.shape] * STEPS + [(wide, 2, narrow + 16, LANES)] * 2 + [(wide, narrow, depth)] * 2
    return [pltpu.VMEM(s, jnp.float32) for s in shapes]


def inner(b, c, r, narrow_halos):
    shapes = state_shapes(b) + [jax.ShapeDtypeStruct((2 * STEPS, 8, LANES), jnp.float32)]
    return pl.pallas_call(
        inner_kernel,
        out_shape=shapes,
        in_specs=[VMEM] * 5,
        out_specs=[VMEM] * len(shapes),
        compiler_params=pltpu.CompilerParams(vmem_limit_bytes=26 * MIB),
    )(b, c, r, *narrow_halos)


def outer(b, wide_halos, diagonal, state, moments, peers):
    shapes = state_shapes(b) + [jax.ShapeDtypeStruct((peers, 8, LANES), jnp.float32)]
    out = pl.pallas_call(
        outer_kernel,
        out_shape=shapes,
        in_specs=[VMEM] * (6 + len(state)),
        out_specs=[VMEM] * len(shapes),
        input_output_aliases={6 + k: k for k in range(len(state))},
        compiler_params=pltpu.CompilerParams(vmem_limit_bytes=26 * MIB),
    )(b, moments, *wide_halos, *diagonal, *state)
    return out[:STEPS], out[-1]


def coordinates(moment):
    shape = moment[0].shape
    count = shape[0]
    row = lax.broadcasted_iota(jnp.int32, shape, 0)

    def later(v):
        return jnp.where(row == count - 1, 0.0, pltpu.roll(v, count - 1, 0))

    def raised(v):
        return jnp.where(row == 0, 0.0, pltpu.roll(v, 1, 0))

    def spread(v):
        return jnp.broadcast_to(v, shape)

    residual = search = moment
    resid_coord = jnp.where(row == 0, 1.0, 0.0)
    search_coord = resid_coord
    sol_coord = jnp.zeros(shape, jnp.float32)
    for i in range(STEPS):
        mapped = pair_add((later(search[0]), later(search[1])), search)
        old = residual[0][i : i + 1]
        length = old / mapped[0][i : i + 1]
        lengths = spread(length)
        residual = pair_add(residual, pair_scale(mapped, -lengths))
        grown = spread(-length * residual[0][i + 1 : i + 2] / old)
        search = pair_add(residual, pair_scale(search, grown))
        sol_coord = sol_coord + (lengths * (1.0 / SCALE)) * search_coord
        resid_coord = resid_coord - lengths * (raised(search_coord) + search_coord)
        search_coord = resid_coord + grown * search_coord
    return sol_coord, resid_coord


def combine_kernel(m_ref, b_ref, *refs):
    field, (x_ref, r_ref) = refs[:STEPS], refs[STEPS:]
    total, error = m_ref[0], jnp.zeros((8, LANES), jnp.float32)
    for k in range(1, m_ref.shape[0]):
        total, lost = two_sum(total, m_ref[k])
        error = error + lost

    def lane(v, k):
        return jnp.broadcast_to(v[:, k * LANES // 4 : k * LANES // 4 + 1], (8, LANES))

    high = jnp.concatenate([lane(total, 0), lane(total, 2)], axis=0)
    low = jnp.concatenate(
        [lane(error, 0) + lane(total, 1), lane(error, 2) + lane(total, 3)], axis=0
    )
    sol_coord, resid_coord = coordinates(fast_two_sum(high, low))
    sol = [jnp.broadcast_to(sol_coord[k : k + 1], (8, LANES)) for k in range(STEPS)]
    res = [jnp.broadcast_to(resid_coord[k : k + 1], (8, LANES)) for k in range(STEPS + 1)]

    def plane(i, _):
        for t in range(b_ref.shape[1] // 8):
            for half in range(b_ref.shape[2] // LANES):
                at = (i, pl.ds(8 * t, 8), pl.ds(half * LANES, LANES))
                fields = [b_ref[at]] + [f[at] for f in field]
                x, r = sol[0] * fields[0], res[0] * fields[0]
                for k in range(1, STEPS + 1):
                    if k < STEPS:
                        x = x + sol[k] * fields[k]
                    r = r + res[k] * fields[k]
                x_ref[at] = x
                r_ref[at] = r
        return 0

    lax.fori_loop(0, b_ref.shape[0], plane, 0)


def combine(gathered, b, fields):
    return pl.pallas_call(
        combine_kernel,
        out_shape=[jax.ShapeDtypeStruct(b.shape, jnp.float32)] * 2,
        in_specs=[VMEM] * (STEPS + 2),
        out_specs=[VMEM] * 2,
        compiler_params=pltpu.CompilerParams(vmem_limit_bytes=20 * MIB),
    )(gathered, b, *fields)


def on_device(right_side, conduct_half, reaction_half):
    peers = lax.axis_size("wide") * lax.axis_size("narrow")
    sent = messages(right_side, conduct_half, reaction_half)
    wide_halos = [swapped(sent[k], k, None) for k in range(2)]
    narrow_halos = [swapped(sent[2 + k], None, k) for k in range(2)]
    diagonal = [swapped(block, k, None) for k, block in enumerate(corners(narrow_halos))]
    *state, moments = inner(right_side, conduct_half, reaction_half, narrow_halos)
    fields, moments = outer(right_side, wide_halos, diagonal, state, moments, peers)
    gathered = lax.all_to_all(moments, AXES, 0, 0, tiled=True)
    solution, residual = combine(gathered, right_side, fields)
    return (solution, residual)


def solution(mesh):
    placed = P(("group", "wide"), "narrow", None)
    return jax.shard_map(
        on_device,
        mesh=mesh,
        in_specs=(placed, placed, placed),
        out_specs=(placed, placed),
        check_vma=False,
    )
```

time: 52.5 us -> 49.3 us (0.939)
  blocking collectives: 21.1 us -> 16.6 us
  local copies, waits for them, and re-layouts: 0.01 us -> 2.08 us
    all_to_all x1, blocking collectives: 21.1 us -> 16.6 us  [on_device(): gathered = lax.all_to_all(moments, AXES, 0, 0, tiled=True)]
    unnamed x6, local copies, waits for them, and re-layouts: 0.01 us -> 2.08 us
    pallas_call x1 -> x2, Pallas kernels: 13 us -> 12.8 us  [the longest x1 8.84 us: outer(): pl.pallas_call(outer_kernel, out_shape=shapes, in_specs=[VMEM] * (6 + len...]
  transfers between devices with their start and end apart: 6 -> 6, of which waited for: 2 -> 1; matrix products, arithmetic and copies ran while one was open for 0% -> 0% of each run, Pallas kernels for 0% -> 8%
where the time goes in v3:
time: 49.3 us; the launch traced here: 49 us
  Pallas kernels  18 us (37%)
  blocking collectives  16.6 us (34%)
  starting transfers between devices  7.46 us (15%)
  waiting for transfers between devices  4.14 us (8%)
  local copies, waits for them, and re-layouts  2.08 us (4%)
  between operations  0.73 us (1%)
    all_to_all x1, blocking collectives, on_device(): gathered = lax.all_to_all(moments, AXES, 0, 0, tiled=True)  16.6 us
    pallas_call x1, Pallas kernels, outer(): pl.pallas_call(outer_kernel, out_shape=shapes, in_specs=[VMEM] * (6 + len...  8.84 us
    ppermute x6, starting transfers between devices, swapped(): return lax.ppermute(array, AXES, pairs)  7.46 us
    ppermute x6, waiting for transfers between devices, swapped(): return lax.ppermute(array, AXES, pairs)  4.14 us
    pallas_call x1, Pallas kernels, inner(): pl.pallas_call(inner_kernel, out_shape=shapes, in_specs=[VMEM] * 5, out_s...  3.96 us
    pallas_call x1, Pallas kernels, combine(): pl.pallas_call(combine_kernel, out_shape=[jax.ShapeDtypeStruct(b.shape, j...  3.02 us
    pallas_call x1, Pallas kernels, messages(): pl.pallas_call(send_kernel, out_shape=[jax.ShapeDtypeStruct(s, jnp.float3...  2.14 us
    unnamed x6, local copies, waits for them, and re-layouts  2.08 us
  transfers between devices with their start and end apart: 6, of which 1 were waited for; matrix products, arithmetic and copies ran while one was open for 0% of the time, Pallas kernels for 8%

profile of v3, /device:TPU:0, one launch (start us, length us, event | category | flops | bytes accessed | tf_op | source)
XLA Modules:
  0.0 49.0 jit_solution(5432848124452425296)
XLA Ops:
  0.6 0.0 copy-start
  0.6 2.1 %shard_map.50 = (f32[15,64,256]{2,1,0:T(8,128)S(1)}, f32[15,64,256]{2,1,0:T(8,128)S(1)}, f32[2,16,8,256]{3,2,1,0:T(8,128)S(1)}, f32[2,16,8,256]{3,2,1,0:T(8,128)S(1)}) custom-call(f32[16,64,256]{2,1,0:T(8,128)} %b_ref.5, bf16[16,64,256]{2,1,0:T(8,128)(2,1)} %c_ref.1, bf16[16,64,256]{2,1,0:T(8,128)(2,1)} %r_ref.1), custom_call_target="tpu_custom_call" | custom-call | tf_op jit(solution)/shard_map/pallas_call | solution.py:112
  2.8 0.5 %collective-permute-start.2 = (f32[15,64,256]{2,1,0:T(8,128)S(1)}, f32[15,64,256]{2,1,0:T(8,128)S(1)}, u32[]{:S(2)}, u32[]{:S(2)}) collective-permute-start(f32[15,64,256]{2,1,0:T(8,128)S(1)} %get-tuple-element.33), channel_id=1, source_target_pairs={{0,4},{1,5},{2,6},{3,7},{4,0},{5,1},{6,2},{7,3},{8,12},{9,13},{10,... | collective-permute-start | bytes 2949128 | tf_op jit(solution)/shard_map/ppermute | solution.py:167
  3.3 0.7 %collective-permute-start.3 = (f32[15,64,256]{2,1,0:T(8,128)S(1)}, f32[15,64,256]{2,1,0:T(8,128)S(1)}, u32[]{:S(2)}, u32[]{:S(2)}) collective-permute-start(f32[15,64,256]{2,1,0:T(8,128)S(1)} %get-tuple-element.34), channel_id=1, source_target_pairs={{4,8},{5,9},{6,10},{7,11},{8,4},{9,5},{10,6},{11,7},{20,24},{21,25... | collective-permute-start | bytes 2949128 | tf_op jit(solution)/shard_map/ppermute | solution.py:167
  4.0 2.7 %collective-permute-start = (f32[2,16,8,256]{3,2,1,0:T(8,128)S(1)}, f32[2,16,8,256]{3,2,1,0:T(8,128)S(1)}, u32[]{:S(2)}, u32[]{:S(2)}) collective-permute-start(f32[2,16,8,256]{3,2,1,0:T(8,128)S(1)} %get-tuple-element.30), channel_id=1, source_target_pairs={{0,1},{1,0},{2,3},{3,2},{4,5},{5,4},{6,7},{7,6},{8,9},{9,8},{10,11... | collective-permute-start | bytes 786440 | tf_op jit(solution)/shard_map/ppermute | solution.py:167
  6.7 0.7 %collective-permute-start.1 = (f32[2,16,8,256]{3,2,1,0:T(8,128)S(1)}, f32[2,16,8,256]{3,2,1,0:T(8,128)S(1)}, u32[]{:S(2)}, u32[]{:S(2)}) collective-permute-start(f32[2,16,8,256]{3,2,1,0:T(8,128)S(1)} %get-tuple-element.31), channel_id=1, source_target_pairs={{1,2},{2,1},{5,6},{6,5},{9,10},{10,9},{13,14},{14,13},{17,18},{18,... | collective-permute-start | bytes 786440 | tf_op jit(solution)/shard_map/ppermute | solution.py:167
  7.4 4.1 %collective-permute-done.refs_0_ = f32[2,16,8,256]{3,2,1,0:T(8,128)S(1)} collective-permute-done((f32[2,16,8,256]{3,2,1,0:T(8,128)S(1)}, f32[2,16,8,256]{3,2,1,0:T(8,128)S(1)}, u32[]{:S(2)}, u32[]{:S(2)}) %collective-permute-start) | collective-permute-done | bytes 262176 | tf_op jit(solution)/shard_map/ppermute | solution.py:167
  11.5 0.0 collective-permute-done.1.refs_1_
  11.5 2.2 %collective-permute-start.4 = (f32[2,4,2,8,256]{4,3,2,1,0:T(8,128)S(1)}, f32[2,4,2,8,256]{4,3,2,1,0:T(8,128)S(1)}, u32[]{:S(2)}, u32[]{:S(2)}) collective-permute-start(f32[2,4,2,8,256]{4,3,2,1,0:T(8,128)S(1)} %get-tuple-element.35), channel_id=1, source_target_pairs={{0,4},{1,5},{2,6},{3,7},{4,0},{5,1},{6,2},{7,3},{8,12},{9,13},{10,... | collective-permute-start | bytes 393224 | tf_op jit(solution)/shard_map/ppermute | solution.py:167
  13.8 0.7 %collective-permute-start.5 = (f32[2,4,2,8,256]{4,3,2,1,0:T(8,128)S(1)}, f32[2,4,2,8,256]{4,3,2,1,0:T(8,128)S(1)}, u32[]{:S(2)}, u32[]{:S(2)}) collective-permute-start(f32[2,4,2,8,256]{4,3,2,1,0:T(8,128)S(1)} %get-tuple-element.36), channel_id=1, source_target_pairs={{4,8},{5,9},{6,10},{7,11},{8,4},{9,5},{10,6},{11,7},{20,24},{21,25... | collective-permute-start | bytes 393224 | tf_op jit(solution)/shard_map/ppermute | solution.py:167
  14.4 0.0 copy-done
  14.5 0.0 copy-start.1
  14.5 1.0 %copy-done.1 = bf16[16,64,256]{2,1,0:T(8,128)(2,1)S(1)} copy-done((bf16[16,64,256]{2,1,0:T(8,128)(2,1)S(1)}, bf16[16,64,256]{2,1,0:T(8,128)(2,1)}, u32[]{:S(2)}) %copy-start.1) | copy-done | bytes 524312
  15.5 0.0 copy-start.2
  15.5 1.0 %copy-done.2 = bf16[16,64,256]{2,1,0:T(8,128)(2,1)S(1)} copy-done((bf16[16,64,256]{2,1,0:T(8,128)(2,1)S(1)}, bf16[16,64,256]{2,1,0:T(8,128)(2,1)}, u32[]{:S(2)}) %copy-start.2) | copy-done | bytes 524312
  16.5 4.0 %shard_map.51 = (f32[16,64,256]{2,1,0:T(8,128)S(1)}, f32[16,64,256]{2,1,0:T(8,128)S(1)}, f32[16,64,256]{2,1,0:T(8,128)S(1)}, f32[16,64,256]{2,1,0:T(8,128)S(1)},...) custom-call(f32[16,64,256]{2,1,0:T(8,128)S(1)} %copy-done, ...), custom_call_target="tpu_custom_call" | custom-call | tf_op jit(solution)/shard_map/pallas_call | solution.py:386
  20.5 0.0 collective-permute-done.4.refs_2_
  20.5 0.0 collective-permute-done.5.refs_3_
  20.5 0.0 collective-permute-done.2.refs_0_
  20.5 0.0 collective-permute-done.3.refs_1_
  20.6 8.8 %shard_map.53 = (f32[16,64,256]{2,1,0:T(8,128)S(1)}, f32[16,64,256]{2,1,0:T(8,128)S(1)}, f32[16,64,256]{2,1,0:T(8,128)S(1)}, f32[16,64,256]{2,1,0:T(8,128)S(1)},...) custom-call(f32[16,64,256]{2,1,0:T(8,128)S(1)} %copy-done, ...), custom_call_target="tpu_custom_call", output_to_operand_aliasing={{0}: (6, {}), {1}: (7, {}), {2}: (8, {}), {3}: (9, {}), {4}... | custom-call | tf_op jit(solution)/shard_map/pallas_call | solution.py:397
  29.4 16.6 %all_to_all.5.m_ref = f32[16,8,128]{2,1,0:T(8,128)S(1)} all-to-all(f32[16,8,128]{2,1,0:T(8,128)S(1)} %get-tuple-element.49), channel_id=1, replica_groups=mesh['group'=2,'wide'=4,'narrow'=4] {'wide','narrow'}, dimensions={0} | all-to-all | bytes 131072 | tf_op jit(solution)/shard_map/all_to_all | solution.py:493
  46.0 3.0 %shard_map.54 = (f32[16,64,256]{2,1,0:T(8,128)}, f32[16,64,256]{2,1,0:T(8,128)}) custom-call(f32[16,8,128]{2,1,0:T(8,128)S(1)} %all_to_all.5.m_ref, f32[16,64,256]{2,1,0:T(8,128)S(1)} %copy-done, f32[16,64,256]{2,1,0:T(8,128)S(1)} %get-tuple-element.50.refs_0_, f32[16,64,256]{2,1,0:T(8,128)S(1)} %get-tuple-element.51.refs_1_, ...), custom_call_target="tpu_custom_call" | custom-call | tf_op jit(solution)/shard_map/pallas_call | solution.py:476
  (1 shorter events, 0.0 us)
Async XLA Ops:
  0.6 13.8 %copy-start = (f32[16,64,256]{2,1,0:T(8,128)S(1)}, f32[16,64,256]{2,1,0:T(8,128)}, u32[]{:S(2)}) copy-start(f32[16,64,256]{2,1,0:T(8,128)} %b_ref.5) | copy-start | bytes 3145732
  2.8 17.7 %collective-permute-start.2 = (f32[15,64,256]{2,1,0:T(8,128)S(1)}, f32[15,64,256]{2,1,0:T(8,128)S(1)}, u32[]{:S(2)}, u32[]{:S(2)}) collective-permute-start(f32[15,64,256]{2,1,0:T(8,128)S(1)} %get-tuple-element.33), channel_id=1, source_target_pairs={{0,4},{1,5},{2,6},{3,7},{4,0},{5,1},{6,2},{7,3},{8,12},{9,13},{10,... | collective-permute-start | bytes 2949128 | tf_op jit(solution)/shard_map/ppermute | solution.py:167
  3.3 17.2 %collective-permute-start.3 = (f32[15,64,256]{2,1,0:T(8,128)S(1)}, f32[15,64,256]{2,1,0:T(8,128)S(1)}, u32[]{:S(2)}, u32[]{:S(2)}) collective-permute-start(f32[15,64,256]{2,1,0:T(8,128)S(1)} %get-tuple-element.34), channel_id=1, source_target_pairs={{4,8},{5,9},{6,10},{7,11},{8,4},{9,5},{10,6},{11,7},{20,24},{21,25... | collective-permute-start | bytes 2949128 | tf_op jit(solution)/shard_map/ppermute | solution.py:167
  4.0 7.5 %collective-permute-start = (f32[2,16,8,256]{3,2,1,0:T(8,128)S(1)}, f32[2,16,8,256]{3,2,1,0:T(8,128)S(1)}, u32[]{:S(2)}, u32[]{:S(2)}) collective-permute-start(f32[2,16,8,256]{3,2,1,0:T(8,128)S(1)} %get-tuple-element.30), channel_id=1, source_target_pairs={{0,1},{1,0},{2,3},{3,2},{4,5},{5,4},{6,7},{7,6},{8,9},{9,8},{10,11... | collective-permute-start | bytes 786440 | tf_op jit(solution)/shard_map/ppermute | solution.py:167
  6.7 4.8 %collective-permute-start.1 = (f32[2,16,8,256]{3,2,1,0:T(8,128)S(1)}, f32[2,16,8,256]{3,2,1,0:T(8,128)S(1)}, u32[]{:S(2)}, u32[]{:S(2)}) collective-permute-start(f32[2,16,8,256]{3,2,1,0:T(8,128)S(1)} %get-tuple-element.31), channel_id=1, source_target_pairs={{1,2},{2,1},{5,6},{6,5},{9,10},{10,9},{13,14},{14,13},{17,18},{18,... | collective-permute-start | bytes 786440 | tf_op jit(solution)/shard_map/ppermute | solution.py:167
  11.5 9.0 %collective-permute-start.4 = (f32[2,4,2,8,256]{4,3,2,1,0:T(8,128)S(1)}, f32[2,4,2,8,256]{4,3,2,1,0:T(8,128)S(1)}, u32[]{:S(2)}, u32[]{:S(2)}) collective-permute-start(f32[2,4,2,8,256]{4,3,2,1,0:T(8,128)S(1)} %get-tuple-element.35), channel_id=1, source_target_pairs={{0,4},{1,5},{2,6},{3,7},{4,0},{5,1},{6,2},{7,3},{8,12},{9,13},{10,... | collective-permute-start | bytes 393224 | tf_op jit(solution)/shard_map/ppermute | solution.py:167
  13.8 6.7 %collective-permute-start.5 = (f32[2,4,2,8,256]{4,3,2,1,0:T(8,128)S(1)}, f32[2,4,2,8,256]{4,3,2,1,0:T(8,128)S(1)}, u32[]{:S(2)}, u32[]{:S(2)}) collective-permute-start(f32[2,4,2,8,256]{4,3,2,1,0:T(8,128)S(1)} %get-tuple-element.36), channel_id=1, source_target_pairs={{4,8},{5,9},{6,10},{7,11},{8,4},{9,5},{10,6},{11,7},{20,24},{21,25... | collective-permute-start | bytes 393224 | tf_op jit(solution)/shard_map/ppermute | solution.py:167
  14.5 1.0 %copy-start.1 = (bf16[16,64,256]{2,1,0:T(8,128)(2,1)S(1)}, bf16[16,64,256]{2,1,0:T(8,128)(2,1)}, u32[]{:S(2)}) copy-start(bf16[16,64,256]{2,1,0:T(8,128)(2,1)} %c_ref.1) | copy-start | bytes 1572868
  15.5 1.0 %copy-start.2 = (bf16[16,64,256]{2,1,0:T(8,128)(2,1)S(1)}, bf16[16,64,256]{2,1,0:T(8,128)(2,1)}, u32[]{:S(2)}) copy-start(bf16[16,64,256]{2,1,0:T(8,128)(2,1)} %r_ref.1) | copy-start | bytes 1572868

commit v4 on v3

--- a/solution.py
+++ b/solution.py
@@ -111,11 +111,11 @@
     shapes = [(2 * h - 1, columns, depth)] * 2 + [(2, rows, h, depth)] * 2
     return pl.pallas_call(
         send_kernel,
-        out_shape=[jax.ShapeDtypeStruct(s, jnp.float32) for s in shapes],
+        out_shape=[jax.ShapeDtypeStruct(s, jnp.float32) for s in shapes]
+        + [pltpu.VMEM(a.shape, a.dtype) for a in (b, c, r)],
         in_specs=[HBM] * 3,
-        out_specs=[VMEM] * 4,
-        scratch_shapes=[pltpu.VMEM(a.shape, a.dtype) for a in (b, c, r)]
-        + [pltpu.VMEM(b.shape, jnp.float32), pltpu.SemaphoreType.DMA((3,))],
+        out_specs=[VMEM] * 7,
+        scratch_shapes=[pltpu.VMEM(b.shape, jnp.float32), pltpu.SemaphoreType.DMA((3,))],
         compiler_params=pltpu.CompilerParams(vmem_limit_bytes=16 * MIB),
     )(*[pltpu.with_memory_space_constraint(a, pltpu.HBM) for a in (b, c, r)])
 
@@ -124,7 +124,7 @@
 
 
 def corner_kernel(*refs):
-    n_in, c_out = refs[:2], refs[2:]
+    n_in, c_out = refs[:2], refs[3:]
     rows = n_in[0].shape[1]
     wide, narrow = sides()
     sub = lax.broadcasted_iota(jnp.int32, n_in[0].shape[2:], 0)
@@ -140,16 +140,16 @@
                     c_out[a][k, p, side] = jnp.where(mine, near, pltpu.roll(far, shift, 0))
 
 
-def corners(narrow_halos):
+def corners(narrow_halos, after):
     depth = narrow_halos[0].shape[-1]
     shape = jax.ShapeDtypeStruct((2, len(PAIRS), 2, STEPS, depth), jnp.float32)
     return pl.pallas_call(
         corner_kernel,
         out_shape=[shape] * 2,
-        in_specs=[VMEM] * 2,
+        in_specs=[VMEM] * 3,
         out_specs=[VMEM] * 2,
         compiler_params=pltpu.CompilerParams(vmem_limit_bytes=8 * MIB),
-    )(*narrow_halos)
+    )(*narrow_halos, after)
 
 
 def swapped(array, across, along):
@@ -196,7 +196,7 @@
     diag[i, pl.ds(y, count), :] = diagonal_of(conduct, reaction)
 
 
-def advance(step, runs, refs, carry):
+def advance(step, runs, refs, carry, chosen=None, silent=()):
     b_ref, field, u_even, u_odd, diag, coef = refs
     h = STEPS
     tiles = diag.shape[1] // 8
@@ -206,7 +206,7 @@
     before = b_ref if step == 1 else field[step - 2]
     now = field[step - 1]
     cross, own = [], []
-    for t in range(tiles):
+    for t in range(tiles) if chosen is None else chosen:
         edge = t in (0, tiles - 1)
         if edge and step == STEPS:
             continue
@@ -240,9 +240,12 @@
                         root = coef[at]
                         value = diag[at] * old - root * around
                         now[here] = value
+                        if step < STEPS:
+                            target[i, half, rows, :] = root * value
+                        if t in silent:
+                            continue
                         cross.append(value * old)
                         if step < STEPS:
-                            target[i, half, rows, :] = root * value
                             own.append(value * value)
                     else:
                         target[i, half, rows, :] = (
@@ -254,16 +257,14 @@
 
 
 def inner_kernel(b_ref, c_ref, r_ref, *refs):
-    n_in, field, (u_even, u_odd, diag, coef, m_ref) = refs[:2], refs[2 : 2 + STEPS], refs[2 + STEPS :]
+    field, (u_even, u_odd, diag, coef, m_ref) = refs[:STEPS], refs[STEPS:]
     rows, columns, depth = b_ref.shape
     h = STEPS
-    left = [pl.multiple_of(jnp.where(up, columns + h, 0), 8) for up in sides()[1]]
     everything = (b_ref, field, u_even, u_odd, diag, coef)
+    tiles = range(1, columns // 8 + 1)
 
     def fill(i, total):
         at = i + h
-        for side in range(2):
-            outside(u_even, diag, coef, at, left[side], n_in[side][0, i], n_in[side][1, i])
         value = b_ref[i]
         conduct = c_ref[i].astype(jnp.float32)
         root = conduct * ROOT
@@ -284,15 +285,59 @@
     for step in range(1, STEPS + 1):
         quads, rest = divmod(max(rows - 2 * step, 0), 4)
 
-        def body(m, carry, step=step):
-            return advance(step, [(4 * m + h + step, 4, True)], everything, carry)
+        def work(start, count, carry, step=step):
+            runs = [(start, count, True)]
+            return advance(step, runs, everything, carry, tiles, (tiles[0], tiles[-1]))
+
+        def body(m, carry, step=step, work=work):
+            return work(4 * m + h + step, 4, carry)
 
         carry = lax.fori_loop(0, quads, body, (zero, zero))
         if rest:
-            carry = advance(step, [(h + rows - step - rest, rest, True)], everything, carry)
+            carry = work(h + rows - step - rest, rest, carry)
         m_ref[2 * step - 1] = carry[0]
         if step < STEPS:
             m_ref[2 * step] = carry[1]
+
+
+def border_kernel(b_ref, m_in, *refs):
+    n_in, refs = refs[:2], refs[2 + STEPS + 4 :]
+    field, (u_even, u_odd, diag, coef, m_out) = refs[:STEPS], refs[STEPS:]
+    rows, columns, depth = b_ref.shape
+    h = STEPS
+    tiles = columns // 8 + 2
+    left = [pl.multiple_of(jnp.where(up, columns + h, 0), 8) for up in sides()[1]]
+    everything = (b_ref, field, u_even, u_odd, diag, coef)
+
+    def fill(i, _):
+        at = i + h
+        for side in range(2):
+            outside(u_even, diag, coef, at, left[side], n_in[side][0, i], n_in[side][1, i])
+        for y in (0, columns - 8):
+            place_u(u_even, at, y + h, coef[at, pl.ds(y + h, 8), :] * b_ref[i, pl.ds(y, 8), :])
+        return 0
+
+    lax.fori_loop(0, rows, fill, 0)
+    m_out[0] = m_in[0]
+    for step in range(1, STEPS + 1):
+        source = u_even if step % 2 else u_odd
+        before = b_ref if step == 1 else field[step - 2]
+        for i in range(step - 1, rows - step + 1):
+            for y in (8, columns - 9):
+                row = coef[i + h, y + h : y + h + 1, :] * before[i, y : y + 1, :]
+                for half in range(2):
+                    source[i + h, half, y + h + 8 : y + h + 9, :] = row[
+                        :, half * LANES : (half + 1) * LANES
+                    ]
+        count = max(rows - 2 * step, 0)
+        carry = (m_in[2 * step - 1], m_in[2 * step] if step < STEPS else m_in[0])
+        for start, part in ((step, count // 2), (step + count // 2, count - count // 2)):
+            if part:
+                runs = [(start + h, part, True)]
+                carry = advance(step, runs, everything, carry, (0, 1, tiles - 2, tiles - 1))
+        m_out[2 * step - 1] = carry[0]
+        if step < STEPS:
+            m_out[2 * step] = carry[1]
 
 
 def outer_kernel(b_ref, m_in, *refs):
@@ -381,28 +426,33 @@
     return [pltpu.VMEM(s, jnp.float32) for s in shapes]
 
 
-def inner(b, c, r, narrow_halos):
+def inner(b, c, r):
     shapes = state_shapes(b) + [jax.ShapeDtypeStruct((2 * STEPS, 8, LANES), jnp.float32)]
-    return pl.pallas_call(
+    *state, moments = pl.pallas_call(
         inner_kernel,
+        cost_estimate=pl.CostEstimate(
+            flops=120 * b.size, bytes_accessed=24 * b.size, transcendentals=0
+        ),
         out_shape=shapes,
-        in_specs=[VMEM] * 5,
+        in_specs=[VMEM] * 3,
         out_specs=[VMEM] * len(shapes),
         compiler_params=pltpu.CompilerParams(vmem_limit_bytes=26 * MIB),
-    )(b, c, r, *narrow_halos)
-
-
-def outer(b, wide_halos, diagonal, state, moments, peers):
-    shapes = state_shapes(b) + [jax.ShapeDtypeStruct((peers, 8, LANES), jnp.float32)]
-    out = pl.pallas_call(
-        outer_kernel,
+    )(b, c, r)
+    return state, moments
+
+
+def onward(kernel, b, moments, received, state, moments_shape):
+    shapes = state_shapes(b) + [jax.ShapeDtypeStruct(moments_shape, jnp.float32)]
+    others = 2 + len(received)
+    *state, moments = pl.pallas_call(
+        kernel,
         out_shape=shapes,
-        in_specs=[VMEM] * (6 + len(state)),
+        in_specs=[VMEM] * (others + len(state)),
         out_specs=[VMEM] * len(shapes),
-        input_output_aliases={6 + k: k for k in range(len(state))},
+        input_output_aliases={others + k: k for k in range(len(state))},
         compiler_params=pltpu.CompilerParams(vmem_limit_bytes=26 * MIB),
-    )(b, moments, *wide_halos, *diagonal, *state)
-    return out[:STEPS], out[-1]
+    )(b, moments, *received, *state)
+    return state, moments
 
 
 def coordinates(moment):
@@ -484,14 +534,18 @@
 
 def on_device(right_side, conduct_half, reaction_half):
     peers = lax.axis_size("wide") * lax.axis_size("narrow")
-    sent = messages(right_side, conduct_half, reaction_half)
-    wide_halos = [swapped(sent[k], k, None) for k in range(2)]
+    *sent, b, c, r = messages(right_side, conduct_half, reaction_half)
+    far, near = swapped(sent[1], 1, None), swapped(sent[0], 0, None)
     narrow_halos = [swapped(sent[2 + k], None, k) for k in range(2)]
-    diagonal = [swapped(block, k, None) for k, block in enumerate(corners(narrow_halos))]
-    *state, moments = inner(right_side, conduct_half, reaction_half, narrow_halos)
-    fields, moments = outer(right_side, wide_halos, diagonal, state, moments, peers)
+    state, moments = inner(b, c, r)
+    diagonal = corners(narrow_halos, moments)
+    diagonal = [swapped(block, k, None) for k, block in enumerate(diagonal)]
+    state, moments = onward(border_kernel, b, moments, narrow_halos, state, moments.shape)
+    received = [near, far, *diagonal]
+    state, moments = onward(outer_kernel, b, moments, received, state, (peers, 8, LANES))
+    fields = state[:STEPS]
     gathered = lax.all_to_all(moments, AXES, 0, 0, tiled=True)
-    solution, residual = combine(gathered, right_side, fields)
+    solution, residual = combine(gathered, b, fields)
     return (solution, residual)
 
 

time: 49.3 us -> 46.7 us (0.947)
  waiting for transfers between devices: 4.14 us -> 0.82 us
  blocking collectives: 16.6 us -> 18.7 us
  local copies, waits for them, and re-layouts: 2.08 us -> 0 us
  Pallas kernels: 18 us -> 18.7 us
    ppermute x6, waiting for transfers between devices: 4.14 us -> 0.82 us  [swapped(): return lax.ppermute(array, AXES, pairs)]
    all_to_all x1, blocking collectives: 16.6 us -> 18.7 us  [on_device(): gathered = lax.all_to_all(moments, AXES, 0, 0, tiled=True)]
    unnamed x6 -> x0, local copies, waits for them, and re-layouts: 2.08 us -> none
    pallas_call x3 -> x4, Pallas kernels: 12.8 us -> 13.7 us  [the longest x2 10.3 us: onward(): pl.pallas_call(kernel, out_shape=shapes, in_specs=[VMEM] * (others + len(...]
  transfers between devices with their start and end apart: 6 -> 6, of which waited for: 1 -> 1; matrix products, arithmetic and copies ran while one was open for 0% -> 0% of each run, Pallas kernels for 8% -> 10%
where the time goes in v4:
time: 46.7 us; the launch traced here: 46.5 us
  Pallas kernels  18.7 us (40%)
  blocking collectives  18.7 us (40%)
  starting transfers between devices  7.46 us (16%)
  waiting for transfers between devices  0.82 us (2%)
  between operations  0.71 us (2%)
    all_to_all x1, blocking collectives, on_device(): gathered = lax.all_to_all(moments, AXES, 0, 0, tiled=True)  18.7 us
    pallas_call x2, Pallas kernels, onward(): pl.pallas_call(kernel, out_shape=shapes, in_specs=[VMEM] * (others + len(...  10.3 us
    ppermute x6, starting transfers between devices, swapped(): return lax.ppermute(array, AXES, pairs)  7.46 us
    pallas_call x1, Pallas kernels, inner(): pl.pallas_call(inner_kernel, cost_estimate=pl.CostEstimate(flops=120 * b....  3.31 us
    pallas_call x1, Pallas kernels, combine(): pl.pallas_call(combine_kernel, out_shape=[jax.ShapeDtypeStruct(b.shape, j...  3.02 us
    pallas_call x1, Pallas kernels, messages(): pl.pallas_call(send_kernel, out_shape=[jax.ShapeDtypeStruct(s, jnp.float3...  2.05 us
  transfers between devices with their start and end apart: 6, of which 1 were waited for; matrix products, arithmetic and copies ran while one was open for 0% of the time, Pallas kernels for 10%

profile of v4, /device:TPU:0, one launch (start us, length us, event | category | flops | bytes accessed | tf_op | source)
XLA Modules:
  0.0 46.5 jit_solution(13073243808779042412)
XLA Ops:
  0.6 2.1 %shard_map.50 = (f32[15,64,256]{2,1,0:T(8,128)S(1)}, f32[15,64,256]{2,1,0:T(8,128)S(1)}, f32[2,16,8,256]{3,2,1,0:T(8,128)S(1)}, f32[2,16,8,256]{3,2,1,0:T(8,128)...) custom-call(f32[16,64,256]{2,1,0:T(8,128)} %refs_0_.1, ...), custom_call_target="tpu_custom_call" | custom-call | tf_op jit(solution)/shard_map/pallas_call | solution.py:112
  2.7 0.5 %collective-permute-start.2 = (f32[15,64,256]{2,1,0:T(8,128)S(1)}, f32[15,64,256]{2,1,0:T(8,128)S(1)}, u32[]{:S(2)}, u32[]{:S(2)}) collective-permute-start(f32[15,64,256]{2,1,0:T(8,128)S(1)} %get-tuple-element.65), channel_id=1, source_target_pairs={{0,4},{1,5},{2,6},{3,7},{4,0},{5,1},{6,2},{7,3},{8,12},{9,13},{10,... | collective-permute-start | bytes 2949128 | tf_op jit(solution)/shard_map/ppermute | solution.py:167
  3.2 0.7 %collective-permute-start.3 = (f32[15,64,256]{2,1,0:T(8,128)S(1)}, f32[15,64,256]{2,1,0:T(8,128)S(1)}, u32[]{:S(2)}, u32[]{:S(2)}) collective-permute-start(f32[15,64,256]{2,1,0:T(8,128)S(1)} %get-tuple-element.66), channel_id=1, source_target_pairs={{4,8},{5,9},{6,10},{7,11},{8,4},{9,5},{10,6},{11,7},{20,24},{21,25... | collective-permute-start | bytes 2949128 | tf_op jit(solution)/shard_map/ppermute | solution.py:167
  3.9 2.7 %collective-permute-start = (f32[2,16,8,256]{3,2,1,0:T(8,128)S(1)}, f32[2,16,8,256]{3,2,1,0:T(8,128)S(1)}, u32[]{:S(2)}, u32[]{:S(2)}) collective-permute-start(f32[2,16,8,256]{3,2,1,0:T(8,128)S(1)} %get-tuple-element.50), channel_id=1, source_target_pairs={{0,1},{1,0},{2,3},{3,2},{4,5},{5,4},{6,7},{7,6},{8,9},{9,8},{10,11... | collective-permute-start | bytes 786440 | tf_op jit(solution)/shard_map/ppermute | solution.py:167
  6.6 0.7 %collective-permute-start.1 = (f32[2,16,8,256]{3,2,1,0:T(8,128)S(1)}, f32[2,16,8,256]{3,2,1,0:T(8,128)S(1)}, u32[]{:S(2)}, u32[]{:S(2)}) collective-permute-start(f32[2,16,8,256]{3,2,1,0:T(8,128)S(1)} %get-tuple-element.51), channel_id=1, source_target_pairs={{1,2},{2,1},{5,6},{6,5},{9,10},{10,9},{13,14},{14,13},{17,18},{18,... | collective-permute-start | bytes 786440 | tf_op jit(solution)/shard_map/ppermute | solution.py:167
  7.3 3.3 %shard_map.51 = (f32[16,64,256]{2,1,0:T(8,128)S(1)}, f32[16,64,256]{2,1,0:T(8,128)S(1)}, f32[16,64,256]{2,1,0:T(8,128)S(1)}, f32[16,64,256]{2,1,0:T(8,128)S(1)},...) custom-call(f32[16,64,256]{2,1,0:T(8,128)S(1)} %get-tuple-element.46, ...), custom_call_target="tpu_custom_call" | custom-call | flops 31457280 | bytes 6291456 | tf_op jit(solution)/shard_map/pallas_call | solution.py:431
  10.6 0.8 %collective-permute-done.refs_0_ = f32[2,16,8,256]{3,2,1,0:T(8,128)S(1)} collective-permute-done((f32[2,16,8,256]{3,2,1,0:T(8,128)S(1)}, f32[2,16,8,256]{3,2,1,0:T(8,128)S(1)}, u32[]{:S(2)}, u32[]{:S(2)}) %collective-permute-start) | collective-permute-done | bytes 262176 | tf_op jit(solution)/shard_map/ppermute | solution.py:167
  11.4 0.0 collective-permute-done.1.refs_1_
  11.4 2.2 %collective-permute-start.4 = (f32[2,4,2,8,256]{4,3,2,1,0:T(8,128)S(1)}, f32[2,4,2,8,256]{4,3,2,1,0:T(8,128)S(1)}, u32[]{:S(2)}, u32[]{:S(2)}) collective-permute-start(f32[2,4,2,8,256]{4,3,2,1,0:T(8,128)S(1)} %get-tuple-element.67), channel_id=1, source_target_pairs={{0,4},{1,5},{2,6},{3,7},{4,0},{5,1},{6,2},{7,3},{8,12},{9,13},{10,... | collective-permute-start | bytes 393224 | tf_op jit(solution)/shard_map/ppermute | solution.py:167
  13.7 0.7 %collective-permute-start.5 = (f32[2,4,2,8,256]{4,3,2,1,0:T(8,128)S(1)}, f32[2,4,2,8,256]{4,3,2,1,0:T(8,128)S(1)}, u32[]{:S(2)}, u32[]{:S(2)}) collective-permute-start(f32[2,4,2,8,256]{4,3,2,1,0:T(8,128)S(1)} %get-tuple-element.68), channel_id=1, source_target_pairs={{4,8},{5,9},{6,10},{7,11},{8,4},{9,5},{10,6},{11,7},{20,24},{21,25... | collective-permute-start | bytes 393224 | tf_op jit(solution)/shard_map/ppermute | solution.py:167
  14.3 1.5 %shard_map.52 = (f32[16,64,256]{2,1,0:T(8,128)S(1)}, f32[16,64,256]{2,1,0:T(8,128)S(1)}, f32[16,64,256]{2,1,0:T(8,128)S(1)}, f32[16,64,256]{2,1,0:T(8,128)S(1)},...) custom-call(f32[16,64,256]{2,1,0:T(8,128)S(1)} %get-tuple-element.46, ...), custom_call_target="tpu_custom_call", output_to_operand_aliasing={{0}: (4, {}), {1}: (5, {}), {2}: (6, {}), {3}: (7, {}), {4}... | custom-call | tf_op jit(solution)/shard_map/pallas_call | solution.py:447
  15.8 0.0 collective-permute-done.4.refs_2_
  15.8 0.0 collective-permute-done.5.refs_3_
  15.9 0.0 collective-permute-done.2.refs_0_
  15.9 0.0 collective-permute-done.3.refs_1_
  15.9 8.8 %shard_map.54 = (f32[16,64,256]{2,1,0:T(8,128)S(1)}, f32[16,64,256]{2,1,0:T(8,128)S(1)}, f32[16,64,256]{2,1,0:T(8,128)S(1)}, f32[16,64,256]{2,1,0:T(8,128)S(1)},...) custom-call(f32[16,64,256]{2,1,0:T(8,128)S(1)} %get-tuple-element.46, ...), custom_call_target="tpu_custom_call", output_to_operand_aliasing={{0}: (6, {}), {1}: (7, {}), {2}: (8, {}), {3}: (9, {}), {4}... | custom-call | tf_op jit(solution)/shard_map/pallas_call | solution.py:447
  24.7 18.7 %all_to_all.5.m_ref = f32[16,8,128]{2,1,0:T(8,128)S(1)} all-to-all(f32[16,8,128]{2,1,0:T(8,128)S(1)} %get-tuple-element.81), channel_id=1, replica_groups=mesh['group'=2,'wide'=4,'narrow'=4] {'wide','narrow'}, dimensions={0} | all-to-all | bytes 131072 | tf_op jit(solution)/shard_map/all_to_all | solution.py:547
  43.4 3.0 %shard_map.55 = (f32[16,64,256]{2,1,0:T(8,128)}, f32[16,64,256]{2,1,0:T(8,128)}) custom-call(f32[16,8,128]{2,1,0:T(8,128)S(1)} %all_to_all.5.m_ref, f32[16,64,256]{2,1,0:T(8,128)S(1)} %get-tuple-element.46.b_ref, f32[16,64,256]{2,1,0:T(8,128)S(1)} %get-tuple-element.82.refs_0_, f32[16,64,256]{2,1,0:T(8,128)S(1)} %get-tuple-element.83.refs_1_, ...), custom_call_target="tpu_custom_call" | custom-call | tf_op jit(solution)/shard_map/pallas_call | solution.py:526
  (1 shorter events, 0.0 us)
Async XLA Ops:
  2.7 13.2 %collective-permute-start.2 = (f32[15,64,256]{2,1,0:T(8,128)S(1)}, f32[15,64,256]{2,1,0:T(8,128)S(1)}, u32[]{:S(2)}, u32[]{:S(2)}) collective-permute-start(f32[15,64,256]{2,1,0:T(8,128)S(1)} %get-tuple-element.65), channel_id=1, source_target_pairs={{0,4},{1,5},{2,6},{3,7},{4,0},{5,1},{6,2},{7,3},{8,12},{9,13},{10,... | collective-permute-start | bytes 2949128 | tf_op jit(solution)/shard_map/ppermute | solution.py:167
  3.2 12.7 %collective-permute-start.3 = (f32[15,64,256]{2,1,0:T(8,128)S(1)}, f32[15,64,256]{2,1,0:T(8,128)S(1)}, u32[]{:S(2)}, u32[]{:S(2)}) collective-permute-start(f32[15,64,256]{2,1,0:T(8,128)S(1)} %get-tuple-element.66), channel_id=1, source_target_pairs={{4,8},{5,9},{6,10},{7,11},{8,4},{9,5},{10,6},{11,7},{20,24},{21,25... | collective-permute-start | bytes 2949128 | tf_op jit(solution)/shard_map/ppermute | solution.py:167
  3.9 7.5 %collective-permute-start = (f32[2,16,8,256]{3,2,1,0:T(8,128)S(1)}, f32[2,16,8,256]{3,2,1,0:T(8,128)S(1)}, u32[]{:S(2)}, u32[]{:S(2)}) collective-permute-start(f32[2,16,8,256]{3,2,1,0:T(8,128)S(1)} %get-tuple-element.50), channel_id=1, source_target_pairs={{0,1},{1,0},{2,3},{3,2},{4,5},{5,4},{6,7},{7,6},{8,9},{9,8},{10,11... | collective-permute-start | bytes 786440 | tf_op jit(solution)/shard_map/ppermute | solution.py:167
  6.6 4.8 %collective-permute-start.1 = (f32[2,16,8,256]{3,2,1,0:T(8,128)S(1)}, f32[2,16,8,256]{3,2,1,0:T(8,128)S(1)}, u32[]{:S(2)}, u32[]{:S(2)}) collective-permute-start(f32[2,16,8,256]{3,2,1,0:T(8,128)S(1)} %get-tuple-element.51), channel_id=1, source_target_pairs={{1,2},{2,1},{5,6},{6,5},{9,10},{10,9},{13,14},{14,13},{17,18},{18,... | collective-permute-start | bytes 786440 | tf_op jit(solution)/shard_map/ppermute | solution.py:167
  11.4 4.4 %collective-permute-start.4 = (f32[2,4,2,8,256]{4,3,2,1,0:T(8,128)S(1)}, f32[2,4,2,8,256]{4,3,2,1,0:T(8,128)S(1)}, u32[]{:S(2)}, u32[]{:S(2)}) collective-permute-start(f32[2,4,2,8,256]{4,3,2,1,0:T(8,128)S(1)} %get-tuple-element.67), channel_id=1, source_target_pairs={{0,4},{1,5},{2,6},{3,7},{4,0},{5,1},{6,2},{7,3},{8,12},{9,13},{10,... | collective-permute-start | bytes 393224 | tf_op jit(solution)/shard_map/ppermute | solution.py:167
  13.7 2.2 %collective-permute-start.5 = (f32[2,4,2,8,256]{4,3,2,1,0:T(8,128)S(1)}, f32[2,4,2,8,256]{4,3,2,1,0:T(8,128)S(1)}, u32[]{:S(2)}, u32[]{:S(2)}) collective-permute-start(f32[2,4,2,8,256]{4,3,2,1,0:T(8,128)S(1)} %get-tuple-element.68), channel_id=1, source_target_pairs={{4,8},{5,9},{6,10},{7,11},{8,4},{9,5},{10,6},{11,7},{20,24},{21,25... | collective-permute-start | bytes 393224 | tf_op jit(solution)/shard_map/ppermute | solution.py:167

commit v5 on v4

--- a/solution.py
+++ b/solution.py
@@ -1,3 +1,5 @@
+import functools
+
 import jax
 import jax.numpy as jnp
 from jax import lax
@@ -14,6 +16,7 @@
 ROOT = SCALE**-0.5
 
 LANES = 128
+QUARTER = LANES // 4
 AXES = ("wide", "narrow")
 VMEM = pl.BlockSpec(memory_space=pltpu.VMEM)
 HBM = pl.BlockSpec(memory_space=pltpu.HBM)
@@ -340,56 +343,47 @@
             m_out[2 * step] = carry[1]
 
 
-def outer_kernel(b_ref, m_in, *refs):
-    (w_in, c_in), refs = (refs[:2], refs[2:4]), refs[4 + STEPS + 4 :]
+def outer_kernel(pairing, b_ref, m_in, *refs):
+    (w_in, c_in), refs = refs[:2], refs[2 + STEPS + 4 :]
     field, (u_even, u_odd, diag, coef, m_out) = refs[:STEPS], refs[STEPS:]
     rows, columns, depth = b_ref.shape
     h = STEPS
     wide, narrow = sides()
-    left = [pl.multiple_of(jnp.where(up, columns + h, 0), 8) for up in narrow]
+    up = wide[pairing]
+    left = [pl.multiple_of(jnp.where(side, columns + h, 0), 8) for side in narrow]
     everything = (b_ref, field, u_even, u_odd, diag, coef)
 
-    def halo_layer(a, d):
-        return jnp.where(wide[a], rows + h - 1 + d, h - d)
+    def halo_layer(d):
+        return jnp.where(up, rows + h - 1 + d, h - d)
 
     def fill(d, _):
-        for a in range(2):
-            outside(u_even, diag, coef, halo_layer(a, d), h, w_in[a][d - 1], w_in[a][h + d - 1])
+        outside(u_even, diag, coef, halo_layer(d), h, w_in[d - 1], w_in[h + d - 1])
         return 0
 
     lax.fori_loop(1, h, fill, 0)
-    for a in range(2):
-        place_u(u_even, halo_layer(a, h), h, w_in[a][h - 1])
-        for side in range(2):
-            for p, (d, other) in enumerate(PAIRS):
-                near = [c_in[a][k, p, side] for k in range(2)]
-                outside(u_even, diag, coef, halo_layer(a, d), left[side], *near)
-                if other != d:
-                    shift = jnp.where(narrow[side], d, h - d)
-                    far = [pltpu.roll(block, shift, 0) for block in near]
-                    outside(u_even, diag, coef, halo_layer(a, other), left[side], *far)
+    place_u(u_even, halo_layer(h), h, w_in[h - 1])
+    for side in range(2):
+        for p, (d, other) in enumerate(PAIRS):
+            near = [c_in[k, p, side] for k in range(2)]
+            outside(u_even, diag, coef, halo_layer(d), left[side], *near)
+            if other != d:
+                shift = jnp.where(narrow[side], d, h - d)
+                far = [pltpu.roll(block, shift, 0) for block in near]
+                outside(u_even, diag, coef, halo_layer(other), left[side], *far)
 
     zero = jnp.zeros((8, LANES), jnp.float32)
     moments = [m_in[0]]
     for step in range(1, STEPS + 1):
-        halo = (step, rows + h)
-        inner = (h, rows + h - step)
-
-        def halo_body(m, carry, step=step, halo=halo):
-            advance(step, [(2 * m + first, 2, False) for first in halo], everything, None)
-            return carry
-
-        def inner_body(m, carry, step=step, inner=inner):
-            return advance(step, [(2 * m + first, 2, True) for first in inner], everything, carry)
-
         carry = (m_in[2 * step - 1], m_in[2 * step] if step < STEPS else zero)
-        lax.fori_loop(0, (h - step) // 2, halo_body, 0)
-        carry = lax.fori_loop(0, step // 2, inner_body, carry)
-        if step % 2:
-            runs = [(first + step - 1, 1, True) for first in inner]
-            runs += [(first + h - step - 1, 1, False) for first in halo]
-            carry = advance(step, runs, everything, carry)
+        runs = [(jnp.where(up, rows + h - step, h), step, True)]
+        if step < STEPS:
+            runs.append((jnp.where(up, rows + h, step), h - step, False))
+        carry = advance(step, runs, everything, carry)
         moments += carry if step < STEPS else carry[:1]
+    if pairing == 0:
+        for k, moment in enumerate(moments):
+            m_out[k] = moment
+        return
 
     def folded(high, low, shift, axis):
         total, error = two_sum(high, pltpu.roll(high, shift, axis))
@@ -409,14 +403,42 @@
         for shift in (64, 32, 16, 8, 4, 2, 1):
             highs, lows = folded(highs, lows, shift, 1)
         packed += [highs, lows]
-    quarter = LANES // 4
     message = jnp.where(
-        lane < quarter,
+        lane < QUARTER,
         packed[0],
-        jnp.where(lane < 2 * quarter, packed[1], jnp.where(lane < 3 * quarter, packed[2], packed[3])),
+        jnp.where(lane < 2 * QUARTER, packed[1], jnp.where(lane < 3 * QUARTER, packed[2], packed[3])),
     )
     for k in range(m_out.shape[0]):
         m_out[k] = message
+
+
+def summed(m_ref):
+    total, error = m_ref[0], jnp.zeros((8, LANES), jnp.float32)
+    for k in range(1, m_ref.shape[0]):
+        total, lost = two_sum(total, m_ref[k])
+        error = error + lost
+    return total, error
+
+
+def relay_kernel(m_ref, out_ref):
+    total, error = summed(m_ref)
+    lane = lax.broadcasted_iota(jnp.int32, (8, LANES), 1)
+    low = lax.rem(lane // QUARTER, 2) == 1
+    message = total + jnp.where(low, pltpu.roll(error, QUARTER, 1), 0.0)
+    for k in range(out_ref.shape[0]):
+        out_ref[k] = message
+
+
+def gather(message):
+    over_wide = lax.all_to_all(message, "wide", 0, 0, tiled=True)
+    shape = (lax.axis_size("narrow"), 8, LANES)
+    relayed = pl.pallas_call(
+        relay_kernel,
+        out_shape=jax.ShapeDtypeStruct(shape, jnp.float32),
+        in_specs=[VMEM],
+        out_specs=VMEM,
+    )(over_wide)
+    return lax.all_to_all(relayed, "narrow", 0, 0, tiled=True)
 
 
 def state_shapes(b):
@@ -489,13 +511,10 @@
 
 def combine_kernel(m_ref, b_ref, *refs):
     field, (x_ref, r_ref) = refs[:STEPS], refs[STEPS:]
-    total, error = m_ref[0], jnp.zeros((8, LANES), jnp.float32)
-    for k in range(1, m_ref.shape[0]):
-        total, lost = two_sum(total, m_ref[k])
-        error = error + lost
+    total, error = summed(m_ref)
 
     def lane(v, k):
-        return jnp.broadcast_to(v[:, k * LANES // 4 : k * LANES // 4 + 1], (8, LANES))
+        return jnp.broadcast_to(v[:, k * QUARTER : k * QUARTER + 1], (8, LANES))
 
     high = jnp.concatenate([lane(total, 0), lane(total, 2)], axis=0)
     low = jnp.concatenate(
@@ -533,7 +552,6 @@
 
 
 def on_device(right_side, conduct_half, reaction_half):
-    peers = lax.axis_size("wide") * lax.axis_size("narrow")
     *sent, b, c, r = messages(right_side, conduct_half, reaction_half)
     far, near = swapped(sent[1], 1, None), swapped(sent[0], 0, None)
     narrow_halos = [swapped(sent[2 + k], None, k) for k in range(2)]
@@ -541,10 +559,11 @@
     diagonal = corners(narrow_halos, moments)
     diagonal = [swapped(block, k, None) for k, block in enumerate(diagonal)]
     state, moments = onward(border_kernel, b, moments, narrow_halos, state, moments.shape)
-    received = [near, far, *diagonal]
-    state, moments = onward(outer_kernel, b, moments, received, state, (peers, 8, LANES))
-    fields = state[:STEPS]
-    gathered = lax.all_to_all(moments, AXES, 0, 0, tiled=True)
+    for pairing, received in enumerate(([near, diagonal[0]], [far, diagonal[1]])):
+        shape = (lax.axis_size("wide"), 8, LANES) if pairing else moments.shape
+        kernel = functools.partial(outer_kernel, pairing)
+        state, moments = onward(kernel, b, moments, received, state, shape)
+    gathered, fields = gather(moments), state[:STEPS]
     solution, residual = combine(gathered, b, fields)
     return (solution, residual)
 

time: 46.7 us -> 62.3 us (1.33)
  local copies, waits for them, and re-layouts: 0 us -> 13.2 us
  blocking collectives: 18.7 us -> 21.3 us
    unnamed x0 -> x24, local copies, waits for them, and re-layouts: none -> 13.2 us
    all_to_all x1 -> x2, blocking collectives: 18.7 us -> 21.3 us  [the longest x1 12.9 us: gather(): return lax.all_to_all(relayed, 'narrow', 0, 0, tiled=True)]
    pallas_call x2 -> x3, Pallas kernels: 10.3 us -> 8.47 us  [onward(): pl.pallas_call(kernel, out_shape=shapes, in_specs=[VMEM] * (others + len(...]
    pallas_call x0 -> x1, Pallas kernels: none -> 1.39 us  [gather(): pl.pallas_call(relay_kernel, out_shape=jax.ShapeDtypeStruct(shape, jnp.fl...]
  transfers between devices with their start and end apart: 6 -> 6, of which waited for: 1 -> 1; matrix products, arithmetic and copies ran while one was open for 0% -> 0% of each run, Pallas kernels for 10% -> 13%
where the time goes in v5:
time: 62.3 us; the launch traced here: 61.8 us
  blocking collectives  21.3 us (34%)
  Pallas kernels  18.3 us (29%)
  local copies, waits for them, and re-layouts  13.2 us (21%)
  starting transfers between devices  7.46 us (12%)
  waiting for transfers between devices  0.82 us (1%)
  between operations  0.74 us (1%)
    unnamed x24, local copies, waits for them, and re-layouts  13.2 us
    all_to_all x1, blocking collectives, gather(): return lax.all_to_all(relayed, 'narrow', 0, 0, tiled=True)  12.9 us
    pallas_call x3, Pallas kernels, onward(): pl.pallas_call(kernel, out_shape=shapes, in_specs=[VMEM] * (others + len(...  8.47 us
    all_to_all x1, blocking collectives, gather(): over_wide = lax.all_to_all(message, 'wide', 0, 0, tiled=True)  8.43 us
    ppermute x6, starting transfers between devices, swapped(): return lax.ppermute(array, AXES, pairs)  7.46 us
    pallas_call x1, Pallas kernels, inner(): pl.pallas_call(inner_kernel, cost_estimate=pl.CostEstimate(flops=120 * b....  3.31 us
    pallas_call x1, Pallas kernels, combine(): pl.pallas_call(combine_kernel, out_shape=[jax.ShapeDtypeStruct(b.shape, j...  3.01 us
    pallas_call x1, Pallas kernels, messages(): pl.pallas_call(send_kernel, out_shape=[jax.ShapeDtypeStruct(s, jnp.float3...  2.05 us
  transfers between devices with their start and end apart: 6, of which 1 were waited for; matrix products, arithmetic and copies ran while one was open for 0% of the time, Pallas kernels for 13%

profile of v5, /device:TPU:0, one launch (start us, length us, event | category | flops | bytes accessed | tf_op | source)
XLA Modules:
  0.0 61.8 jit_solution(3142396406802336533)
XLA Ops:
  0.6 2.1 %shard_map.50 = (f32[15,64,256]{2,1,0:T(8,128)S(1)}, f32[15,64,256]{2,1,0:T(8,128)S(1)}, f32[2,16,8,256]{3,2,1,0:T(8,128)S(1)}, f32[2,16,8,256]{3,2,1,0:T(8,128)...) custom-call(f32[16,64,256]{2,1,0:T(8,128)} %refs_0_.1, ...), custom_call_target="tpu_custom_call" | custom-call | tf_op jit(solution)/shard_map/pallas_call | solution.py:115
  2.7 0.5 collective-permute-start.2
  3.2 0.7 %collective-permute-start.4 = (f32[15,64,256]{2,1,0:T(8,128)S(1)}, f32[15,64,256]{2,1,0:T(8,128)S(1)}, u32[]{:S(2)}, u32[]{:S(2)}) collective-permute-start(f32[15,64,256]{2,1,0:T(8,128)S(1)} %get-tuple-element.93), channel_id=1, source_target_pairs={{4,8},{5,9},{6,10},{7,11},{8,4},{9,5},{10,6},{11,7},{20,24},{21,25... | collective-permute-start | bytes 2949128 | tf_op jit(solution)/shard_map/ppermute | solution.py:170
  3.9 2.7 %collective-permute-start = (f32[2,16,8,256]{3,2,1,0:T(8,128)S(1)}, f32[2,16,8,256]{3,2,1,0:T(8,128)S(1)}, u32[]{:S(2)}, u32[]{:S(2)}) collective-permute-start(f32[2,16,8,256]{3,2,1,0:T(8,128)S(1)} %get-tuple-element.63), channel_id=1, source_target_pairs={{0,1},{1,0},{2,3},{3,2},{4,5},{5,4},{6,7},{7,6},{8,9},{9,8},{10,11... | collective-permute-start | bytes 786440 | tf_op jit(solution)/shard_map/ppermute | solution.py:170
  6.6 0.7 %collective-permute-start.1 = (f32[2,16,8,256]{3,2,1,0:T(8,128)S(1)}, f32[2,16,8,256]{3,2,1,0:T(8,128)S(1)}, u32[]{:S(2)}, u32[]{:S(2)}) collective-permute-start(f32[2,16,8,256]{3,2,1,0:T(8,128)S(1)} %get-tuple-element.64), channel_id=1, source_target_pairs={{1,2},{2,1},{5,6},{6,5},{9,10},{10,9},{13,14},{14,13},{17,18},{18,... | collective-permute-start | bytes 786440 | tf_op jit(solution)/shard_map/ppermute | solution.py:170
  7.3 3.3 %shard_map.51 = (f32[16,64,256]{2,1,0:T(8,128)S(1)}, f32[16,64,256]{2,1,0:T(8,128)S(1)}, f32[16,64,256]{2,1,0:T(8,128)S(1)}, f32[16,64,256]{2,1,0:T(8,128)S(1)},...) custom-call(f32[16,64,256]{2,1,0:T(8,128)S(1)} %get-tuple-element.59, ...), custom_call_target="tpu_custom_call" | custom-call | flops 31457280 | bytes 6291456 | tf_op jit(solution)/shard_map/pallas_call | solution.py:453
  10.6 0.8 %collective-permute-done.refs_0_ = f32[2,16,8,256]{3,2,1,0:T(8,128)S(1)} collective-permute-done((f32[2,16,8,256]{3,2,1,0:T(8,128)S(1)}, f32[2,16,8,256]{3,2,1,0:T(8,128)S(1)}, u32[]{:S(2)}, u32[]{:S(2)}) %collective-permute-start) | collective-permute-done | bytes 262176 | tf_op jit(solution)/shard_map/ppermute | solution.py:170
  11.4 0.0 collective-permute-done.1.refs_1_
  11.4 2.2 %collective-permute-start.3 = (f32[2,4,2,8,256]{4,3,2,1,0:T(8,128)S(1)}, f32[2,4,2,8,256]{4,3,2,1,0:T(8,128)S(1)}, u32[]{:S(2)}, u32[]{:S(2)}) collective-permute-start(f32[2,4,2,8,256]{4,3,2,1,0:T(8,128)S(1)} %get-tuple-element.79), channel_id=1, source_target_pairs={{0,4},{1,5},{2,6},{3,7},{4,0},{5,1},{6,2},{7,3},{8,12},{9,13},{10,... | collective-permute-start | bytes 393224 | tf_op jit(solution)/shard_map/ppermute | solution.py:170
  13.7 0.7 %collective-permute-start.5 = (f32[2,4,2,8,256]{4,3,2,1,0:T(8,128)S(1)}, f32[2,4,2,8,256]{4,3,2,1,0:T(8,128)S(1)}, u32[]{:S(2)}, u32[]{:S(2)}) collective-permute-start(f32[2,4,2,8,256]{4,3,2,1,0:T(8,128)S(1)} %get-tuple-element.94), channel_id=1, source_target_pairs={{4,8},{5,9},{6,10},{7,11},{8,4},{9,5},{10,6},{11,7},{20,24},{21,25... | collective-permute-start | bytes 393224 | tf_op jit(solution)/shard_map/ppermute | solution.py:170
  14.3 1.5 %shard_map.52 = (f32[16,64,256]{2,1,0:T(8,128)S(1)}, f32[16,64,256]{2,1,0:T(8,128)S(1)}, f32[16,64,256]{2,1,0:T(8,128)S(1)}, f32[16,64,256]{2,1,0:T(8,128)S(1)},...) custom-call(f32[16,64,256]{2,1,0:T(8,128)S(1)} %get-tuple-element.59, ...), custom_call_target="tpu_custom_call", output_to_operand_aliasing={{0}: (4, {}), {1}: (5, {}), {2}: (6, {}), {3}: (7, {}), {4}... | custom-call | tf_op jit(solution)/shard_map/pallas_call | solution.py:469
  15.8 0.0 collective-permute-done.2.refs_0_
  15.9 3.2 %shard_map.54 = (f32[16,64,256]{2,1,0:T(8,128)S(1)}, f32[16,64,256]{2,1,0:T(8,128)S(1)}, f32[16,64,256]{2,1,0:T(8,128)S(1)}, f32[16,64,256]{2,1,0:T(8,128)S(1)},...) custom-call(f32[16,64,256]{2,1,0:T(8,128)S(1)} %get-tuple-element.59, ...), custom_call_target="tpu_custom_call", output_to_operand_aliasing={{0}: (4, {}), {1}: (5, {}), {2}: (6, {}), {3}: (7, {}), {4}... | custom-call | tf_op jit(solution)/shard_map/pallas_call | solution.py:469
  19.1 0.0 collective-permute-done.5.refs_1_
  19.1 3.8 %shard_map.55 = (f32[16,64,256]{2,1,0:T(8,128)S(1)}, f32[16,64,256]{2,1,0:T(8,128)S(1)}, f32[16,64,256]{2,1,0:T(8,128)S(1)}, f32[16,64,256]{2,1,0:T(8,128)S(1)},...) custom-call(f32[16,64,256]{2,1,0:T(8,128)S(1)} %get-tuple-element.59, ...), custom_call_target="tpu_custom_call", output_to_operand_aliasing={{0}: (4, {}), {1}: (5, {}), {2}: (6, {}), {3}: (7, {}), {4}... | custom-call | tf_op jit(solution)/shard_map/pallas_call | solution.py:469
  22.9 0.0 copy-start
  22.9 1.0 %copy-done = f32[16,64,256]{2,1,0:T(8,128)} copy-done((f32[16,64,256]{2,1,0:T(8,128)}, f32[16,64,256]{2,1,0:T(8,128)S(1)}, u32[]{:S(2)}) %copy-start) | copy-done | bytes 1048600
  23.9 1.0 %copy-done.2 = f32[16,64,256]{2,1,0:T(8,128)} copy-done((f32[16,64,256]{2,1,0:T(8,128)}, f32[16,64,256]{2,1,0:T(8,128)S(1)}, u32[]{:S(2)}) %copy-start.2) | copy-done | bytes 1048600
  24.8 1.0 %copy-done.4 = f32[16,64,256]{2,1,0:T(8,128)} copy-done((f32[16,64,256]{2,1,0:T(8,128)}, f32[16,64,256]{2,1,0:T(8,128)S(1)}, u32[]{:S(2)}) %copy-start.4) | copy-done | bytes 1048600
  25.8 1.0 %copy-done.6 = f32[16,64,256]{2,1,0:T(8,128)} copy-done((f32[16,64,256]{2,1,0:T(8,128)}, f32[16,64,256]{2,1,0:T(8,128)S(1)}, u32[]{:S(2)}) %copy-start.6) | copy-done | bytes 1048600
  26.8 1.0 %copy-done.8 = f32[16,64,256]{2,1,0:T(8,128)} copy-done((f32[16,64,256]{2,1,0:T(8,128)}, f32[16,64,256]{2,1,0:T(8,128)S(1)}, u32[]{:S(2)}) %copy-start.8) | copy-done | bytes 1048600
  27.8 1.0 %copy-done.10 = f32[16,64,256]{2,1,0:T(8,128)} copy-done((f32[16,64,256]{2,1,0:T(8,128)}, f32[16,64,256]{2,1,0:T(8,128)S(1)}, u32[]{:S(2)}) %copy-start.10) | copy-done | bytes 1048600
  28.7 8.4 %all_to_all.10.m_ref = f32[4,8,128]{2,1,0:T(8,128)} all-to-all(f32[4,8,128]{2,1,0:T(8,128)S(1)} %get-tuple-element.107), channel_id=1, replica_groups=mesh['group'=2,'wide'=4,'narrow'=4] {'wide'}, dimensions={0} | all-to-all | bytes 32768 | tf_op jit(solution)/shard_map/all_to_all | solution.py:433
  37.2 1.4 %shard_map.56 = f32[4,8,128]{2,1,0:T(8,128)} custom-call(f32[4,8,128]{2,1,0:T(8,128)} %all_to_all.10.m_ref), custom_call_target="tpu_custom_call" | custom-call | tf_op jit(solution)/shard_map/pallas_call | solution.py:435
  38.6 12.9 %all_to_all.11.m_ref = f32[4,8,128]{2,1,0:T(8,128)S(1)} all-to-all(f32[4,8,128]{2,1,0:T(8,128)} %shard_map.56), channel_id=1, replica_groups=mesh['group'=2,'wide'=4,'narrow'=4] {'narrow'}, dimensions={0} | all-to-all | bytes 32768 | tf_op jit(solution)/shard_map/all_to_all | solution.py:441
  51.4 1.2 %copy-done.1 = f32[16,64,256]{2,1,0:T(8,128)S(1)} copy-done((f32[16,64,256]{2,1,0:T(8,128)S(1)}, f32[16,64,256]{2,1,0:T(8,128)}, u32[]{:S(2)}) %copy-start.1) | copy-done | bytes 1048600
  52.6 1.2 %copy-done.3 = f32[16,64,256]{2,1,0:T(8,128)S(1)} copy-done((f32[16,64,256]{2,1,0:T(8,128)S(1)}, f32[16,64,256]{2,1,0:T(8,128)}, u32[]{:S(2)}) %copy-start.3) | copy-done | bytes 1048600
  53.9 1.2 %copy-done.5 = f32[16,64,256]{2,1,0:T(8,128)S(1)} copy-done((f32[16,64,256]{2,1,0:T(8,128)S(1)}, f32[16,64,256]{2,1,0:T(8,128)}, u32[]{:S(2)}) %copy-start.5) | copy-done | bytes 1048600
  55.1 1.2 %copy-done.7 = f32[16,64,256]{2,1,0:T(8,128)S(1)} copy-done((f32[16,64,256]{2,1,0:T(8,128)S(1)}, f32[16,64,256]{2,1,0:T(8,128)}, u32[]{:S(2)}) %copy-start.7) | copy-done | bytes 1048600
  56.3 1.2 %copy-done.9 = f32[16,64,256]{2,1,0:T(8,128)S(1)} copy-done((f32[16,64,256]{2,1,0:T(8,128)S(1)}, f32[16,64,256]{2,1,0:T(8,128)}, u32[]{:S(2)}) %copy-start.9) | copy-done | bytes 1048600
  57.5 1.2 %copy-done.11 = f32[16,64,256]{2,1,0:T(8,128)S(1)} copy-done((f32[16,64,256]{2,1,0:T(8,128)S(1)}, f32[16,64,256]{2,1,0:T(8,128)}, u32[]{:S(2)}) %copy-start.11) | copy-done | bytes 1048600
  58.8 3.0 %shard_map.57 = (f32[16,64,256]{2,1,0:T(8,128)}, f32[16,64,256]{2,1,0:T(8,128)}) custom-call(f32[4,8,128]{2,1,0:T(8,128)S(1)} %all_to_all.11.m_ref, f32[16,64,256]{2,1,0:T(8,128)S(1)} %get-tuple-element.59.b_ref, f32[16,64,256]{2,1,0:T(8,128)S(1)} %get-tuple-element.108.refs_0_, f32[16,64,256]{2,1,0:T(8,128)S(1)} %get-tuple-element.109.refs_1_, ...), custom_call_target="tpu_custom_call" | custom-call | tf_op jit(solution)/shard_map/pallas_call | solution.py:545
  (14 shorter events, 0.1 us)
Async XLA Ops:
  2.7 13.2 %collective-permute-start.2 = (f32[15,64,256]{2,1,0:T(8,128)S(1)}, f32[15,64,256]{2,1,0:T(8,128)S(1)}, u32[]{:S(2)}, u32[]{:S(2)}) collective-permute-start(f32[15,64,256]{2,1,0:T(8,128)S(1)} %get-tuple-element.78), channel_id=1, source_target_pairs={{0,4},{1,5},{2,6},{3,7},{4,0},{5,1},{6,2},{7,3},{8,12},{9,13},{10,... | collective-permute-start | bytes 2949128 | tf_op jit(solution)/shard_map/ppermute | solution.py:170
  3.2 15.9 %collective-permute-start.4 = (f32[15,64,256]{2,1,0:T(8,128)S(1)}, f32[15,64,256]{2,1,0:T(8,128)S(1)}, u32[]{:S(2)}, u32[]{:S(2)}) collective-permute-start(f32[15,64,256]{2,1,0:T(8,128)S(1)} %get-tuple-element.93), channel_id=1, source_target_pairs={{4,8},{5,9},{6,10},{7,11},{8,4},{9,5},{10,6},{11,7},{20,24},{21,25... | collective-permute-start | bytes 2949128 | tf_op jit(solution)/shard_map/ppermute | solution.py:170
  3.9 7.5 %collective-permute-start = (f32[2,16,8,256]{3,2,1,0:T(8,128)S(1)}, f32[2,16,8,256]{3,2,1,0:T(8,128)S(1)}, u32[]{:S(2)}, u32[]{:S(2)}) collective-permute-start(f32[2,16,8,256]{3,2,1,0:T(8,128)S(1)} %get-tuple-element.63), channel_id=1, source_target_pairs={{0,1},{1,0},{2,3},{3,2},{4,5},{5,4},{6,7},{7,6},{8,9},{9,8},{10,11... | collective-permute-start | bytes 786440 | tf_op jit(solution)/shard_map/ppermute | solution.py:170
  6.6 4.8 %collective-permute-start.1 = (f32[2,16,8,256]{3,2,1,0:T(8,128)S(1)}, f32[2,16,8,256]{3,2,1,0:T(8,128)S(1)}, u32[]{:S(2)}, u32[]{:S(2)}) collective-permute-start(f32[2,16,8,256]{3,2,1,0:T(8,128)S(1)} %get-tuple-element.64), channel_id=1, source_target_pairs={{1,2},{2,1},{5,6},{6,5},{9,10},{10,9},{13,14},{14,13},{17,18},{18,... | collective-permute-start | bytes 786440 | tf_op jit(solution)/shard_map/ppermute | solution.py:170
  11.4 4.4 %collective-permute-start.3 = (f32[2,4,2,8,256]{4,3,2,1,0:T(8,128)S(1)}, f32[2,4,2,8,256]{4,3,2,1,0:T(8,128)S(1)}, u32[]{:S(2)}, u32[]{:S(2)}) collective-permute-start(f32[2,4,2,8,256]{4,3,2,1,0:T(8,128)S(1)} %get-tuple-element.79), channel_id=1, source_target_pairs={{0,4},{1,5},{2,6},{3,7},{4,0},{5,1},{6,2},{7,3},{8,12},{9,13},{10,... | collective-permute-start | bytes 393224 | tf_op jit(solution)/shard_map/ppermute | solution.py:170
  13.7 5.4 %collective-permute-start.5 = (f32[2,4,2,8,256]{4,3,2,1,0:T(8,128)S(1)}, f32[2,4,2,8,256]{4,3,2,1,0:T(8,128)S(1)}, u32[]{:S(2)}, u32[]{:S(2)}) collective-permute-start(f32[2,4,2,8,256]{4,3,2,1,0:T(8,128)S(1)} %get-tuple-element.94), channel_id=1, source_target_pairs={{4,8},{5,9},{6,10},{7,11},{8,4},{9,5},{10,6},{11,7},{20,24},{21,25... | collective-permute-start | bytes 393224 | tf_op jit(solution)/shard_map/ppermute | solution.py:170
  22.9 1.0 %copy-start = (f32[16,64,256]{2,1,0:T(8,128)}, f32[16,64,256]{2,1,0:T(8,128)S(1)}, u32[]{:S(2)}) copy-start(f32[16,64,256]{2,1,0:T(8,128)S(1)} %get-tuple-element.110.refs_2_) | copy-start | bytes 3145732
  23.8 1.0 %copy-start.2 = (f32[16,64,256]{2,1,0:T(8,128)}, f32[16,64,256]{2,1,0:T(8,128)S(1)}, u32[]{:S(2)}) copy-start(f32[16,64,256]{2,1,0:T(8,128)S(1)} %get-tuple-element.111.refs_3_) | copy-start | bytes 3145732
  24.8 1.0 %copy-start.4 = (f32[16,64,256]{2,1,0:T(8,128)}, f32[16,64,256]{2,1,0:T(8,128)S(1)}, u32[]{:S(2)}) copy-start(f32[16,64,256]{2,1,0:T(8,128)S(1)} %get-tuple-element.112.refs_4_) | copy-start | bytes 3145732
  25.8 1.0 %copy-start.6 = (f32[16,64,256]{2,1,0:T(8,128)}, f32[16,64,256]{2,1,0:T(8,128)S(1)}, u32[]{:S(2)}) copy-start(f32[16,64,256]{2,1,0:T(8,128)S(1)} %get-tuple-element.113.refs_5_) | copy-start | bytes 3145732
  26.8 1.0 %copy-start.8 = (f32[16,64,256]{2,1,0:T(8,128)}, f32[16,64,256]{2,1,0:T(8,128)S(1)}, u32[]{:S(2)}) copy-start(f32[16,64,256]{2,1,0:T(8,128)S(1)} %get-tuple-element.114.refs_6_) | copy-start | bytes 3145732
  27.8 1.0 %copy-start.10 = (f32[16,64,256]{2,1,0:T(8,128)}, f32[16,64,256]{2,1,0:T(8,128)S(1)}, u32[]{:S(2)}) copy-start(f32[16,64,256]{2,1,0:T(8,128)S(1)} %get-tuple-element.115.refs_7_) | copy-start | bytes 3145732
  51.4 1.2 %copy-start.1 = (f32[16,64,256]{2,1,0:T(8,128)S(1)}, f32[16,64,256]{2,1,0:T(8,128)}, u32[]{:S(2)}) copy-start(f32[16,64,256]{2,1,0:T(8,128)} %copy-done) | copy-start | bytes 3145732
  52.6 1.2 %copy-start.3 = (f32[16,64,256]{2,1,0:T(8,128)S(1)}, f32[16,64,256]{2,1,0:T(8,128)}, u32[]{:S(2)}) copy-start(f32[16,64,256]{2,1,0:T(8,128)} %copy-done.2) | copy-start | bytes 3145732
  53.9 1.2 %copy-start.5 = (f32[16,64,256]{2,1,0:T(8,128)S(1)}, f32[16,64,256]{2,1,0:T(8,128)}, u32[]{:S(2)}) copy-start(f32[16,64,256]{2,1,0:T(8,128)} %copy-done.4) | copy-start | bytes 3145732
  55.1 1.2 %copy-start.7 = (f32[16,64,256]{2,1,0:T(8,128)S(1)}, f32[16,64,256]{2,1,0:T(8,128)}, u32[]{:S(2)}) copy-start(f32[16,64,256]{2,1,0:T(8,128)} %copy-done.6) | copy-start | bytes 3145732
  56.3 1.2 %copy-start.9 = (f32[16,64,256]{2,1,0:T(8,128)S(1)}, f32[16,64,256]{2,1,0:T(8,128)}, u32[]{:S(2)}) copy-start(f32[16,64,256]{2,1,0:T(8,128)} %copy-done.8) | copy-start | bytes 3145732
  57.5 1.2 %copy-start.11 = (f32[16,64,256]{2,1,0:T(8,128)S(1)}, f32[16,64,256]{2,1,0:T(8,128)}, u32[]{:S(2)}) copy-start(f32[16,64,256]{2,1,0:T(8,128)} %copy-done.10) | copy-start | bytes 3145732

commit v6 on v5

--- a/solution.py
+++ b/solution.py
@@ -17,6 +17,7 @@
 
 LANES = 128
 QUARTER = LANES // 4
+CHUNKS = 4
 AXES = ("wide", "narrow")
 VMEM = pl.BlockSpec(memory_space=pltpu.VMEM)
 HBM = pl.BlockSpec(memory_space=pltpu.HBM)
@@ -53,9 +54,9 @@
     return fast_two_sum(total, error + (a[1] + b[1]))
 
 
-def pair_scale(a, factor):
+def loose_scale(a, factor):
     product, error = two_product(a[0], factor)
-    return fast_two_sum(product, error + a[1] * factor)
+    return product, error + a[1] * factor
 
 
 def sides():
@@ -75,11 +76,9 @@
     (b_ref, c_ref, r_ref), (pack, done) = refs[:3], refs[3:]
     rows, columns = b_ref.shape[:2]
     h = STEPS
-    copies = [pltpu.make_async_copy(args[k], refs[k], done.at[k]) for k in range(3)]
+    copies = [pltpu.make_async_copy(args[k], refs[k], done.at[k]) for k in (1, 2, 0)]
     for copy in copies:
         copy.start()
-    for copy in copies:
-        copy.wait()
     wide, narrow = sides()
     left = [pl.multiple_of(jnp.where(up, columns - h, 0), 8) for up in narrow]
 
@@ -100,8 +99,11 @@
             w_out[a][h + d - 1] = pack[at]
         return 0
 
-    lax.fori_loop(0, rows, code, 0)
-    lax.fori_loop(0, rows, edges, 0)
+    copies[0].wait()
+    copies[1].wait()
+    lax.fori_loop(0, rows, code, 0, unroll=2)
+    copies[2].wait()
+    lax.fori_loop(0, rows, edges, 0, unroll=4)
     lax.fori_loop(1, h, layers, 0)
     for a in range(2):
         at = edge_layer(wide[a], rows, h)
@@ -420,27 +422,6 @@
     return total, error
 
 
-def relay_kernel(m_ref, out_ref):
-    total, error = summed(m_ref)
-    lane = lax.broadcasted_iota(jnp.int32, (8, LANES), 1)
-    low = lax.rem(lane // QUARTER, 2) == 1
-    message = total + jnp.where(low, pltpu.roll(error, QUARTER, 1), 0.0)
-    for k in range(out_ref.shape[0]):
-        out_ref[k] = message
-
-
-def gather(message):
-    over_wide = lax.all_to_all(message, "wide", 0, 0, tiled=True)
-    shape = (lax.axis_size("narrow"), 8, LANES)
-    relayed = pl.pallas_call(
-        relay_kernel,
-        out_shape=jax.ShapeDtypeStruct(shape, jnp.float32),
-        in_specs=[VMEM],
-        out_specs=VMEM,
-    )(over_wide)
-    return lax.all_to_all(relayed, "narrow", 0, 0, tiled=True)
-
-
 def state_shapes(b):
     rows, columns, depth = b.shape
     wide, narrow = rows + 2 * STEPS, columns + 2 * STEPS
@@ -496,13 +477,15 @@
     search_coord = resid_coord
     sol_coord = jnp.zeros(shape, jnp.float32)
     for i in range(STEPS):
-        mapped = pair_add((later(search[0]), later(search[1])), search)
+        mapped, lost = two_sum(later(search[0]), search[0])
+        lost = lost + (later(search[1]) + search[1])
         old = residual[0][i : i + 1]
-        length = old / mapped[0][i : i + 1]
+        inverse = 1.0 / old
+        length = old / mapped[i : i + 1]
         lengths = spread(length)
-        residual = pair_add(residual, pair_scale(mapped, -lengths))
-        grown = spread(-length * residual[0][i + 1 : i + 2] / old)
-        search = pair_add(residual, pair_scale(search, grown))
+        residual = pair_add(residual, loose_scale((mapped, lost), -lengths))
+        grown = spread(-length * inverse * residual[0][i + 1 : i + 2])
+        search = pair_add(residual, loose_scale(search, grown))
         sol_coord = sol_coord + (lengths * (1.0 / SCALE)) * search_coord
         resid_coord = resid_coord - lengths * (raised(search_coord) + search_coord)
         search_coord = resid_coord + grown * search_coord
@@ -510,7 +493,8 @@
 
 
 def combine_kernel(m_ref, b_ref, *refs):
-    field, (x_ref, r_ref) = refs[:STEPS], refs[STEPS:]
+    field, outs, (x_ref, r_ref, done) = refs[:STEPS], refs[STEPS : STEPS + 2], refs[STEPS + 2 :]
+    rows = b_ref.shape[0]
     total, error = summed(m_ref)
 
     def lane(v, k):
@@ -538,7 +522,17 @@
                 r_ref[at] = r
         return 0
 
-    lax.fori_loop(0, b_ref.shape[0], plane, 0)
+    copies = []
+    for chunk in range(CHUNKS):
+        part = pl.ds(chunk * rows // CHUNKS, rows // CHUNKS)
+        lax.fori_loop(part.start, part.start + part.size, plane, 0)
+        for k, source in enumerate((x_ref, r_ref)):
+            copies.append(
+                pltpu.make_async_copy(source.at[part], outs[k].at[part], done.at[k, chunk])
+            )
+            copies[-1].start()
+    for copy in copies:
+        copy.wait()
 
 
 def combine(gathered, b, fields):
@@ -546,12 +540,15 @@
         combine_kernel,
         out_shape=[jax.ShapeDtypeStruct(b.shape, jnp.float32)] * 2,
         in_specs=[VMEM] * (STEPS + 2),
-        out_specs=[VMEM] * 2,
+        out_specs=[HBM] * 2,
+        scratch_shapes=[pltpu.VMEM(b.shape, jnp.float32)] * 2
+        + [pltpu.SemaphoreType.DMA((2, CHUNKS))],
         compiler_params=pltpu.CompilerParams(vmem_limit_bytes=20 * MIB),
     )(gathered, b, *fields)
 
 
 def on_device(right_side, conduct_half, reaction_half):
+    peers = lax.axis_size("wide") * lax.axis_size("narrow")
     *sent, b, c, r = messages(right_side, conduct_half, reaction_half)
     far, near = swapped(sent[1], 1, None), swapped(sent[0], 0, None)
     narrow_halos = [swapped(sent[2 + k], None, k) for k in range(2)]
@@ -560,10 +557,10 @@
     diagonal = [swapped(block, k, None) for k, block in enumerate(diagonal)]
     state, moments = onward(border_kernel, b, moments, narrow_halos, state, moments.shape)
     for pairing, received in enumerate(([near, diagonal[0]], [far, diagonal[1]])):
-        shape = (lax.axis_size("wide"), 8, LANES) if pairing else moments.shape
+        shape = (peers, 8, LANES) if pairing else moments.shape
         kernel = functools.partial(outer_kernel, pairing)
         state, moments = onward(kernel, b, moments, received, state, shape)
-    gathered, fields = gather(moments), state[:STEPS]
+    gathered, fields = lax.all_to_all(moments, AXES, 0, 0, tiled=True), state[:STEPS]
     solution, residual = combine(gathered, b, fields)
     return (solution, residual)
 

time: 62.3 us -> 41.9 us (0.67)
  local copies, waits for them, and re-layouts: 13.2 us -> 0 us
  blocking collectives: 21.3 us -> 16.6 us
  Pallas kernels: 18.3 us -> 16 us
    unnamed x24 -> x0, local copies, waits for them, and re-layouts: 13.2 us -> none
    all_to_all x2 -> x1, blocking collectives: 21.3 us -> 16.6 us  [on_device(): lax.all_to_all(moments, AXES, 0, 0, tiled=True)]
    pallas_call x1 -> x0, Pallas kernels: 1.39 us -> none  [gather(): pl.pallas_call(relay_kernel, out_shape=jax.ShapeDtypeStruct(shape, jnp.fl...]
  transfers between devices with their start and end apart: 6 -> 6, of which waited for: 1 -> 1; matrix products, arithmetic and copies ran while one was open for 0% -> 0% of each run, Pallas kernels for 13% -> 19%
where the time goes in v6:
time: 41.9 us; the launch traced here: 41.7 us
  blocking collectives  16.6 us (40%)
  Pallas kernels  16 us (38%)
  starting transfers between devices  7.46 us (18%)
  waiting for transfers between devices  0.82 us (2%)
  between operations  0.72 us (2%)
    all_to_all x1, blocking collectives, on_device(): lax.all_to_all(moments, AXES, 0, 0, tiled=True)  16.6 us
    pallas_call x3, Pallas kernels, onward(): pl.pallas_call(kernel, out_shape=shapes, in_specs=[VMEM] * (others + len(...  8.47 us
    ppermute x6, starting transfers between devices, swapped(): return lax.ppermute(array, AXES, pairs)  7.46 us
    pallas_call x1, Pallas kernels, inner(): pl.pallas_call(inner_kernel, cost_estimate=pl.CostEstimate(flops=120 * b....  3.31 us
    pallas_call x1, Pallas kernels, combine(): pl.pallas_call(combine_kernel, out_shape=[jax.ShapeDtypeStruct(b.shape, j...  2.44 us
    pallas_call x1, Pallas kernels, messages(): pl.pallas_call(send_kernel, out_shape=[jax.ShapeDtypeStruct(s, jnp.float3...  1.77 us
  transfers between devices with their start and end apart: 6, of which 1 were waited for; matrix products, arithmetic and copies ran while one was open for 0% of the time, Pallas kernels for 19%

profile of v6, /device:TPU:0, one launch (start us, length us, event | category | flops | bytes accessed | tf_op | source)
XLA Modules:
  0.0 41.7 jit_solution(2683288627185832605)
XLA Ops:
  0.6 1.8 %shard_map.50 = (f32[15,64,256]{2,1,0:T(8,128)S(1)}, f32[15,64,256]{2,1,0:T(8,128)S(1)}, f32[2,16,8,256]{3,2,1,0:T(8,128)S(1)}, f32[2,16,8,256]{3,2,1,0:T(8,128)...) custom-call(f32[16,64,256]{2,1,0:T(8,128)} %refs_0_.1, ...), custom_call_target="tpu_custom_call" | custom-call | tf_op jit(solution)/shard_map/pallas_call | solution.py:117
  2.4 0.5 %collective-permute-start.2 = (f32[15,64,256]{2,1,0:T(8,128)S(1)}, f32[15,64,256]{2,1,0:T(8,128)S(1)}, u32[]{:S(2)}, u32[]{:S(2)}) collective-permute-start(f32[15,64,256]{2,1,0:T(8,128)S(1)} %get-tuple-element.78), channel_id=1, source_target_pairs={{0,4},{1,5},{2,6},{3,7},{4,0},{5,1},{6,2},{7,3},{8,12},{9,13},{10,... | collective-permute-start | bytes 2949128 | tf_op jit(solution)/shard_map/ppermute | solution.py:172
  2.9 0.7 %collective-permute-start.4 = (f32[15,64,256]{2,1,0:T(8,128)S(1)}, f32[15,64,256]{2,1,0:T(8,128)S(1)}, u32[]{:S(2)}, u32[]{:S(2)}) collective-permute-start(f32[15,64,256]{2,1,0:T(8,128)S(1)} %get-tuple-element.93), channel_id=1, source_target_pairs={{4,8},{5,9},{6,10},{7,11},{8,4},{9,5},{10,6},{11,7},{20,24},{21,25... | collective-permute-start | bytes 2949128 | tf_op jit(solution)/shard_map/ppermute | solution.py:172
  3.6 2.7 %collective-permute-start = (f32[2,16,8,256]{3,2,1,0:T(8,128)S(1)}, f32[2,16,8,256]{3,2,1,0:T(8,128)S(1)}, u32[]{:S(2)}, u32[]{:S(2)}) collective-permute-start(f32[2,16,8,256]{3,2,1,0:T(8,128)S(1)} %get-tuple-element.63), channel_id=1, source_target_pairs={{0,1},{1,0},{2,3},{3,2},{4,5},{5,4},{6,7},{7,6},{8,9},{9,8},{10,11... | collective-permute-start | bytes 786440 | tf_op jit(solution)/shard_map/ppermute | solution.py:172
  6.3 0.7 %collective-permute-start.1 = (f32[2,16,8,256]{3,2,1,0:T(8,128)S(1)}, f32[2,16,8,256]{3,2,1,0:T(8,128)S(1)}, u32[]{:S(2)}, u32[]{:S(2)}) collective-permute-start(f32[2,16,8,256]{3,2,1,0:T(8,128)S(1)} %get-tuple-element.64), channel_id=1, source_target_pairs={{1,2},{2,1},{5,6},{6,5},{9,10},{10,9},{13,14},{14,13},{17,18},{18,... | collective-permute-start | bytes 786440 | tf_op jit(solution)/shard_map/ppermute | solution.py:172
  7.0 3.3 %shard_map.51 = (f32[16,64,256]{2,1,0:T(8,128)S(1)}, f32[16,64,256]{2,1,0:T(8,128)S(1)}, f32[16,64,256]{2,1,0:T(8,128)S(1)}, f32[16,64,256]{2,1,0:T(8,128)S(1)},...) custom-call(f32[16,64,256]{2,1,0:T(8,128)S(1)} %get-tuple-element.59, ...), custom_call_target="tpu_custom_call" | custom-call | flops 31457280 | bytes 6291456 | tf_op jit(solution)/shard_map/pallas_call | solution.py:434
  10.3 0.8 %collective-permute-done.refs_0_ = f32[2,16,8,256]{3,2,1,0:T(8,128)S(1)} collective-permute-done((f32[2,16,8,256]{3,2,1,0:T(8,128)S(1)}, f32[2,16,8,256]{3,2,1,0:T(8,128)S(1)}, u32[]{:S(2)}, u32[]{:S(2)}) %collective-permute-start) | collective-permute-done | bytes 262176 | tf_op jit(solution)/shard_map/ppermute | solution.py:172
  11.1 0.0 collective-permute-done.1.refs_1_
  11.2 2.2 %collective-permute-start.3 = (f32[2,4,2,8,256]{4,3,2,1,0:T(8,128)S(1)}, f32[2,4,2,8,256]{4,3,2,1,0:T(8,128)S(1)}, u32[]{:S(2)}, u32[]{:S(2)}) collective-permute-start(f32[2,4,2,8,256]{4,3,2,1,0:T(8,128)S(1)} %get-tuple-element.79), channel_id=1, source_target_pairs={{0,4},{1,5},{2,6},{3,7},{4,0},{5,1},{6,2},{7,3},{8,12},{9,13},{10,... | collective-permute-start | bytes 393224 | tf_op jit(solution)/shard_map/ppermute | solution.py:172
  13.4 0.7 %collective-permute-start.5 = (f32[2,4,2,8,256]{4,3,2,1,0:T(8,128)S(1)}, f32[2,4,2,8,256]{4,3,2,1,0:T(8,128)S(1)}, u32[]{:S(2)}, u32[]{:S(2)}) collective-permute-start(f32[2,4,2,8,256]{4,3,2,1,0:T(8,128)S(1)} %get-tuple-element.94), channel_id=1, source_target_pairs={{4,8},{5,9},{6,10},{7,11},{8,4},{9,5},{10,6},{11,7},{20,24},{21,25... | collective-permute-start | bytes 393224 | tf_op jit(solution)/shard_map/ppermute | solution.py:172
  14.1 1.5 %shard_map.52 = (f32[16,64,256]{2,1,0:T(8,128)S(1)}, f32[16,64,256]{2,1,0:T(8,128)S(1)}, f32[16,64,256]{2,1,0:T(8,128)S(1)}, f32[16,64,256]{2,1,0:T(8,128)S(1)},...) custom-call(f32[16,64,256]{2,1,0:T(8,128)S(1)} %get-tuple-element.59, ...), custom_call_target="tpu_custom_call", output_to_operand_aliasing={{0}: (4, {}), {1}: (5, {}), {2}: (6, {}), {3}: (7, {}), {4}... | custom-call | tf_op jit(solution)/shard_map/pallas_call | solution.py:450
  15.6 0.0 collective-permute-done.3.refs_1_
  15.6 0.0 collective-permute-done.2.refs_0_
  15.6 3.2 %shard_map.54 = (f32[16,64,256]{2,1,0:T(8,128)S(1)}, f32[16,64,256]{2,1,0:T(8,128)S(1)}, f32[16,64,256]{2,1,0:T(8,128)S(1)}, f32[16,64,256]{2,1,0:T(8,128)S(1)},...) custom-call(f32[16,64,256]{2,1,0:T(8,128)S(1)} %get-tuple-element.59, ...), custom_call_target="tpu_custom_call", output_to_operand_aliasing={{0}: (4, {}), {1}: (5, {}), {2}: (6, {}), {3}: (7, {}), {4}... | custom-call | tf_op jit(solution)/shard_map/pallas_call | solution.py:450
  18.8 0.0 collective-permute-done.5.refs_1_
  18.8 0.0 collective-permute-done.4.refs_0_
  18.8 3.8 %shard_map.55 = (f32[16,64,256]{2,1,0:T(8,128)S(1)}, f32[16,64,256]{2,1,0:T(8,128)S(1)}, f32[16,64,256]{2,1,0:T(8,128)S(1)}, f32[16,64,256]{2,1,0:T(8,128)S(1)},...) custom-call(f32[16,64,256]{2,1,0:T(8,128)S(1)} %get-tuple-element.59, ...), custom_call_target="tpu_custom_call", output_to_operand_aliasing={{0}: (4, {}), {1}: (5, {}), {2}: (6, {}), {3}: (7, {}), {4}... | custom-call | tf_op jit(solution)/shard_map/pallas_call | solution.py:450
  22.6 16.6 %all_to_all.5.m_ref = f32[16,8,128]{2,1,0:T(8,128)S(1)} all-to-all(f32[16,8,128]{2,1,0:T(8,128)S(1)} %get-tuple-element.107), channel_id=1, replica_groups=mesh['group'=2,'wide'=4,'narrow'=4] {'wide','narrow'}, dimensions={0} | all-to-all | bytes 131072 | tf_op jit(solution)/shard_map/all_to_all | solution.py:563
  39.2 2.4 %shard_map.56 = (f32[16,64,256]{2,1,0:T(8,128)}, f32[16,64,256]{2,1,0:T(8,128)}) custom-call(f32[16,8,128]{2,1,0:T(8,128)S(1)} %all_to_all.5.m_ref, f32[16,64,256]{2,1,0:T(8,128)S(1)} %get-tuple-element.59.b_ref, f32[16,64,256]{2,1,0:T(8,128)S(1)} %get-tuple-element.108.refs_0_, f32[16,64,256]{2,1,0:T(8,128)S(1)} %get-tuple-element.109.refs_1_, ...), custom_call_target="tpu_custom_call" | custom-call | tf_op jit(solution)/shard_map/pallas_call | solution.py:539
  (1 shorter events, 0.0 us)
Async XLA Ops:
  2.4 13.2 %collective-permute-start.2 = (f32[15,64,256]{2,1,0:T(8,128)S(1)}, f32[15,64,256]{2,1,0:T(8,128)S(1)}, u32[]{:S(2)}, u32[]{:S(2)}) collective-permute-start(f32[15,64,256]{2,1,0:T(8,128)S(1)} %get-tuple-element.78), channel_id=1, source_target_pairs={{0,4},{1,5},{2,6},{3,7},{4,0},{5,1},{6,2},{7,3},{8,12},{9,13},{10,... | collective-permute-start | bytes 2949128 | tf_op jit(solution)/shard_map/ppermute | solution.py:172
  2.9 15.9 %collective-permute-start.4 = (f32[15,64,256]{2,1,0:T(8,128)S(1)}, f32[15,64,256]{2,1,0:T(8,128)S(1)}, u32[]{:S(2)}, u32[]{:S(2)}) collective-permute-start(f32[15,64,256]{2,1,0:T(8,128)S(1)} %get-tuple-element.93), channel_id=1, source_target_pairs={{4,8},{5,9},{6,10},{7,11},{8,4},{9,5},{10,6},{11,7},{20,24},{21,25... | collective-permute-start | bytes 2949128 | tf_op jit(solution)/shard_map/ppermute | solution.py:172
  3.6 7.5 %collective-permute-start = (f32[2,16,8,256]{3,2,1,0:T(8,128)S(1)}, f32[2,16,8,256]{3,2,1,0:T(8,128)S(1)}, u32[]{:S(2)}, u32[]{:S(2)}) collective-permute-start(f32[2,16,8,256]{3,2,1,0:T(8,128)S(1)} %get-tuple-element.63), channel_id=1, source_target_pairs={{0,1},{1,0},{2,3},{3,2},{4,5},{5,4},{6,7},{7,6},{8,9},{9,8},{10,11... | collective-permute-start | bytes 786440 | tf_op jit(solution)/shard_map/ppermute | solution.py:172
  6.3 4.8 %collective-permute-start.1 = (f32[2,16,8,256]{3,2,1,0:T(8,128)S(1)}, f32[2,16,8,256]{3,2,1,0:T(8,128)S(1)}, u32[]{:S(2)}, u32[]{:S(2)}) collective-permute-start(f32[2,16,8,256]{3,2,1,0:T(8,128)S(1)} %get-tuple-element.64), channel_id=1, source_target_pairs={{1,2},{2,1},{5,6},{6,5},{9,10},{10,9},{13,14},{14,13},{17,18},{18,... | collective-permute-start | bytes 786440 | tf_op jit(solution)/shard_map/ppermute | solution.py:172
  11.2 4.4 %collective-permute-start.3 = (f32[2,4,2,8,256]{4,3,2,1,0:T(8,128)S(1)}, f32[2,4,2,8,256]{4,3,2,1,0:T(8,128)S(1)}, u32[]{:S(2)}, u32[]{:S(2)}) collective-permute-start(f32[2,4,2,8,256]{4,3,2,1,0:T(8,128)S(1)} %get-tuple-element.79), channel_id=1, source_target_pairs={{0,4},{1,5},{2,6},{3,7},{4,0},{5,1},{6,2},{7,3},{8,12},{9,13},{10,... | collective-permute-start | bytes 393224 | tf_op jit(solution)/shard_map/ppermute | solution.py:172
  13.4 5.4 %collective-permute-start.5 = (f32[2,4,2,8,256]{4,3,2,1,0:T(8,128)S(1)}, f32[2,4,2,8,256]{4,3,2,1,0:T(8,128)S(1)}, u32[]{:S(2)}, u32[]{:S(2)}) collective-permute-start(f32[2,4,2,8,256]{4,3,2,1,0:T(8,128)S(1)} %get-tuple-element.94), channel_id=1, source_target_pairs={{4,8},{5,9},{6,10},{7,11},{8,4},{9,5},{10,6},{11,7},{20,24},{21,25... | collective-permute-start | bytes 393224 | tf_op jit(solution)/shard_map/ppermute | solution.py:172

commit v7 on v6

--- a/solution.py
+++ b/solution.py
@@ -548,7 +548,6 @@
 
 
 def on_device(right_side, conduct_half, reaction_half):
-    peers = lax.axis_size("wide") * lax.axis_size("narrow")
     *sent, b, c, r = messages(right_side, conduct_half, reaction_half)
     far, near = swapped(sent[1], 1, None), swapped(sent[0], 0, None)
     narrow_halos = [swapped(sent[2 + k], None, k) for k in range(2)]
@@ -557,10 +556,10 @@
     diagonal = [swapped(block, k, None) for k, block in enumerate(diagonal)]
     state, moments = onward(border_kernel, b, moments, narrow_halos, state, moments.shape)
     for pairing, received in enumerate(([near, diagonal[0]], [far, diagonal[1]])):
-        shape = (peers, 8, LANES) if pairing else moments.shape
+        shape = (1, 8, LANES) if pairing else moments.shape
         kernel = functools.partial(outer_kernel, pairing)
         state, moments = onward(kernel, b, moments, received, state, shape)
-    gathered, fields = lax.all_to_all(moments, AXES, 0, 0, tiled=True), state[:STEPS]
+    gathered, fields = lax.all_gather(moments, AXES, axis=0, tiled=True), state[:STEPS]
     solution, residual = combine(gathered, b, fields)
     return (solution, residual)
 

time: 41.9 us -> 59.1 us (1.41)
  blocking collectives: 16.6 us -> 33.9 us
    all_gather x0 -> x1, blocking collectives: none -> 33.9 us  [on_device(): lax.all_gather(moments, AXES, axis=0, tiled=True)]
    all_to_all x1 -> x0, blocking collectives: 16.6 us -> none  [on_device(): lax.all_to_all(moments, AXES, 0, 0, tiled=True)]
  transfers between devices with their start and end apart: 6 -> 6, of which waited for: 1 -> 1; matrix products, arithmetic and copies ran while one was open for 0% -> 0% of each run, Pallas kernels for 19% -> 14%
where the time goes in v7:
time: 59.1 us; the launch traced here: 58.9 us
  blocking collectives  33.9 us (57%)
  Pallas kernels  16 us (27%)
  starting transfers between devices  7.46 us (13%)
  waiting for transfers between devices  0.82 us (1%)
  between operations  0.72 us (1%)
    all_gather x1, blocking collectives, on_device(): lax.all_gather(moments, AXES, axis=0, tiled=True)  33.9 us
    pallas_call x3, Pallas kernels, onward(): pl.pallas_call(kernel, out_shape=shapes, in_specs=[VMEM] * (others + len(...  8.47 us
    ppermute x6, starting transfers between devices, swapped(): return lax.ppermute(array, AXES, pairs)  7.46 us
    pallas_call x1, Pallas kernels, inner(): pl.pallas_call(inner_kernel, cost_estimate=pl.CostEstimate(flops=120 * b....  3.31 us
    pallas_call x1, Pallas kernels, combine(): pl.pallas_call(combine_kernel, out_shape=[jax.ShapeDtypeStruct(b.shape, j...  2.44 us
    pallas_call x1, Pallas kernels, messages(): pl.pallas_call(send_kernel, out_shape=[jax.ShapeDtypeStruct(s, jnp.float3...  1.77 us
  transfers between devices with their start and end apart: 6, of which 1 were waited for; matrix products, arithmetic and copies ran while one was open for 0% of the time, Pallas kernels for 14%

profile of v7, /device:TPU:0, one launch (start us, length us, event | category | flops | bytes accessed | tf_op | source)
XLA Modules:
  0.0 58.9 jit_solution(3258310990046435621)
XLA Ops:
  0.6 1.8 %shard_map.50 = (f32[15,64,256]{2,1,0:T(8,128)S(1)}, f32[15,64,256]{2,1,0:T(8,128)S(1)}, f32[2,16,8,256]{3,2,1,0:T(8,128)S(1)}, f32[2,16,8,256]{3,2,1,0:T(8,128)...) custom-call(f32[16,64,256]{2,1,0:T(8,128)} %refs_0_.1, ...), custom_call_target="tpu_custom_call" | custom-call | tf_op jit(solution)/shard_map/pallas_call | solution.py:117
  2.4 0.5 collective-permute-start.2
  2.9 0.7 %collective-permute-start.4 = (f32[15,64,256]{2,1,0:T(8,128)S(1)}, f32[15,64,256]{2,1,0:T(8,128)S(1)}, u32[]{:S(2)}, u32[]{:S(2)}) collective-permute-start(f32[15,64,256]{2,1,0:T(8,128)S(1)} %get-tuple-element.93), channel_id=1, source_target_pairs={{4,8},{5,9},{6,10},{7,11},{8,4},{9,5},{10,6},{11,7},{20,24},{21,25... | collective-permute-start | bytes 2949128 | tf_op jit(solution)/shard_map/ppermute | solution.py:172
  3.6 2.7 %collective-permute-start = (f32[2,16,8,256]{3,2,1,0:T(8,128)S(1)}, f32[2,16,8,256]{3,2,1,0:T(8,128)S(1)}, u32[]{:S(2)}, u32[]{:S(2)}) collective-permute-start(f32[2,16,8,256]{3,2,1,0:T(8,128)S(1)} %get-tuple-element.63), channel_id=1, source_target_pairs={{0,1},{1,0},{2,3},{3,2},{4,5},{5,4},{6,7},{7,6},{8,9},{9,8},{10,11... | collective-permute-start | bytes 786440 | tf_op jit(solution)/shard_map/ppermute | solution.py:172
  6.3 0.7 %collective-permute-start.1 = (f32[2,16,8,256]{3,2,1,0:T(8,128)S(1)}, f32[2,16,8,256]{3,2,1,0:T(8,128)S(1)}, u32[]{:S(2)}, u32[]{:S(2)}) collective-permute-start(f32[2,16,8,256]{3,2,1,0:T(8,128)S(1)} %get-tuple-element.64), channel_id=1, source_target_pairs={{1,2},{2,1},{5,6},{6,5},{9,10},{10,9},{13,14},{14,13},{17,18},{18,... | collective-permute-start | bytes 786440 | tf_op jit(solution)/shard_map/ppermute | solution.py:172
  7.0 3.3 %shard_map.51 = (f32[16,64,256]{2,1,0:T(8,128)S(1)}, f32[16,64,256]{2,1,0:T(8,128)S(1)}, f32[16,64,256]{2,1,0:T(8,128)S(1)}, f32[16,64,256]{2,1,0:T(8,128)S(1)},...) custom-call(f32[16,64,256]{2,1,0:T(8,128)S(1)} %get-tuple-element.59, ...), custom_call_target="tpu_custom_call" | custom-call | flops 31457280 | bytes 6291456 | tf_op jit(solution)/shard_map/pallas_call | solution.py:434
  10.3 0.8 %collective-permute-done.refs_0_ = f32[2,16,8,256]{3,2,1,0:T(8,128)S(1)} collective-permute-done((f32[2,16,8,256]{3,2,1,0:T(8,128)S(1)}, f32[2,16,8,256]{3,2,1,0:T(8,128)S(1)}, u32[]{:S(2)}, u32[]{:S(2)}) %collective-permute-start) | collective-permute-done | bytes 262176 | tf_op jit(solution)/shard_map/ppermute | solution.py:172
  11.1 0.0 collective-permute-done.1.refs_1_
  11.2 2.2 %collective-permute-start.3 = (f32[2,4,2,8,256]{4,3,2,1,0:T(8,128)S(1)}, f32[2,4,2,8,256]{4,3,2,1,0:T(8,128)S(1)}, u32[]{:S(2)}, u32[]{:S(2)}) collective-permute-start(f32[2,4,2,8,256]{4,3,2,1,0:T(8,128)S(1)} %get-tuple-element.79), channel_id=1, source_target_pairs={{0,4},{1,5},{2,6},{3,7},{4,0},{5,1},{6,2},{7,3},{8,12},{9,13},{10,... | collective-permute-start | bytes 393224 | tf_op jit(solution)/shard_map/ppermute | solution.py:172
  13.4 0.7 %collective-permute-start.5 = (f32[2,4,2,8,256]{4,3,2,1,0:T(8,128)S(1)}, f32[2,4,2,8,256]{4,3,2,1,0:T(8,128)S(1)}, u32[]{:S(2)}, u32[]{:S(2)}) collective-permute-start(f32[2,4,2,8,256]{4,3,2,1,0:T(8,128)S(1)} %get-tuple-element.94), channel_id=1, source_target_pairs={{4,8},{5,9},{6,10},{7,11},{8,4},{9,5},{10,6},{11,7},{20,24},{21,25... | collective-permute-start | bytes 393224 | tf_op jit(solution)/shard_map/ppermute | solution.py:172
  14.1 1.5 %shard_map.52 = (f32[16,64,256]{2,1,0:T(8,128)S(1)}, f32[16,64,256]{2,1,0:T(8,128)S(1)}, f32[16,64,256]{2,1,0:T(8,128)S(1)}, f32[16,64,256]{2,1,0:T(8,128)S(1)},...) custom-call(f32[16,64,256]{2,1,0:T(8,128)S(1)} %get-tuple-element.59, ...), custom_call_target="tpu_custom_call", output_to_operand_aliasing={{0}: (4, {}), {1}: (5, {}), {2}: (6, {}), {3}: (7, {}), {4}... | custom-call | tf_op jit(solution)/shard_map/pallas_call | solution.py:450
  15.6 0.0 collective-permute-done.3.refs_1_
  15.6 0.0 collective-permute-done.2.refs_0_
  15.6 3.2 %shard_map.54 = (f32[16,64,256]{2,1,0:T(8,128)S(1)}, f32[16,64,256]{2,1,0:T(8,128)S(1)}, f32[16,64,256]{2,1,0:T(8,128)S(1)}, f32[16,64,256]{2,1,0:T(8,128)S(1)},...) custom-call(f32[16,64,256]{2,1,0:T(8,128)S(1)} %get-tuple-element.59, ...), custom_call_target="tpu_custom_call", output_to_operand_aliasing={{0}: (4, {}), {1}: (5, {}), {2}: (6, {}), {3}: (7, {}), {4}... | custom-call | tf_op jit(solution)/shard_map/pallas_call | solution.py:450
  18.8 0.0 collective-permute-done.5.refs_1_
  18.8 0.0 collective-permute-done.4.refs_0_
  18.8 3.7 %shard_map.55 = (f32[16,64,256]{2,1,0:T(8,128)S(1)}, f32[16,64,256]{2,1,0:T(8,128)S(1)}, f32[16,64,256]{2,1,0:T(8,128)S(1)}, f32[16,64,256]{2,1,0:T(8,128)S(1)},...) custom-call(f32[16,64,256]{2,1,0:T(8,128)S(1)} %get-tuple-element.59, ...), custom_call_target="tpu_custom_call", output_to_operand_aliasing={{0}: (4, {}), {1}: (5, {}), {2}: (6, {}), {3}: (7, {}), {4}... | custom-call | tf_op jit(solution)/shard_map/pallas_call | solution.py:450
  22.6 33.9 %all_gather.3.m_ref = f32[16,8,128]{2,1,0:T(8,128)S(1)} all-gather(f32[1,8,128]{2,1,0:T(8,128)S(1)} %get-tuple-element.107), channel_id=1, replica_groups=mesh['group'=2,'wide'=4,'narrow'=4] {'wide','narrow'}, dimensions={0}, use_global_device_ids=true | all-gather | bytes 69632 | tf_op jit(solution)/shard_map/all_gather | solution.py:562
  56.5 2.4 %shard_map.56 = (f32[16,64,256]{2,1,0:T(8,128)}, f32[16,64,256]{2,1,0:T(8,128)}) custom-call(f32[16,8,128]{2,1,0:T(8,128)S(1)} %all_gather.3.m_ref, f32[16,64,256]{2,1,0:T(8,128)S(1)} %get-tuple-element.59.b_ref, f32[16,64,256]{2,1,0:T(8,128)S(1)} %get-tuple-element.108.refs_0_, f32[16,64,256]{2,1,0:T(8,128)S(1)} %get-tuple-element.109.refs_1_, ...), custom_call_target="tpu_custom_call" | custom-call | tf_op jit(solution)/shard_map/pallas_call | solution.py:539
  (1 shorter events, 0.0 us)
Async XLA Ops:
  2.4 13.2 %collective-permute-start.2 = (f32[15,64,256]{2,1,0:T(8,128)S(1)}, f32[15,64,256]{2,1,0:T(8,128)S(1)}, u32[]{:S(2)}, u32[]{:S(2)}) collective-permute-start(f32[15,64,256]{2,1,0:T(8,128)S(1)} %get-tuple-element.78), channel_id=1, source_target_pairs={{0,4},{1,5},{2,6},{3,7},{4,0},{5,1},{6,2},{7,3},{8,12},{9,13},{10,... | collective-permute-start | bytes 2949128 | tf_op jit(solution)/shard_map/ppermute | solution.py:172
  2.9 15.9 %collective-permute-start.4 = (f32[15,64,256]{2,1,0:T(8,128)S(1)}, f32[15,64,256]{2,1,0:T(8,128)S(1)}, u32[]{:S(2)}, u32[]{:S(2)}) collective-permute-start(f32[15,64,256]{2,1,0:T(8,128)S(1)} %get-tuple-element.93), channel_id=1, source_target_pairs={{4,8},{5,9},{6,10},{7,11},{8,4},{9,5},{10,6},{11,7},{20,24},{21,25... | collective-permute-start | bytes 2949128 | tf_op jit(solution)/shard_map/ppermute | solution.py:172
  3.6 7.5 %collective-permute-start = (f32[2,16,8,256]{3,2,1,0:T(8,128)S(1)}, f32[2,16,8,256]{3,2,1,0:T(8,128)S(1)}, u32[]{:S(2)}, u32[]{:S(2)}) collective-permute-start(f32[2,16,8,256]{3,2,1,0:T(8,128)S(1)} %get-tuple-element.63), channel_id=1, source_target_pairs={{0,1},{1,0},{2,3},{3,2},{4,5},{5,4},{6,7},{7,6},{8,9},{9,8},{10,11... | collective-permute-start | bytes 786440 | tf_op jit(solution)/shard_map/ppermute | solution.py:172
  6.3 4.8 %collective-permute-start.1 = (f32[2,16,8,256]{3,2,1,0:T(8,128)S(1)}, f32[2,16,8,256]{3,2,1,0:T(8,128)S(1)}, u32[]{:S(2)}, u32[]{:S(2)}) collective-permute-start(f32[2,16,8,256]{3,2,1,0:T(8,128)S(1)} %get-tuple-element.64), channel_id=1, source_target_pairs={{1,2},{2,1},{5,6},{6,5},{9,10},{10,9},{13,14},{14,13},{17,18},{18,... | collective-permute-start | bytes 786440 | tf_op jit(solution)/shard_map/ppermute | solution.py:172
  11.2 4.4 %collective-permute-start.3 = (f32[2,4,2,8,256]{4,3,2,1,0:T(8,128)S(1)}, f32[2,4,2,8,256]{4,3,2,1,0:T(8,128)S(1)}, u32[]{:S(2)}, u32[]{:S(2)}) collective-permute-start(f32[2,4,2,8,256]{4,3,2,1,0:T(8,128)S(1)} %get-tuple-element.79), channel_id=1, source_target_pairs={{0,4},{1,5},{2,6},{3,7},{4,0},{5,1},{6,2},{7,3},{8,12},{9,13},{10,... | collective-permute-start | bytes 393224 | tf_op jit(solution)/shard_map/ppermute | solution.py:172
  13.4 5.4 %collective-permute-start.5 = (f32[2,4,2,8,256]{4,3,2,1,0:T(8,128)S(1)}, f32[2,4,2,8,256]{4,3,2,1,0:T(8,128)S(1)}, u32[]{:S(2)}, u32[]{:S(2)}) collective-permute-start(f32[2,4,2,8,256]{4,3,2,1,0:T(8,128)S(1)} %get-tuple-element.94), channel_id=1, source_target_pairs={{4,8},{5,9},{6,10},{7,11},{8,4},{9,5},{10,6},{11,7},{20,24},{21,25... | collective-permute-start | bytes 393224 | tf_op jit(solution)/shard_map/ppermute | solution.py:172

commit v8 on v6

--- a/solution.py
+++ b/solution.py
@@ -101,10 +101,11 @@
 
     copies[0].wait()
     copies[1].wait()
-    lax.fori_loop(0, rows, code, 0, unroll=2)
+    lax.fori_loop(0, rows, code, 0, unroll=8)
     copies[2].wait()
-    lax.fori_loop(0, rows, edges, 0, unroll=4)
-    lax.fori_loop(1, h, layers, 0)
+    lax.fori_loop(0, rows, edges, 0, unroll=16)
+    for d in range(1, h):
+        layers(d, 0)
     for a in range(2):
         at = edge_layer(wide[a], rows, h)
         w_out[a][h - 1] = c_ref[at].astype(jnp.float32) * ROOT * b_ref[at]
@@ -286,7 +287,7 @@
         )
 
     zero = jnp.zeros((8, LANES), jnp.float32)
-    m_ref[0] = lax.fori_loop(0, rows, fill, zero)
+    m_ref[0] = lax.fori_loop(0, rows, fill, zero, unroll=4)
     for step in range(1, STEPS + 1):
         quads, rest = divmod(max(rows - 2 * step, 0), 4)
 
@@ -322,7 +323,8 @@
             place_u(u_even, at, y + h, coef[at, pl.ds(y + h, 8), :] * b_ref[i, pl.ds(y, 8), :])
         return 0
 
-    lax.fori_loop(0, rows, fill, 0)
+    for i in range(rows):
+        fill(i, 0)
     m_out[0] = m_in[0]
     for step in range(1, STEPS + 1):
         source = u_even if step % 2 else u_odd
@@ -362,7 +364,8 @@
         outside(u_even, diag, coef, halo_layer(d), h, w_in[d - 1], w_in[h + d - 1])
         return 0
 
-    lax.fori_loop(1, h, fill, 0)
+    for d in range(1, h):
+        fill(d, 0)
     place_u(u_even, halo_layer(h), h, w_in[h - 1])
     for side in range(2):
         for p, (d, other) in enumerate(PAIRS):
@@ -525,7 +528,7 @@
     copies = []
     for chunk in range(CHUNKS):
         part = pl.ds(chunk * rows // CHUNKS, rows // CHUNKS)
-        lax.fori_loop(part.start, part.start + part.size, plane, 0)
+        lax.fori_loop(part.start, part.start + part.size, plane, 0, unroll=2)
         for k, source in enumerate((x_ref, r_ref)):
             copies.append(
                 pltpu.make_async_copy(source.at[part], outs[k].at[part], done.at[k, chunk])

time: 41.9 us -> 42.5 us (1.014)
  Pallas kernels: 16 us -> 16.6 us
    pallas_call x3, Pallas kernels: 8.47 us -> 9.18 us  [onward(): pl.pallas_call(kernel, out_shape=shapes, in_specs=[VMEM] * (others + len(...]
  transfers between devices with their start and end apart: 6 -> 6, of which waited for: 1 -> 1; matrix products, arithmetic and copies ran while one was open for 0% -> 0% of each run, Pallas kernels for 19% -> 20%
where the time goes in v8:
time: 42.5 us; the launch traced here: 42.3 us
  Pallas kernels  16.6 us (39%)
  blocking collectives  16.6 us (39%)
  starting transfers between devices  7.46 us (18%)
  waiting for transfers between devices  0.89 us (2%)
  between operations  0.72 us (2%)
    all_to_all x1, blocking collectives, on_device(): lax.all_to_all(moments, AXES, 0, 0, tiled=True)  16.6 us
    pallas_call x3, Pallas kernels, onward(): pl.pallas_call(kernel, out_shape=shapes, in_specs=[VMEM] * (others + len(...  9.18 us
    ppermute x6, starting transfers between devices, swapped(): return lax.ppermute(array, AXES, pairs)  7.46 us
    pallas_call x1, Pallas kernels, inner(): pl.pallas_call(inner_kernel, cost_estimate=pl.CostEstimate(flops=120 * b....  3.25 us
    pallas_call x1, Pallas kernels, combine(): pl.pallas_call(combine_kernel, out_shape=[jax.ShapeDtypeStruct(b.shape, j...  2.38 us
    pallas_call x1, Pallas kernels, messages(): pl.pallas_call(send_kernel, out_shape=[jax.ShapeDtypeStruct(s, jnp.float3...  1.74 us
    ppermute x6, waiting for transfers between devices, swapped(): return lax.ppermute(array, AXES, pairs)  0.89 us
  transfers between devices with their start and end apart: 6, of which 1 were waited for; matrix products, arithmetic and copies ran while one was open for 0% of the time, Pallas kernels for 20%

profile of v8, /device:TPU:0, one launch (start us, length us, event | category | flops | bytes accessed | tf_op | source)
XLA Modules:
  0.0 42.3 jit_solution(9852579751884908341)
XLA Ops:
  0.6 1.7 %shard_map.50 = (f32[15,64,256]{2,1,0:T(8,128)S(1)}, f32[15,64,256]{2,1,0:T(8,128)S(1)}, f32[2,16,8,256]{3,2,1,0:T(8,128)S(1)}, f32[2,16,8,256]{3,2,1,0:T(8,128)...) custom-call(f32[16,64,256]{2,1,0:T(8,128)} %refs_0_.1, ...), custom_call_target="tpu_custom_call" | custom-call | tf_op jit(solution)/shard_map/pallas_call | solution.py:118
  2.4 0.5 %collective-permute-start.2 = (f32[15,64,256]{2,1,0:T(8,128)S(1)}, f32[15,64,256]{2,1,0:T(8,128)S(1)}, u32[]{:S(2)}, u32[]{:S(2)}) collective-permute-start(f32[15,64,256]{2,1,0:T(8,128)S(1)} %get-tuple-element.78), channel_id=1, source_target_pairs={{0,4},{1,5},{2,6},{3,7},{4,0},{5,1},{6,2},{7,3},{8,12},{9,13},{10,... | collective-permute-start | bytes 2949128 | tf_op jit(solution)/shard_map/ppermute | solution.py:173
  2.9 0.7 %collective-permute-start.4 = (f32[15,64,256]{2,1,0:T(8,128)S(1)}, f32[15,64,256]{2,1,0:T(8,128)S(1)}, u32[]{:S(2)}, u32[]{:S(2)}) collective-permute-start(f32[15,64,256]{2,1,0:T(8,128)S(1)} %get-tuple-element.93), channel_id=1, source_target_pairs={{4,8},{5,9},{6,10},{7,11},{8,4},{9,5},{10,6},{11,7},{20,24},{21,25... | collective-permute-start | bytes 2949128 | tf_op jit(solution)/shard_map/ppermute | solution.py:173
  3.6 2.7 %collective-permute-start = (f32[2,16,8,256]{3,2,1,0:T(8,128)S(1)}, f32[2,16,8,256]{3,2,1,0:T(8,128)S(1)}, u32[]{:S(2)}, u32[]{:S(2)}) collective-permute-start(f32[2,16,8,256]{3,2,1,0:T(8,128)S(1)} %get-tuple-element.63), channel_id=1, source_target_pairs={{0,1},{1,0},{2,3},{3,2},{4,5},{5,4},{6,7},{7,6},{8,9},{9,8},{10,11... | collective-permute-start | bytes 786440 | tf_op jit(solution)/shard_map/ppermute | solution.py:173
  6.3 0.7 %collective-permute-start.1 = (f32[2,16,8,256]{3,2,1,0:T(8,128)S(1)}, f32[2,16,8,256]{3,2,1,0:T(8,128)S(1)}, u32[]{:S(2)}, u32[]{:S(2)}) collective-permute-start(f32[2,16,8,256]{3,2,1,0:T(8,128)S(1)} %get-tuple-element.64), channel_id=1, source_target_pairs={{1,2},{2,1},{5,6},{6,5},{9,10},{10,9},{13,14},{14,13},{17,18},{18,... | collective-permute-start | bytes 786440 | tf_op jit(solution)/shard_map/ppermute | solution.py:173
  7.0 3.2 %shard_map.51 = (f32[16,64,256]{2,1,0:T(8,128)S(1)}, f32[16,64,256]{2,1,0:T(8,128)S(1)}, f32[16,64,256]{2,1,0:T(8,128)S(1)}, f32[16,64,256]{2,1,0:T(8,128)S(1)},...) custom-call(f32[16,64,256]{2,1,0:T(8,128)S(1)} %get-tuple-element.59, ...), custom_call_target="tpu_custom_call" | custom-call | flops 31457280 | bytes 6291456 | tf_op jit(solution)/shard_map/pallas_call | solution.py:437
  10.2 0.9 %collective-permute-done.refs_0_ = f32[2,16,8,256]{3,2,1,0:T(8,128)S(1)} collective-permute-done((f32[2,16,8,256]{3,2,1,0:T(8,128)S(1)}, f32[2,16,8,256]{3,2,1,0:T(8,128)S(1)}, u32[]{:S(2)}, u32[]{:S(2)}) %collective-permute-start) | collective-permute-done | bytes 262176 | tf_op jit(solution)/shard_map/ppermute | solution.py:173
  11.1 0.0 collective-permute-done.1.refs_1_
  11.1 2.2 %collective-permute-start.3 = (f32[2,4,2,8,256]{4,3,2,1,0:T(8,128)S(1)}, f32[2,4,2,8,256]{4,3,2,1,0:T(8,128)S(1)}, u32[]{:S(2)}, u32[]{:S(2)}) collective-permute-start(f32[2,4,2,8,256]{4,3,2,1,0:T(8,128)S(1)} %get-tuple-element.79), channel_id=1, source_target_pairs={{0,4},{1,5},{2,6},{3,7},{4,0},{5,1},{6,2},{7,3},{8,12},{9,13},{10,... | collective-permute-start | bytes 393224 | tf_op jit(solution)/shard_map/ppermute | solution.py:173
  13.4 0.7 %collective-permute-start.5 = (f32[2,4,2,8,256]{4,3,2,1,0:T(8,128)S(1)}, f32[2,4,2,8,256]{4,3,2,1,0:T(8,128)S(1)}, u32[]{:S(2)}, u32[]{:S(2)}) collective-permute-start(f32[2,4,2,8,256]{4,3,2,1,0:T(8,128)S(1)} %get-tuple-element.94), channel_id=1, source_target_pairs={{4,8},{5,9},{6,10},{7,11},{8,4},{9,5},{10,6},{11,7},{20,24},{21,25... | collective-permute-start | bytes 393224 | tf_op jit(solution)/shard_map/ppermute | solution.py:173
  14.0 1.3 %shard_map.52 = (f32[16,64,256]{2,1,0:T(8,128)S(1)}, f32[16,64,256]{2,1,0:T(8,128)S(1)}, f32[16,64,256]{2,1,0:T(8,128)S(1)}, f32[16,64,256]{2,1,0:T(8,128)S(1)},...) custom-call(f32[16,64,256]{2,1,0:T(8,128)S(1)} %get-tuple-element.59, ...), custom_call_target="tpu_custom_call", output_to_operand_aliasing={{0}: (4, {}), {1}: (5, {}), {2}: (6, {}), {3}: (7, {}), {4}... | custom-call | tf_op jit(solution)/shard_map/pallas_call | solution.py:453
  15.4 0.0 collective-permute-done.3.refs_1_
  15.4 0.0 collective-permute-done.2.refs_0_
  15.4 3.7 %shard_map.54 = (f32[16,64,256]{2,1,0:T(8,128)S(1)}, f32[16,64,256]{2,1,0:T(8,128)S(1)}, f32[16,64,256]{2,1,0:T(8,128)S(1)}, f32[16,64,256]{2,1,0:T(8,128)S(1)},...) custom-call(f32[16,64,256]{2,1,0:T(8,128)S(1)} %get-tuple-element.59, ...), custom_call_target="tpu_custom_call", output_to_operand_aliasing={{0}: (4, {}), {1}: (5, {}), {2}: (6, {}), {3}: (7, {}), {4}... | custom-call | tf_op jit(solution)/shard_map/pallas_call | solution.py:453
  19.1 0.0 collective-permute-done.5.refs_1_
  19.2 0.0 collective-permute-done.4.refs_0_
  19.2 4.1 %shard_map.55 = (f32[16,64,256]{2,1,0:T(8,128)S(1)}, f32[16,64,256]{2,1,0:T(8,128)S(1)}, f32[16,64,256]{2,1,0:T(8,128)S(1)}, f32[16,64,256]{2,1,0:T(8,128)S(1)},...) custom-call(f32[16,64,256]{2,1,0:T(8,128)S(1)} %get-tuple-element.59, ...), custom_call_target="tpu_custom_call", output_to_operand_aliasing={{0}: (4, {}), {1}: (5, {}), {2}: (6, {}), {3}: (7, {}), {4}... | custom-call | tf_op jit(solution)/shard_map/pallas_call | solution.py:453
  23.3 16.6 %all_to_all.5.m_ref = f32[16,8,128]{2,1,0:T(8,128)S(1)} all-to-all(f32[16,8,128]{2,1,0:T(8,128)S(1)} %get-tuple-element.107), channel_id=1, replica_groups=mesh['group'=2,'wide'=4,'narrow'=4] {'wide','narrow'}, dimensions={0} | all-to-all | bytes 131072 | tf_op jit(solution)/shard_map/all_to_all | solution.py:566
  39.9 2.4 %shard_map.56 = (f32[16,64,256]{2,1,0:T(8,128)}, f32[16,64,256]{2,1,0:T(8,128)}) custom-call(f32[16,8,128]{2,1,0:T(8,128)S(1)} %all_to_all.5.m_ref, f32[16,64,256]{2,1,0:T(8,128)S(1)} %get-tuple-element.59.b_ref, f32[16,64,256]{2,1,0:T(8,128)S(1)} %get-tuple-element.108.refs_0_, f32[16,64,256]{2,1,0:T(8,128)S(1)} %get-tuple-element.109.refs_1_, ...), custom_call_target="tpu_custom_call" | custom-call | tf_op jit(solution)/shard_map/pallas_call | solution.py:542
  (1 shorter events, 0.0 us)
Async XLA Ops:
  2.4 13.0 %collective-permute-start.2 = (f32[15,64,256]{2,1,0:T(8,128)S(1)}, f32[15,64,256]{2,1,0:T(8,128)S(1)}, u32[]{:S(2)}, u32[]{:S(2)}) collective-permute-start(f32[15,64,256]{2,1,0:T(8,128)S(1)} %get-tuple-element.78), channel_id=1, source_target_pairs={{0,4},{1,5},{2,6},{3,7},{4,0},{5,1},{6,2},{7,3},{8,12},{9,13},{10,... | collective-permute-start | bytes 2949128 | tf_op jit(solution)/shard_map/ppermute | solution.py:173
  2.9 16.3 %collective-permute-start.4 = (f32[15,64,256]{2,1,0:T(8,128)S(1)}, f32[15,64,256]{2,1,0:T(8,128)S(1)}, u32[]{:S(2)}, u32[]{:S(2)}) collective-permute-start(f32[15,64,256]{2,1,0:T(8,128)S(1)} %get-tuple-element.93), channel_id=1, source_target_pairs={{4,8},{5,9},{6,10},{7,11},{8,4},{9,5},{10,6},{11,7},{20,24},{21,25... | collective-permute-start | bytes 2949128 | tf_op jit(solution)/shard_map/ppermute | solution.py:173
  3.6 7.5 %collective-permute-start = (f32[2,16,8,256]{3,2,1,0:T(8,128)S(1)}, f32[2,16,8,256]{3,2,1,0:T(8,128)S(1)}, u32[]{:S(2)}, u32[]{:S(2)}) collective-permute-start(f32[2,16,8,256]{3,2,1,0:T(8,128)S(1)} %get-tuple-element.63), channel_id=1, source_target_pairs={{0,1},{1,0},{2,3},{3,2},{4,5},{5,4},{6,7},{7,6},{8,9},{9,8},{10,11... | collective-permute-start | bytes 786440 | tf_op jit(solution)/shard_map/ppermute | solution.py:173
  6.3 4.8 %collective-permute-start.1 = (f32[2,16,8,256]{3,2,1,0:T(8,128)S(1)}, f32[2,16,8,256]{3,2,1,0:T(8,128)S(1)}, u32[]{:S(2)}, u32[]{:S(2)}) collective-permute-start(f32[2,16,8,256]{3,2,1,0:T(8,128)S(1)} %get-tuple-element.64), channel_id=1, source_target_pairs={{1,2},{2,1},{5,6},{6,5},{9,10},{10,9},{13,14},{14,13},{17,18},{18,... | collective-permute-start | bytes 786440 | tf_op jit(solution)/shard_map/ppermute | solution.py:173
  11.1 4.3 %collective-permute-start.3 = (f32[2,4,2,8,256]{4,3,2,1,0:T(8,128)S(1)}, f32[2,4,2,8,256]{4,3,2,1,0:T(8,128)S(1)}, u32[]{:S(2)}, u32[]{:S(2)}) collective-permute-start(f32[2,4,2,8,256]{4,3,2,1,0:T(8,128)S(1)} %get-tuple-element.79), channel_id=1, source_target_pairs={{0,4},{1,5},{2,6},{3,7},{4,0},{5,1},{6,2},{7,3},{8,12},{9,13},{10,... | collective-permute-start | bytes 393224 | tf_op jit(solution)/shard_map/ppermute | solution.py:173
  13.4 5.8 %collective-permute-start.5 = (f32[2,4,2,8,256]{4,3,2,1,0:T(8,128)S(1)}, f32[2,4,2,8,256]{4,3,2,1,0:T(8,128)S(1)}, u32[]{:S(2)}, u32[]{:S(2)}) collective-permute-start(f32[2,4,2,8,256]{4,3,2,1,0:T(8,128)S(1)} %get-tuple-element.94), channel_id=1, source_target_pairs={{4,8},{5,9},{6,10},{7,11},{8,4},{9,5},{10,6},{11,7},{20,24},{21,25... | collective-permute-start | bytes 393224 | tf_op jit(solution)/shard_map/ppermute | solution.py:173

commit v9 on v8

--- a/solution.py
+++ b/solution.py
@@ -18,6 +18,7 @@
 LANES = 128
 QUARTER = LANES // 4
 CHUNKS = 4
+NEAR = 2
 AXES = ("wide", "narrow")
 VMEM = pl.BlockSpec(memory_space=pltpu.VMEM)
 HBM = pl.BlockSpec(memory_space=pltpu.HBM)
@@ -60,11 +61,15 @@
 
 
 def sides():
-    out = []
-    for axis in AXES:
-        even = lax.rem(lax.axis_index(axis), 2) == 0
-        out.append((even, jnp.logical_not(even)))
-    return out
+    wide, narrow = (lax.rem(lax.axis_index(axis), 2) == 0 for axis in AXES)
+    return (wide, jnp.logical_not(wide)), (jnp.logical_not(narrow), narrow)
+
+
+def wide_plane(d, near):
+    return 4 * (d - 1) if near else 3 * (d - 1) + NEAR
+
+
+WIDE_PLANES = wide_plane(STEPS, False) + 1
 
 
 def edge_layer(up, count, d):
@@ -83,7 +88,10 @@
     left = [pl.multiple_of(jnp.where(up, columns - h, 0), 8) for up in narrow]
 
     def code(i, _):
-        pack[i] = r_ref[i].astype(jnp.float32) + c_ref[i].astype(jnp.float32) * (1.0 / 256.0)
+        for y in (0, columns - 2 * h):
+            at = (i, pl.ds(y, 2 * h))
+            reaction, conduct = r_ref[at].astype(jnp.float32), c_ref[at].astype(jnp.float32)
+            pack[at] = reaction + conduct * (1.0 / 256.0)
         return 0
 
     def edges(i, _):
@@ -92,32 +100,34 @@
                 n_out[side][k, i] = source[i, pl.ds(left[side], h), :]
         return 0
 
-    def layers(d, _):
-        for a in range(2):
-            at = edge_layer(wide[a], rows, d)
-            w_out[a][d - 1] = b_ref[at]
-            w_out[a][h + d - 1] = pack[at]
-        return 0
-
     copies[0].wait()
     copies[1].wait()
     lax.fori_loop(0, rows, code, 0, unroll=8)
     copies[2].wait()
     lax.fori_loop(0, rows, edges, 0, unroll=16)
-    for d in range(1, h):
-        layers(d, 0)
     for a in range(2):
+        for d in range(1, h):
+            at, k = edge_layer(wide[a], rows, d), wide_plane(d, d <= NEAR)
+            high = b_ref[at].astype(jnp.bfloat16)
+            w_out[a][k] = high
+            if d <= NEAR:
+                k += 1
+                w_out[a][k] = (b_ref[at] - high.astype(jnp.float32)).astype(jnp.bfloat16)
+            w_out[a][k + 1] = c_ref[at]
+            w_out[a][k + 2] = r_ref[at]
         at = edge_layer(wide[a], rows, h)
-        w_out[a][h - 1] = c_ref[at].astype(jnp.float32) * ROOT * b_ref[at]
+        root = c_ref[at].astype(jnp.float32) * ROOT
+        w_out[a][WIDE_PLANES - 1] = (root * b_ref[at]).astype(jnp.bfloat16)
 
 
 def messages(b, c, r):
     rows, columns, depth = b.shape
     h = STEPS
-    shapes = [(2 * h - 1, columns, depth)] * 2 + [(2, rows, h, depth)] * 2
+    outs = [jax.ShapeDtypeStruct((WIDE_PLANES, columns, depth), jnp.bfloat16)] * 2
+    outs += [jax.ShapeDtypeStruct((2, rows, h, depth), jnp.float32)] * 2
     return pl.pallas_call(
         send_kernel,
-        out_shape=[jax.ShapeDtypeStruct(s, jnp.float32) for s in shapes]
+        out_shape=outs
         + [pltpu.VMEM(a.shape, a.dtype) for a in (b, c, r)],
         in_specs=[HBM] * 3,
         out_specs=[VMEM] * 7,
@@ -192,14 +202,18 @@
     return ((reaction - CENTER) + 6.0 * (conduct * conduct)) * (1.0 / SCALE)
 
 
-def outside(u_even, diag, coef, i, y, value, packed):
+def settle(u_even, diag, coef, i, y, value, conduct, reaction):
     count = value.shape[0]
-    reaction = jnp.floor(packed * 128.0) * (1.0 / 128.0)
-    conduct = (packed - reaction) * 256.0
     root = conduct * ROOT
     place_u(u_even, i, y, root * value)
     coef[i, pl.ds(y, count), :] = root * root
     diag[i, pl.ds(y, count), :] = diagonal_of(conduct, reaction)
+
+
+def outside(u_even, diag, coef, i, y, value, packed):
+    reaction = jnp.floor(packed * 128.0) * (1.0 / 128.0)
+    conduct = (packed - reaction) * 256.0
+    settle(u_even, diag, coef, i, y, value, conduct, reaction)
 
 
 def advance(step, runs, refs, carry, chosen=None, silent=()):
@@ -360,13 +374,21 @@
     def halo_layer(d):
         return jnp.where(up, rows + h - 1 + d, h - d)
 
-    def fill(d, _):
-        outside(u_even, diag, coef, halo_layer(d), h, w_in[d - 1], w_in[h + d - 1])
+    def plane(k):
+        return w_in[k].astype(jnp.float32)
+
+    def fill(near, d, _):
+        k = wide_plane(d, near)
+        value = plane(k)
+        if near:
+            k += 1
+            value = value + plane(k)
+        settle(u_even, diag, coef, halo_layer(d), h, value, plane(k + 1), plane(k + 2))
         return 0
 
-    for d in range(1, h):
-        fill(d, 0)
-    place_u(u_even, halo_layer(h), h, w_in[h - 1])
+    lax.fori_loop(1, NEAR + 1, functools.partial(fill, True), 0)
+    lax.fori_loop(NEAR + 1, h, functools.partial(fill, False), 0)
+    place_u(u_even, halo_layer(h), h, plane(WIDE_PLANES - 1))
     for side in range(2):
         for p, (d, other) in enumerate(PAIRS):
             near = [c_in[k, p, side] for k in range(2)]
@@ -554,7 +576,7 @@
     peers = lax.axis_size("wide") * lax.axis_size("narrow")
     *sent, b, c, r = messages(right_side, conduct_half, reaction_half)
     far, near = swapped(sent[1], 1, None), swapped(sent[0], 0, None)
-    narrow_halos = [swapped(sent[2 + k], None, k) for k in range(2)]
+    narrow_halos = [swapped(sent[2 + k], None, 1 - k) for k in range(2)]
     state, moments = inner(b, c, r)
     diagonal = corners(narrow_halos, moments)
     diagonal = [swapped(block, k, None) for k, block in enumerate(diagonal)]

time: 42.5 us -> 40.6 us (0.955)
  blocking collectives: 16.6 us -> 12.2 us
  starting transfers between devices: 7.46 us -> 9.84 us
  waiting for transfers between devices: 0.89 us -> 1.99 us
  Pallas kernels: 16.6 us -> 15.6 us
    all_to_all x1, blocking collectives: 16.6 us -> 12.2 us  [on_device(): lax.all_to_all(moments, AXES, 0, 0, tiled=True)]
    ppermute x6, starting transfers between devices: 7.46 us -> 9.84 us  [swapped(): return lax.ppermute(array, AXES, pairs)]
    ppermute x6, waiting for transfers between devices: 0.89 us -> 1.99 us  [swapped(): return lax.ppermute(array, AXES, pairs)]
    pallas_call x3, Pallas kernels: 9.18 us -> 8.26 us  [onward(): pl.pallas_call(kernel, out_shape=shapes, in_specs=[VMEM] * (others + len(...]
  transfers between devices with their start and end apart: 6 -> 6, of which waited for: 1 -> 1; matrix products, arithmetic and copies ran while one was open for 0% -> 0% of each run, Pallas kernels for 20% -> 19%
where the time goes in v9:
time: 40.6 us; the launch traced here: 40.4 us
  Pallas kernels  15.6 us (38%)
  blocking collectives  12.2 us (30%)
  starting transfers between devices  9.84 us (24%)
  waiting for transfers between devices  1.99 us (5%)
  between operations  0.73 us (2%)
    all_to_all x1, blocking collectives, on_device(): lax.all_to_all(moments, AXES, 0, 0, tiled=True)  12.2 us
    ppermute x6, starting transfers between devices, swapped(): return lax.ppermute(array, AXES, pairs)  9.84 us
    pallas_call x3, Pallas kernels, onward(): pl.pallas_call(kernel, out_shape=shapes, in_specs=[VMEM] * (others + len(...  8.26 us
    pallas_call x1, Pallas kernels, inner(): pl.pallas_call(inner_kernel, cost_estimate=pl.CostEstimate(flops=120 * b....  3.24 us
    pallas_call x1, Pallas kernels, combine(): pl.pallas_call(combine_kernel, out_shape=[jax.ShapeDtypeStruct(b.shape, j...  2.38 us
    ppermute x6, waiting for transfers between devices, swapped(): return lax.ppermute(array, AXES, pairs)  1.99 us
    pallas_call x1, Pallas kernels, messages(): pl.pallas_call(send_kernel, out_shape=outs + [pltpu.VMEM(a.shape, a.dtype...  1.73 us
  transfers between devices with their start and end apart: 6, of which 1 were waited for; matrix products, arithmetic and copies ran while one was open for 0% of the time, Pallas kernels for 19%

profile of v9, /device:TPU:0, one launch (start us, length us, event | category | flops | bytes accessed | tf_op | source)
XLA Modules:
  0.0 40.4 jit_solution(17186789782128746247)
XLA Ops:
  0.6 1.7 %shard_map.50 = (bf16[24,64,256]{2,1,0:T(8,128)(2,1)S(1)}, bf16[24,64,256]{2,1,0:T(8,128)(2,1)S(1)}, f32[2,16,8,256]{3,2,1,0:T(8,128)S(1)}, f32[2,16,8,256]{3,2,...) custom-call(f32[16,64,256]{2,1,0:T(8,128)} %refs_0_.1, ...), custom_call_target="tpu_custom_call" | custom-call | tf_op jit(solution)/shard_map/pallas_call | solution.py:128
  2.4 0.5 %collective-permute-start.2 = (bf16[24,64,256]{2,1,0:T(8,128)(2,1)S(1)}, bf16[24,64,256]{2,1,0:T(8,128)(2,1)S(1)}, u32[]{:S(2)}, u32[]{:S(2)}) collective-permute-start(bf16[24,64,256]{2,1,0:T(8,128)(2,1)S(1)} %get-tuple-element.78), channel_id=1, source_target_pairs={{0,4},{1,5},{2,6},{3,7},{4,0},{5,1},{6,2},{7,3},{8,12},{9,13},{10,... | collective-permute-start | bytes 2359304 | tf_op jit(solution)/shard_map/ppermute | solution.py:183
  2.9 0.7 %collective-permute-start.4 = (bf16[24,64,256]{2,1,0:T(8,128)(2,1)S(1)}, bf16[24,64,256]{2,1,0:T(8,128)(2,1)S(1)}, u32[]{:S(2)}, u32[]{:S(2)}) collective-permute-start(bf16[24,64,256]{2,1,0:T(8,128)(2,1)S(1)} %get-tuple-element.93), channel_id=1, source_target_pairs={{4,8},{5,9},{6,10},{7,11},{8,4},{9,5},{10,6},{11,7},{20,24},{21,25... | collective-permute-start | bytes 2359304 | tf_op jit(solution)/shard_map/ppermute | solution.py:183
  3.6 0.7 %collective-permute-start = (f32[2,16,8,256]{3,2,1,0:T(8,128)S(1)}, f32[2,16,8,256]{3,2,1,0:T(8,128)S(1)}, u32[]{:S(2)}, u32[]{:S(2)}) collective-permute-start(f32[2,16,8,256]{3,2,1,0:T(8,128)S(1)} %get-tuple-element.63), channel_id=1, source_target_pairs={{1,2},{2,1},{5,6},{6,5},{9,10},{10,9},{13,14},{14,13},{17,18},{18,... | collective-permute-start | bytes 786440 | tf_op jit(solution)/shard_map/ppermute | solution.py:183
  4.3 5.5 %collective-permute-start.1 = (f32[2,16,8,256]{3,2,1,0:T(8,128)S(1)}, f32[2,16,8,256]{3,2,1,0:T(8,128)S(1)}, u32[]{:S(2)}, u32[]{:S(2)}) collective-permute-start(f32[2,16,8,256]{3,2,1,0:T(8,128)S(1)} %get-tuple-element.64), channel_id=1, source_target_pairs={{0,1},{1,0},{2,3},{3,2},{4,5},{5,4},{6,7},{7,6},{8,9},{9,8},{10,11... | collective-permute-start | bytes 786440 | tf_op jit(solution)/shard_map/ppermute | solution.py:183
  9.8 3.2 %shard_map.51 = (f32[16,64,256]{2,1,0:T(8,128)S(1)}, f32[16,64,256]{2,1,0:T(8,128)S(1)}, f32[16,64,256]{2,1,0:T(8,128)S(1)}, f32[16,64,256]{2,1,0:T(8,128)S(1)},...) custom-call(f32[16,64,256]{2,1,0:T(8,128)S(1)} %get-tuple-element.59, ...), custom_call_target="tpu_custom_call" | custom-call | flops 31457280 | bytes 6291456 | tf_op jit(solution)/shard_map/pallas_call | solution.py:459
  13.0 0.0 collective-permute-done.refs_0_
  13.0 2.0 %collective-permute-done.1.refs_1_ = f32[2,16,8,256]{3,2,1,0:T(8,128)S(1)} collective-permute-done((f32[2,16,8,256]{3,2,1,0:T(8,128)S(1)}, f32[2,16,8,256]{3,2,1,0:T(8,128)S(1)}, u32[]{:S(2)}, u32[]{:S(2)}) %collective-permute-start.1) | collective-permute-done | bytes 262176 | tf_op jit(solution)/shard_map/ppermute | solution.py:183
  15.0 1.8 %collective-permute-start.3 = (f32[2,4,2,8,256]{4,3,2,1,0:T(8,128)S(1)}, f32[2,4,2,8,256]{4,3,2,1,0:T(8,128)S(1)}, u32[]{:S(2)}, u32[]{:S(2)}) collective-permute-start(f32[2,4,2,8,256]{4,3,2,1,0:T(8,128)S(1)} %get-tuple-element.79), channel_id=1, source_target_pairs={{0,4},{1,5},{2,6},{3,7},{4,0},{5,1},{6,2},{7,3},{8,12},{9,13},{10,... | collective-permute-start | bytes 393224 | tf_op jit(solution)/shard_map/ppermute | solution.py:183
  16.8 0.7 %collective-permute-start.5 = (f32[2,4,2,8,256]{4,3,2,1,0:T(8,128)S(1)}, f32[2,4,2,8,256]{4,3,2,1,0:T(8,128)S(1)}, u32[]{:S(2)}, u32[]{:S(2)}) collective-permute-start(f32[2,4,2,8,256]{4,3,2,1,0:T(8,128)S(1)} %get-tuple-element.94), channel_id=1, source_target_pairs={{4,8},{5,9},{6,10},{7,11},{8,4},{9,5},{10,6},{11,7},{20,24},{21,25... | collective-permute-start | bytes 393224 | tf_op jit(solution)/shard_map/ppermute | solution.py:183
  17.5 1.3 %shard_map.52 = (f32[16,64,256]{2,1,0:T(8,128)S(1)}, f32[16,64,256]{2,1,0:T(8,128)S(1)}, f32[16,64,256]{2,1,0:T(8,128)S(1)}, f32[16,64,256]{2,1,0:T(8,128)S(1)},...) custom-call(f32[16,64,256]{2,1,0:T(8,128)S(1)} %get-tuple-element.59, ...), custom_call_target="tpu_custom_call", output_to_operand_aliasing={{0}: (4, {}), {1}: (5, {}), {2}: (6, {}), {3}: (7, {}), {4}... | custom-call | tf_op jit(solution)/shard_map/pallas_call | solution.py:475
  18.9 0.0 collective-permute-done.3.refs_1_
  18.9 0.0 collective-permute-done.2.refs_0_
  18.9 3.2 %shard_map.54 = (f32[16,64,256]{2,1,0:T(8,128)S(1)}, f32[16,64,256]{2,1,0:T(8,128)S(1)}, f32[16,64,256]{2,1,0:T(8,128)S(1)}, f32[16,64,256]{2,1,0:T(8,128)S(1)},...) custom-call(f32[16,64,256]{2,1,0:T(8,128)S(1)} %get-tuple-element.59, ...), custom_call_target="tpu_custom_call", output_to_operand_aliasing={{0}: (4, {}), {1}: (5, {}), {2}: (6, {}), {3}: (7, {}), {4}... | custom-call | tf_op jit(solution)/shard_map/pallas_call | solution.py:475
  22.1 0.0 collective-permute-done.5.refs_1_
  22.1 0.0 collective-permute-done.4.refs_0_
  22.1 3.7 %shard_map.55 = (f32[16,64,256]{2,1,0:T(8,128)S(1)}, f32[16,64,256]{2,1,0:T(8,128)S(1)}, f32[16,64,256]{2,1,0:T(8,128)S(1)}, f32[16,64,256]{2,1,0:T(8,128)S(1)},...) custom-call(f32[16,64,256]{2,1,0:T(8,128)S(1)} %get-tuple-element.59, ...), custom_call_target="tpu_custom_call", output_to_operand_aliasing={{0}: (4, {}), {1}: (5, {}), {2}: (6, {}), {3}: (7, {}), {4}... | custom-call | tf_op jit(solution)/shard_map/pallas_call | solution.py:475
  25.8 12.2 %all_to_all.5.m_ref = f32[16,8,128]{2,1,0:T(8,128)S(1)} all-to-all(f32[16,8,128]{2,1,0:T(8,128)S(1)} %get-tuple-element.107), channel_id=1, replica_groups=mesh['group'=2,'wide'=4,'narrow'=4] {'wide','narrow'}, dimensions={0} | all-to-all | bytes 131072 | tf_op jit(solution)/shard_map/all_to_all | solution.py:588
  38.0 2.4 %shard_map.56 = (f32[16,64,256]{2,1,0:T(8,128)}, f32[16,64,256]{2,1,0:T(8,128)}) custom-call(f32[16,8,128]{2,1,0:T(8,128)S(1)} %all_to_all.5.m_ref, f32[16,64,256]{2,1,0:T(8,128)S(1)} %get-tuple-element.59.b_ref, f32[16,64,256]{2,1,0:T(8,128)S(1)} %get-tuple-element.108.refs_0_, f32[16,64,256]{2,1,0:T(8,128)S(1)} %get-tuple-element.109.refs_1_, ...), custom_call_target="tpu_custom_call" | custom-call | tf_op jit(solution)/shard_map/pallas_call | solution.py:564
  (1 shorter events, 0.0 us)
Async XLA Ops:
  2.4 16.5 %collective-permute-start.2 = (bf16[24,64,256]{2,1,0:T(8,128)(2,1)S(1)}, bf16[24,64,256]{2,1,0:T(8,128)(2,1)S(1)}, u32[]{:S(2)}, u32[]{:S(2)}) collective-permute-start(bf16[24,64,256]{2,1,0:T(8,128)(2,1)S(1)} %get-tuple-element.78), channel_id=1, source_target_pairs={{0,4},{1,5},{2,6},{3,7},{4,0},{5,1},{6,2},{7,3},{8,12},{9,13},{10,... | collective-permute-start | bytes 2359304 | tf_op jit(solution)/shard_map/ppermute | solution.py:183
  2.9 19.2 %collective-permute-start.4 = (bf16[24,64,256]{2,1,0:T(8,128)(2,1)S(1)}, bf16[24,64,256]{2,1,0:T(8,128)(2,1)S(1)}, u32[]{:S(2)}, u32[]{:S(2)}) collective-permute-start(bf16[24,64,256]{2,1,0:T(8,128)(2,1)S(1)} %get-tuple-element.93), channel_id=1, source_target_pairs={{4,8},{5,9},{6,10},{7,11},{8,4},{9,5},{10,6},{11,7},{20,24},{21,25... | collective-permute-start | bytes 2359304 | tf_op jit(solution)/shard_map/ppermute | solution.py:183
  3.6 9.4 %collective-permute-start = (f32[2,16,8,256]{3,2,1,0:T(8,128)S(1)}, f32[2,16,8,256]{3,2,1,0:T(8,128)S(1)}, u32[]{:S(2)}, u32[]{:S(2)}) collective-permute-start(f32[2,16,8,256]{3,2,1,0:T(8,128)S(1)} %get-tuple-element.63), channel_id=1, source_target_pairs={{1,2},{2,1},{5,6},{6,5},{9,10},{10,9},{13,14},{14,13},{17,18},{18,... | collective-permute-start | bytes 786440 | tf_op jit(solution)/shard_map/ppermute | solution.py:183
  4.3 10.7 %collective-permute-start.1 = (f32[2,16,8,256]{3,2,1,0:T(8,128)S(1)}, f32[2,16,8,256]{3,2,1,0:T(8,128)S(1)}, u32[]{:S(2)}, u32[]{:S(2)}) collective-permute-start(f32[2,16,8,256]{3,2,1,0:T(8,128)S(1)} %get-tuple-element.64), channel_id=1, source_target_pairs={{0,1},{1,0},{2,3},{3,2},{4,5},{5,4},{6,7},{7,6},{8,9},{9,8},{10,11... | collective-permute-start | bytes 786440 | tf_op jit(solution)/shard_map/ppermute | solution.py:183
  15.0 3.8 %collective-permute-start.3 = (f32[2,4,2,8,256]{4,3,2,1,0:T(8,128)S(1)}, f32[2,4,2,8,256]{4,3,2,1,0:T(8,128)S(1)}, u32[]{:S(2)}, u32[]{:S(2)}) collective-permute-start(f32[2,4,2,8,256]{4,3,2,1,0:T(8,128)S(1)} %get-tuple-element.79), channel_id=1, source_target_pairs={{0,4},{1,5},{2,6},{3,7},{4,0},{5,1},{6,2},{7,3},{8,12},{9,13},{10,... | collective-permute-start | bytes 393224 | tf_op jit(solution)/shard_map/ppermute | solution.py:183
  16.8 5.2 %collective-permute-start.5 = (f32[2,4,2,8,256]{4,3,2,1,0:T(8,128)S(1)}, f32[2,4,2,8,256]{4,3,2,1,0:T(8,128)S(1)}, u32[]{:S(2)}, u32[]{:S(2)}) collective-permute-start(f32[2,4,2,8,256]{4,3,2,1,0:T(8,128)S(1)} %get-tuple-element.94), channel_id=1, source_target_pairs={{4,8},{5,9},{6,10},{7,11},{8,4},{9,5},{10,6},{11,7},{20,24},{21,25... | collective-permute-start | bytes 393224 | tf_op jit(solution)/shard_map/ppermute | solution.py:183

commit v10 on v9

--- a/solution.py
+++ b/solution.py
@@ -320,13 +320,100 @@
             m_ref[2 * step] = carry[1]
 
 
+def end_runs(up, rows, step):
+    h = STEPS
+    runs = [(jnp.where(up, rows + h - step, h), step, True)]
+    if step < h:
+        runs.append((jnp.where(up, rows + h, step), h - step, False))
+    return runs
+
+
+def wide_fill(up, w_in, rows, u_even, diag, coef):
+    h = STEPS
+
+    def layer(d):
+        return jnp.where(up, rows + h - 1 + d, h - d)
+
+    def plane(k):
+        return w_in[k].astype(jnp.float32)
+
+    def fill(near, d, _):
+        k = wide_plane(d, near)
+        value = plane(k)
+        if near:
+            k += 1
+            value = value + plane(k)
+        settle(u_even, diag, coef, layer(d), h, value, plane(k + 1), plane(k + 2))
+        return 0
+
+    lax.fori_loop(1, NEAR + 1, functools.partial(fill, True), 0)
+    lax.fori_loop(NEAR + 1, h, functools.partial(fill, False), 0)
+    place_u(u_even, layer(h), h, plane(WIDE_PLANES - 1))
+
+
+def corner_fill(up, c_in, rows, columns, u_even, diag, coef):
+    h = STEPS
+
+    def layer(d):
+        return jnp.where(up, rows + h - 1 + d, h - d)
+
+    for side, above in enumerate(sides()[1]):
+        left = pl.multiple_of(jnp.where(above, columns + h, 0), 8)
+        for p, (d, other) in enumerate(PAIRS):
+            near = [c_in[k, p, side] for k in range(2)]
+            outside(u_even, diag, coef, layer(d), left, *near)
+            if other != d:
+                shift = jnp.where(above, d, h - d)
+                far = [pltpu.roll(block, shift, 0) for block in near]
+                outside(u_even, diag, coef, layer(other), left, *far)
+
+
+def halo_layers(up, rows, step):
+    base, first = jnp.where(up, rows + STEPS, 0), jnp.where(up, 0, step)
+    return [(first + k, base + first + k) for k in range(STEPS - step)]
+
+
+def early_kernel(b_ref, m_in, w_in, *refs):
+    refs = refs[STEPS + 4 :]
+    field, (u_even, u_odd, diag, coef, m_out, rim, keep) = refs[:STEPS], refs[STEPS:]
+    rows, columns, depth = b_ref.shape
+    up = sides()[0][0]
+    everything = (b_ref, field, u_even, u_odd, diag, coef)
+    tiles = range(1, columns // 8 + 1)
+
+    def save(step, buffer):
+        for k, i in halo_layers(up, rows, step):
+            for which, t in enumerate((tiles[1], tiles[-2])):
+                for half in range(2):
+                    rim[step, k, which, half] = buffer[i, half, pl.ds(8 * t + 8, 8), :]
+
+    wide_fill(up, w_in, rows, u_even, diag, coef)
+    for k, i in halo_layers(up, rows, 0):
+        for which, t in enumerate((tiles[0], tiles[-1])):
+            for half in range(2):
+                keep[k, which, half] = u_even[i, half, pl.ds(8 * t + 8, 8), :]
+    save(0, u_even)
+    m_out[0] = m_in[0]
+    for step in range(1, STEPS + 1):
+        carry = (m_in[2 * step - 1], m_in[2 * step] if step < STEPS else m_in[0])
+        runs = end_runs(up, rows, step)
+        carry = advance(step, runs, everything, carry, tiles, (tiles[0], tiles[-1]))
+        m_out[2 * step - 1] = carry[0]
+        if step < STEPS:
+            m_out[2 * step] = carry[1]
+            save(step, u_odd if step % 2 else u_even)
+
+
 def border_kernel(b_ref, m_in, *refs):
-    n_in, refs = refs[:2], refs[2 + STEPS + 4 :]
+    n_in, (c_in, rim, keep), refs = refs[:2], refs[2:5], refs[5 + STEPS + 4 :]
     field, (u_even, u_odd, diag, coef, m_out) = refs[:STEPS], refs[STEPS:]
     rows, columns, depth = b_ref.shape
     h = STEPS
     tiles = columns // 8 + 2
-    left = [pl.multiple_of(jnp.where(up, columns + h, 0), 8) for up in sides()[1]]
+    outermost = (0, 1, tiles - 2, tiles - 1)
+    wide, narrow = sides()
+    left = [pl.multiple_of(jnp.where(up, columns + h, 0), 8) for up in narrow]
+    up = wide[0]
     everything = (b_ref, field, u_even, u_odd, diag, coef)
 
     def fill(i, _):
@@ -337,80 +424,63 @@
             place_u(u_even, at, y + h, coef[at, pl.ds(y + h, 8), :] * b_ref[i, pl.ds(y, 8), :])
         return 0
 
-    for i in range(rows):
-        fill(i, 0)
-    m_out[0] = m_in[0]
-    for step in range(1, STEPS + 1):
+    def renew(step, layers):
         source = u_even if step % 2 else u_odd
         before = b_ref if step == 1 else field[step - 2]
-        for i in range(step - 1, rows - step + 1):
+        for i in layers:
             for y in (8, columns - 9):
                 row = coef[i + h, y + h : y + h + 1, :] * before[i, y : y + 1, :]
                 for half in range(2):
                     source[i + h, half, y + h + 8 : y + h + 9, :] = row[
                         :, half * LANES : (half + 1) * LANES
                     ]
+
+    for i in range(rows):
+        fill(i, 0)
+    moments = [(m_in[2 * k - 1], m_in[2 * k] if k < h else m_in[0]) for k in range(1, h + 1)]
+    for step in range(1, h + 1):
+        renew(step, range(step - 1, rows - step + 1))
         count = max(rows - 2 * step, 0)
-        carry = (m_in[2 * step - 1], m_in[2 * step] if step < STEPS else m_in[0])
         for start, part in ((step, count // 2), (step + count // 2, count - count // 2)):
             if part:
                 runs = [(start + h, part, True)]
-                carry = advance(step, runs, everything, carry, (0, 1, tiles - 2, tiles - 1))
+                moments[step - 1] = advance(step, runs, everything, moments[step - 1], outermost)
+
+    corner_fill(up, c_in, rows, columns, u_even, diag, coef)
+    for k, i in halo_layers(up, rows, 0):
+        for which, t in enumerate((1, tiles - 2)):
+            for half in range(2):
+                u_even[i, half, pl.ds(8 * t + 8, 8), :] = keep[k, which, half]
+    m_out[0] = m_in[0]
+    for step in range(1, h + 1):
+        source = u_even if step % 2 else u_odd
+        first = jnp.where(up, rows - step, 0)
+        renew(step, [first + k for k in range(step)])
+        for k, i in halo_layers(up, rows, step):
+            for half in range(2):
+                source[i, half, 24:25, :] = rim[step - 1, k, 0, half][:1]
+                source[i, half, columns + 7 : columns + 8, :] = rim[step - 1, k, 1, half][7:]
+        runs = end_runs(up, rows, step)
+        carry = advance(step, runs, everything, moments[step - 1], outermost)
         m_out[2 * step - 1] = carry[0]
-        if step < STEPS:
+        if step < h:
             m_out[2 * step] = carry[1]
 
 
-def outer_kernel(pairing, b_ref, m_in, *refs):
+def late_kernel(b_ref, m_in, *refs):
     (w_in, c_in), refs = refs[:2], refs[2 + STEPS + 4 :]
     field, (u_even, u_odd, diag, coef, m_out) = refs[:STEPS], refs[STEPS:]
     rows, columns, depth = b_ref.shape
-    h = STEPS
-    wide, narrow = sides()
-    up = wide[pairing]
-    left = [pl.multiple_of(jnp.where(side, columns + h, 0), 8) for side in narrow]
+    up = sides()[0][1]
     everything = (b_ref, field, u_even, u_odd, diag, coef)
-
-    def halo_layer(d):
-        return jnp.where(up, rows + h - 1 + d, h - d)
-
-    def plane(k):
-        return w_in[k].astype(jnp.float32)
-
-    def fill(near, d, _):
-        k = wide_plane(d, near)
-        value = plane(k)
-        if near:
-            k += 1
-            value = value + plane(k)
-        settle(u_even, diag, coef, halo_layer(d), h, value, plane(k + 1), plane(k + 2))
-        return 0
-
-    lax.fori_loop(1, NEAR + 1, functools.partial(fill, True), 0)
-    lax.fori_loop(NEAR + 1, h, functools.partial(fill, False), 0)
-    place_u(u_even, halo_layer(h), h, plane(WIDE_PLANES - 1))
-    for side in range(2):
-        for p, (d, other) in enumerate(PAIRS):
-            near = [c_in[k, p, side] for k in range(2)]
-            outside(u_even, diag, coef, halo_layer(d), left[side], *near)
-            if other != d:
-                shift = jnp.where(narrow[side], d, h - d)
-                far = [pltpu.roll(block, shift, 0) for block in near]
-                outside(u_even, diag, coef, halo_layer(other), left[side], *far)
-
+    wide_fill(up, w_in, rows, u_even, diag, coef)
+    corner_fill(up, c_in, rows, columns, u_even, diag, coef)
     zero = jnp.zeros((8, LANES), jnp.float32)
     moments = [m_in[0]]
     for step in range(1, STEPS + 1):
         carry = (m_in[2 * step - 1], m_in[2 * step] if step < STEPS else zero)
-        runs = [(jnp.where(up, rows + h - step, h), step, True)]
-        if step < STEPS:
-            runs.append((jnp.where(up, rows + h, step), h - step, False))
-        carry = advance(step, runs, everything, carry)
+        carry = advance(step, end_runs(up, rows, step), everything, carry)
         moments += carry if step < STEPS else carry[:1]
-    if pairing == 0:
-        for k, moment in enumerate(moments):
-            m_out[k] = moment
-        return
 
     def folded(high, low, shift, axis):
         total, error = two_sum(high, pltpu.roll(high, shift, axis))
@@ -469,18 +539,22 @@
     return state, moments
 
 
-def onward(kernel, b, moments, received, state, moments_shape):
+def onward(kernel, b, moments, received, state, moments_shape, extra=()):
     shapes = state_shapes(b) + [jax.ShapeDtypeStruct(moments_shape, jnp.float32)]
-    others = 2 + len(received)
-    *state, moments = pl.pallas_call(
+    shapes += [pltpu.VMEM(shape, jnp.float32) for shape in extra]
+    others, count = 2 + len(received), len(state)
+    outs = pl.pallas_call(
         kernel,
         out_shape=shapes,
-        in_specs=[VMEM] * (others + len(state)),
+        in_specs=[VMEM] * (others + count),
         out_specs=[VMEM] * len(shapes),
-        input_output_aliases={others + k: k for k in range(len(state))},
-        compiler_params=pltpu.CompilerParams(vmem_limit_bytes=26 * MIB),
+        input_output_aliases={others + k: k for k in range(count)},
+        compiler_params=pltpu.CompilerParams(vmem_limit_bytes=24 * MIB),
+        cost_estimate=pl.CostEstimate(
+            flops=120 * b.size, bytes_accessed=24 * b.size, transcendentals=0
+        ),
     )(b, moments, *received, *state)
-    return state, moments
+    return outs[:count], *outs[count:]
 
 
 def coordinates(moment):
@@ -578,13 +652,15 @@
     far, near = swapped(sent[1], 1, None), swapped(sent[0], 0, None)
     narrow_halos = [swapped(sent[2 + k], None, 1 - k) for k in range(2)]
     state, moments = inner(b, c, r)
+    tiles = (2, 2, 8, LANES)
+    extra = [(STEPS, STEPS, *tiles), (STEPS, *tiles)]
+    state, moments, *saved = onward(early_kernel, b, moments, [near], state, moments.shape, extra)
     diagonal = corners(narrow_halos, moments)
     diagonal = [swapped(block, k, None) for k, block in enumerate(diagonal)]
-    state, moments = onward(border_kernel, b, moments, narrow_halos, state, moments.shape)
-    for pairing, received in enumerate(([near, diagonal[0]], [far, diagonal[1]])):
-        shape = (peers, 8, LANES) if pairing else moments.shape
-        kernel = functools.partial(outer_kernel, pairing)
-        state, moments = onward(kernel, b, moments, received, state, shape)
+    received = [*narrow_halos, diagonal[0], *saved]
+    state, moments = onward(border_kernel, b, moments, received, state, moments.shape)
+    received = [far, diagonal[1]]
+    state, moments = onward(late_kernel, b, moments, received, state, (peers, 8, LANES))
     gathered, fields = lax.all_to_all(moments, AXES, 0, 0, tiled=True), state[:STEPS]
     solution, residual = combine(gathered, b, fields)
     return (solution, residual)

time: 40.6 us -> 40.7 us (level)
  waiting for transfers between devices: 1.99 us -> 0.33 us
  Pallas kernels: 15.6 us -> 17.1 us
  starting transfers between devices: 9.84 us -> 10.4 us
    ppermute x6, waiting for transfers between devices: 1.99 us -> 0.33 us  [swapped(): return lax.ppermute(array, AXES, pairs)]
    pallas_call x3, Pallas kernels: 8.26 us -> 9.72 us  [onward(): pl.pallas_call(kernel, out_shape=shapes, in_specs=[VMEM] * (others + coun...]
    ppermute x6, starting transfers between devices: 9.84 us -> 10.4 us  [swapped(): return lax.ppermute(array, AXES, pairs)]
  transfers between devices with their start and end apart: 6 -> 6, of which waited for: 1 -> 1; matrix products, arithmetic and copies ran while one was open for 0% -> 0% of each run, Pallas kernels for 19% -> 23%
where the time goes in v10:
time: 40.7 us; the launch traced here: 40.5 us
  Pallas kernels  17.1 us (42%)
  blocking collectives  11.9 us (29%)
  starting transfers between devices  10.4 us (26%)
  between operations  0.73 us (2%)
    all_to_all x1, blocking collectives, on_device(): lax.all_to_all(moments, AXES, 0, 0, tiled=True)  11.9 us
    ppermute x6, starting transfers between devices, swapped(): return lax.ppermute(array, AXES, pairs)  10.4 us
    pallas_call x3, Pallas kernels, onward(): pl.pallas_call(kernel, out_shape=shapes, in_specs=[VMEM] * (others + coun...  9.72 us
    pallas_call x1, Pallas kernels, inner(): pl.pallas_call(inner_kernel, cost_estimate=pl.CostEstimate(flops=120 * b....  3.24 us
    pallas_call x1, Pallas kernels, combine(): pl.pallas_call(combine_kernel, out_shape=[jax.ShapeDtypeStruct(b.shape, j...  2.38 us
    pallas_call x1, Pallas kernels, messages(): pl.pallas_call(send_kernel, out_shape=outs + [pltpu.VMEM(a.shape, a.dtype...  1.73 us
  transfers between devices with their start and end apart: 6, of which 1 were waited for; matrix products, arithmetic and copies ran while one was open for 0% of the time, Pallas kernels for 23%

profile of v10, /device:TPU:0, one launch (start us, length us, event | category | flops | bytes accessed | tf_op | source)
XLA Modules:
  0.0 40.5 jit_solution(13654453794850170681)
XLA Ops:
  0.6 1.7 %shard_map.50 = (bf16[24,64,256]{2,1,0:T(8,128)(2,1)S(1)}, bf16[24,64,256]{2,1,0:T(8,128)(2,1)S(1)}, f32[2,16,8,256]{3,2,1,0:T(8,128)S(1)}, f32[2,16,8,256]{3,2,...) custom-call(f32[16,64,256]{2,1,0:T(8,128)} %refs_0_.1, ...), custom_call_target="tpu_custom_call" | custom-call | tf_op jit(solution)/shard_map/pallas_call | solution.py:128
  2.4 0.5 %collective-permute-start = (bf16[24,64,256]{2,1,0:T(8,128)(2,1)S(1)}, bf16[24,64,256]{2,1,0:T(8,128)(2,1)S(1)}, u32[]{:S(2)}, u32[]{:S(2)}) collective-permute-start(bf16[24,64,256]{2,1,0:T(8,128)(2,1)S(1)} %get-tuple-element.65), channel_id=1, source_target_pairs={{0,4},{1,5},{2,6},{3,7},{4,0},{5,1},{6,2},{7,3},{8,12},{9,13},{10,... | collective-permute-start | bytes 2359304 | tf_op jit(solution)/shard_map/ppermute | solution.py:183
  2.9 0.7 %collective-permute-start.4 = (bf16[24,64,256]{2,1,0:T(8,128)(2,1)S(1)}, bf16[24,64,256]{2,1,0:T(8,128)(2,1)S(1)}, u32[]{:S(2)}, u32[]{:S(2)}) collective-permute-start(bf16[24,64,256]{2,1,0:T(8,128)(2,1)S(1)} %get-tuple-element.97), channel_id=1, source_target_pairs={{4,8},{5,9},{6,10},{7,11},{8,4},{9,5},{10,6},{11,7},{20,24},{21,25... | collective-permute-start | bytes 2359304 | tf_op jit(solution)/shard_map/ppermute | solution.py:183
  3.6 0.7 %collective-permute-start.1 = (f32[2,16,8,256]{3,2,1,0:T(8,128)S(1)}, f32[2,16,8,256]{3,2,1,0:T(8,128)S(1)}, u32[]{:S(2)}, u32[]{:S(2)}) collective-permute-start(f32[2,16,8,256]{3,2,1,0:T(8,128)S(1)} %get-tuple-element.79), channel_id=1, source_target_pairs={{1,2},{2,1},{5,6},{6,5},{9,10},{10,9},{13,14},{14,13},{17,18},{18,... | collective-permute-start | bytes 786440 | tf_op jit(solution)/shard_map/ppermute | solution.py:183
  4.3 5.5 %collective-permute-start.2 = (f32[2,16,8,256]{3,2,1,0:T(8,128)S(1)}, f32[2,16,8,256]{3,2,1,0:T(8,128)S(1)}, u32[]{:S(2)}, u32[]{:S(2)}) collective-permute-start(f32[2,16,8,256]{3,2,1,0:T(8,128)S(1)} %get-tuple-element.80), channel_id=1, source_target_pairs={{0,1},{1,0},{2,3},{3,2},{4,5},{5,4},{6,7},{7,6},{8,9},{9,8},{10,11... | collective-permute-start | bytes 786440 | tf_op jit(solution)/shard_map/ppermute | solution.py:183
  9.8 3.2 %shard_map.51 = (f32[16,64,256]{2,1,0:T(8,128)S(1)}, f32[16,64,256]{2,1,0:T(8,128)S(1)}, f32[16,64,256]{2,1,0:T(8,128)S(1)}, f32[16,64,256]{2,1,0:T(8,128)S(1)},...) custom-call(f32[16,64,256]{2,1,0:T(8,128)S(1)} %get-tuple-element.61, ...), custom_call_target="tpu_custom_call" | custom-call | flops 31457280 | bytes 6291456 | tf_op jit(solution)/shard_map/pallas_call | solution.py:529
  13.0 0.0 collective-permute-done.w_in
  13.0 3.0 %shard_map.52 = (f32[16,64,256]{2,1,0:T(8,128)S(1)}, f32[16,64,256]{2,1,0:T(8,128)S(1)}, f32[16,64,256]{2,1,0:T(8,128)S(1)}, f32[16,64,256]{2,1,0:T(8,128)S(1)},...) custom-call(f32[16,64,256]{2,1,0:T(8,128)S(1)} %get-tuple-element.61, ...), custom_call_target="tpu_custom_call", output_to_operand_aliasing={{0}: (3, {}), {1}: (4, {}), {2}: (5, {}), {3}: (6, {}), {4}... | custom-call | flops 31457280 | bytes 6291456 | tf_op jit(solution)/shard_map/pallas_call | solution.py:546
  16.0 0.0 collective-permute-done.1.refs_0_
  16.0 0.0 collective-permute-done.2.refs_1_
  16.1 0.1 shard_map.53
  16.1 2.3 %collective-permute-start.3 = (f32[2,4,2,8,256]{4,3,2,1,0:T(8,128)S(1)}, f32[2,4,2,8,256]{4,3,2,1,0:T(8,128)S(1)}, u32[]{:S(2)}, u32[]{:S(2)}) collective-permute-start(f32[2,4,2,8,256]{4,3,2,1,0:T(8,128)S(1)} %get-tuple-element.81), channel_id=1, source_target_pairs={{0,4},{1,5},{2,6},{3,7},{4,0},{5,1},{6,2},{7,3},{8,12},{9,13},{10,... | collective-permute-start | bytes 393224 | tf_op jit(solution)/shard_map/ppermute | solution.py:183
  18.5 0.7 %collective-permute-start.5 = (f32[2,4,2,8,256]{4,3,2,1,0:T(8,128)S(1)}, f32[2,4,2,8,256]{4,3,2,1,0:T(8,128)S(1)}, u32[]{:S(2)}, u32[]{:S(2)}) collective-permute-start(f32[2,4,2,8,256]{4,3,2,1,0:T(8,128)S(1)} %get-tuple-element.98), channel_id=1, source_target_pairs={{4,8},{5,9},{6,10},{7,11},{8,4},{9,5},{10,6},{11,7},{20,24},{21,25... | collective-permute-start | bytes 393224 | tf_op jit(solution)/shard_map/ppermute | solution.py:183
  19.1 0.3 collective-permute-done.3.refs_2_
  19.4 3.0 %shard_map.54 = (f32[16,64,256]{2,1,0:T(8,128)S(1)}, f32[16,64,256]{2,1,0:T(8,128)S(1)}, f32[16,64,256]{2,1,0:T(8,128)S(1)}, f32[16,64,256]{2,1,0:T(8,128)S(1)},...) custom-call(f32[16,64,256]{2,1,0:T(8,128)S(1)} %get-tuple-element.61, ...), custom_call_target="tpu_custom_call", output_to_operand_aliasing={{0}: (7, {}), {1}: (8, {}), {2}: (9, {}), {3}: (10, {}), {4... | custom-call | flops 31457280 | bytes 6291456 | tf_op jit(solution)/shard_map/pallas_call | solution.py:546
  22.4 0.0 collective-permute-done.4.refs_0_
  22.4 0.0 collective-permute-done.5.refs_1_
  22.4 3.7 %shard_map.55 = (f32[16,64,256]{2,1,0:T(8,128)S(1)}, f32[16,64,256]{2,1,0:T(8,128)S(1)}, f32[16,64,256]{2,1,0:T(8,128)S(1)}, f32[16,64,256]{2,1,0:T(8,128)S(1)},...) custom-call(f32[16,64,256]{2,1,0:T(8,128)S(1)} %get-tuple-element.61, ...), custom_call_target="tpu_custom_call", output_to_operand_aliasing={{0}: (4, {}), {1}: (5, {}), {2}: (6, {}), {3}: (7, {}), {4}... | custom-call | flops 31457280 | bytes 6291456 | tf_op jit(solution)/shard_map/pallas_call | solution.py:546
  26.2 11.9 %all_to_all.5.m_ref = f32[16,8,128]{2,1,0:T(8,128)S(1)} all-to-all(f32[16,8,128]{2,1,0:T(8,128)S(1)} %get-tuple-element.111), channel_id=1, replica_groups=mesh['group'=2,'wide'=4,'narrow'=4] {'wide','narrow'}, dimensions={0} | all-to-all | bytes 131072 | tf_op jit(solution)/shard_map/all_to_all | solution.py:664
  38.1 2.4 %shard_map.56 = (f32[16,64,256]{2,1,0:T(8,128)}, f32[16,64,256]{2,1,0:T(8,128)}) custom-call(f32[16,8,128]{2,1,0:T(8,128)S(1)} %all_to_all.5.m_ref, f32[16,64,256]{2,1,0:T(8,128)S(1)} %get-tuple-element.61.b_ref, f32[16,64,256]{2,1,0:T(8,128)S(1)} %get-tuple-element.112.refs_0_, f32[16,64,256]{2,1,0:T(8,128)S(1)} %get-tuple-element.113.refs_1_, ...), custom_call_target="tpu_custom_call" | custom-call | tf_op jit(solution)/shard_map/pallas_call | solution.py:638
Async XLA Ops:
  2.4 10.6 %collective-permute-start = (bf16[24,64,256]{2,1,0:T(8,128)(2,1)S(1)}, bf16[24,64,256]{2,1,0:T(8,128)(2,1)S(1)}, u32[]{:S(2)}, u32[]{:S(2)}) collective-permute-start(bf16[24,64,256]{2,1,0:T(8,128)(2,1)S(1)} %get-tuple-element.65), channel_id=1, source_target_pairs={{0,4},{1,5},{2,6},{3,7},{4,0},{5,1},{6,2},{7,3},{8,12},{9,13},{10,... | collective-permute-start | bytes 2359304 | tf_op jit(solution)/shard_map/ppermute | solution.py:183
  2.9 19.5 %collective-permute-start.4 = (bf16[24,64,256]{2,1,0:T(8,128)(2,1)S(1)}, bf16[24,64,256]{2,1,0:T(8,128)(2,1)S(1)}, u32[]{:S(2)}, u32[]{:S(2)}) collective-permute-start(bf16[24,64,256]{2,1,0:T(8,128)(2,1)S(1)} %get-tuple-element.97), channel_id=1, source_target_pairs={{4,8},{5,9},{6,10},{7,11},{8,4},{9,5},{10,6},{11,7},{20,24},{21,25... | collective-permute-start | bytes 2359304 | tf_op jit(solution)/shard_map/ppermute | solution.py:183
  3.6 12.4 %collective-permute-start.1 = (f32[2,16,8,256]{3,2,1,0:T(8,128)S(1)}, f32[2,16,8,256]{3,2,1,0:T(8,128)S(1)}, u32[]{:S(2)}, u32[]{:S(2)}) collective-permute-start(f32[2,16,8,256]{3,2,1,0:T(8,128)S(1)} %get-tuple-element.79), channel_id=1, source_target_pairs={{1,2},{2,1},{5,6},{6,5},{9,10},{10,9},{13,14},{14,13},{17,18},{18,... | collective-permute-start | bytes 786440 | tf_op jit(solution)/shard_map/ppermute | solution.py:183
  4.3 11.8 %collective-permute-start.2 = (f32[2,16,8,256]{3,2,1,0:T(8,128)S(1)}, f32[2,16,8,256]{3,2,1,0:T(8,128)S(1)}, u32[]{:S(2)}, u32[]{:S(2)}) collective-permute-start(f32[2,16,8,256]{3,2,1,0:T(8,128)S(1)} %get-tuple-element.80), channel_id=1, source_target_pairs={{0,1},{1,0},{2,3},{3,2},{4,5},{5,4},{6,7},{7,6},{8,9},{9,8},{10,11... | collective-permute-start | bytes 786440 | tf_op jit(solution)/shard_map/ppermute | solution.py:183
  16.1 3.3 %collective-permute-start.3 = (f32[2,4,2,8,256]{4,3,2,1,0:T(8,128)S(1)}, f32[2,4,2,8,256]{4,3,2,1,0:T(8,128)S(1)}, u32[]{:S(2)}, u32[]{:S(2)}) collective-permute-start(f32[2,4,2,8,256]{4,3,2,1,0:T(8,128)S(1)} %get-tuple-element.81), channel_id=1, source_target_pairs={{0,4},{1,5},{2,6},{3,7},{4,0},{5,1},{6,2},{7,3},{8,12},{9,13},{10,... | collective-permute-start | bytes 393224 | tf_op jit(solution)/shard_map/ppermute | solution.py:183
  18.5 4.0 %collective-permute-start.5 = (f32[2,4,2,8,256]{4,3,2,1,0:T(8,128)S(1)}, f32[2,4,2,8,256]{4,3,2,1,0:T(8,128)S(1)}, u32[]{:S(2)}, u32[]{:S(2)}) collective-permute-start(f32[2,4,2,8,256]{4,3,2,1,0:T(8,128)S(1)} %get-tuple-element.98), channel_id=1, source_target_pairs={{4,8},{5,9},{6,10},{7,11},{8,4},{9,5},{10,6},{11,7},{20,24},{21,25... | collective-permute-start | bytes 393224 | tf_op jit(solution)/shard_map/ppermute | solution.py:183

commit v11 on v10

--- a/solution.py
+++ b/solution.py
@@ -139,26 +139,40 @@
 PAIRS = [(d, STEPS - d) for d in range(1, STEPS // 2 + 1)]
 
 
+def unpacked(packed):
+    reaction = jnp.floor(packed * 128.0) * (1.0 / 128.0)
+    return (packed - reaction) * 256.0, reaction
+
+
 def corner_kernel(*refs):
     n_in, c_out = refs[:2], refs[3:]
     rows = n_in[0].shape[1]
     wide, narrow = sides()
     sub = lax.broadcasted_iota(jnp.int32, n_in[0].shape[2:], 0)
     for a in range(2):
-        for side in range(2):
-            up = narrow[side]
-            for p, (d, other) in enumerate(PAIRS):
+        for p, (d, other) in enumerate(PAIRS):
+            blocks = []
+            for side in range(2):
+                up = narrow[side]
                 shift = jnp.where(up, STEPS - d, d)
                 mine = jnp.where(up, sub, STEPS - 1 - sub) < STEPS - d
-                for k in range(2):
-                    near = n_in[side][k, edge_layer(wide[a], rows, d)]
-                    far = n_in[side][k, edge_layer(wide[a], rows, other)]
-                    c_out[a][k, p, side] = jnp.where(mine, near, pltpu.roll(far, shift, 0))
+                value, packed = (
+                    jnp.where(
+                        mine,
+                        n_in[side][k, edge_layer(wide[a], rows, d)],
+                        pltpu.roll(n_in[side][k, edge_layer(wide[a], rows, other)], shift, 0),
+                    )
+                    for k in range(2)
+                )
+                blocks.append((value, *unpacked(packed)))
+            for k in range(3):
+                both = jnp.concatenate([blocks[0][k], blocks[1][k]], axis=0)
+                c_out[a][k, p] = both.astype(jnp.bfloat16)
 
 
 def corners(narrow_halos, after):
     depth = narrow_halos[0].shape[-1]
-    shape = jax.ShapeDtypeStruct((2, len(PAIRS), 2, STEPS, depth), jnp.float32)
+    shape = jax.ShapeDtypeStruct((3, len(PAIRS), 2 * STEPS, depth), jnp.bfloat16)
     return pl.pallas_call(
         corner_kernel,
         out_shape=[shape] * 2,
@@ -211,9 +225,7 @@
 
 
 def outside(u_even, diag, coef, i, y, value, packed):
-    reaction = jnp.floor(packed * 128.0) * (1.0 / 128.0)
-    conduct = (packed - reaction) * 256.0
-    settle(u_even, diag, coef, i, y, value, conduct, reaction)
+    settle(u_even, diag, coef, i, y, value, *unpacked(packed))
 
 
 def advance(step, runs, refs, carry, chosen=None, silent=()):
@@ -303,18 +315,11 @@
     zero = jnp.zeros((8, LANES), jnp.float32)
     m_ref[0] = lax.fori_loop(0, rows, fill, zero, unroll=4)
     for step in range(1, STEPS + 1):
-        quads, rest = divmod(max(rows - 2 * step, 0), 4)
-
-        def work(start, count, carry, step=step):
-            runs = [(start, count, True)]
-            return advance(step, runs, everything, carry, tiles, (tiles[0], tiles[-1]))
-
-        def body(m, carry, step=step, work=work):
-            return work(4 * m + h + step, 4, carry)
-
-        carry = lax.fori_loop(0, quads, body, (zero, zero))
-        if rest:
-            carry = work(h + rows - step - rest, rest, carry)
+        count, carry = max(rows - 2 * step, 0), (zero, zero)
+        for start, part in ((step, count // 2), (step + count // 2, count - count // 2)):
+            if part:
+                runs = [(start + h, part, True)]
+                carry = advance(step, runs, everything, carry, tiles, (tiles[0], tiles[-1]))
         m_ref[2 * step - 1] = carry[0]
         if step < STEPS:
             m_ref[2 * step] = carry[1]
@@ -360,12 +365,12 @@
     for side, above in enumerate(sides()[1]):
         left = pl.multiple_of(jnp.where(above, columns + h, 0), 8)
         for p, (d, other) in enumerate(PAIRS):
-            near = [c_in[k, p, side] for k in range(2)]
-            outside(u_even, diag, coef, layer(d), left, *near)
+            near = [c_in[k, p].astype(jnp.float32)[h * side : h * side + h] for k in range(3)]
+            settle(u_even, diag, coef, layer(d), left, *near)
             if other != d:
                 shift = jnp.where(above, d, h - d)
                 far = [pltpu.roll(block, shift, 0) for block in near]
-                outside(u_even, diag, coef, layer(other), left, *far)
+                settle(u_even, diag, coef, layer(other), left, *far)
 
 
 def halo_layers(up, rows, step):
@@ -517,6 +522,31 @@
     return total, error
 
 
+def merge_kernel(mine, other, out_ref):
+    total, error = two_sum(mine[0], other[0])
+    lane = lax.broadcasted_iota(jnp.int32, (8, LANES), 1)
+    low = lax.rem(lane // QUARTER, 2) == 1
+    message = total + jnp.where(low, pltpu.roll(error, QUARTER, 1), 0.0)
+    for k in range(out_ref.shape[0]):
+        out_ref[k] = message
+
+
+def gather(message):
+    wides, narrows = lax.axis_size("wide"), lax.axis_size("narrow")
+    peers = wides // 2 * narrows
+    merged = pl.pallas_call(
+        merge_kernel,
+        out_shape=jax.ShapeDtypeStruct((peers, 8, LANES), jnp.float32),
+        in_specs=[VMEM] * 2,
+        out_specs=VMEM,
+        compiler_params=pltpu.CompilerParams(vmem_limit_bytes=2 * MIB),
+    )(message, swapped(message, 0, None))
+    groups = [
+        [w * narrows + n for w in range(core, wides, 2) for n in range(narrows)] for core in range(2)
+    ]
+    return lax.all_to_all(merged, AXES, 0, 0, axis_index_groups=groups, tiled=True)
+
+
 def state_shapes(b):
     rows, columns, depth = b.shape
     wide, narrow = rows + 2 * STEPS, columns + 2 * STEPS
@@ -647,7 +677,6 @@
 
 
 def on_device(right_side, conduct_half, reaction_half):
-    peers = lax.axis_size("wide") * lax.axis_size("narrow")
     *sent, b, c, r = messages(right_side, conduct_half, reaction_half)
     far, near = swapped(sent[1], 1, None), swapped(sent[0], 0, None)
     narrow_halos = [swapped(sent[2 + k], None, 1 - k) for k in range(2)]
@@ -660,8 +689,8 @@
     received = [*narrow_halos, diagonal[0], *saved]
     state, moments = onward(border_kernel, b, moments, received, state, moments.shape)
     received = [far, diagonal[1]]
-    state, moments = onward(late_kernel, b, moments, received, state, (peers, 8, LANES))
-    gathered, fields = lax.all_to_all(moments, AXES, 0, 0, tiled=True), state[:STEPS]
+    state, moments = onward(late_kernel, b, moments, received, state, (1, 8, LANES))
+    gathered, fields = gather(moments), state[:STEPS]
     solution, residual = combine(gathered, b, fields)
     return (solution, residual)
 

time: 40.7 us -> 41 us (level)
  starting transfers between devices: 10.4 us -> 13 us
  blocking collectives: 11.9 us -> 9.58 us
  Pallas kernels: 17.1 us -> 16.4 us
  waiting for transfers between devices: 0.33 us -> 0.94 us
    ppermute x6 -> x7, starting transfers between devices: 10.4 us -> 13 us  [swapped(): return lax.ppermute(array, AXES, pairs)]
    all_to_all x1, blocking collectives: 11.9 us -> 9.58 us  [gather(): lax.all_to_all(merged, AXES, 0, 0, axis_index_groups=groups, tiled=True)]
    pallas_call x1, Pallas kernels: 3.24 us -> 2.4 us  [inner(): pl.pallas_call(inner_kernel, cost_estimate=pl.CostEstimate(flops=120 * b....]
    ppermute x6 -> x7, waiting for transfers between devices: 0.33 us -> 0.94 us  [swapped(): return lax.ppermute(array, AXES, pairs)]
  transfers between devices with their start and end apart: 6 -> 7, of which waited for: 1 -> 2; matrix products, arithmetic and copies ran while one was open for 0% -> 0% of each run, Pallas kernels for 23% -> 21%
where the time goes in v11:
time: 41 us; the launch traced here: 40.7 us
  Pallas kernels  16.4 us (40%)
  starting transfers between devices  13 us (32%)
  blocking collectives  9.58 us (23%)
  waiting for transfers between devices  0.94 us (2%)
  between operations  0.9 us (2%)
    ppermute x7, starting transfers between devices, swapped(): return lax.ppermute(array, AXES, pairs)  13 us
    pallas_call x3, Pallas kernels, onward(): pl.pallas_call(kernel, out_shape=shapes, in_specs=[VMEM] * (others + coun...  9.71 us
    all_to_all x1, blocking collectives, gather(): lax.all_to_all(merged, AXES, 0, 0, axis_index_groups=groups, tiled=True)  9.58 us
    pallas_call x1, Pallas kernels, inner(): pl.pallas_call(inner_kernel, cost_estimate=pl.CostEstimate(flops=120 * b....  2.4 us
    pallas_call x1, Pallas kernels, combine(): pl.pallas_call(combine_kernel, out_shape=[jax.ShapeDtypeStruct(b.shape, j...  2.37 us
    pallas_call x1, Pallas kernels, messages(): pl.pallas_call(send_kernel, out_shape=outs + [pltpu.VMEM(a.shape, a.dtype...  1.73 us
    ppermute x7, waiting for transfers between devices, swapped(): return lax.ppermute(array, AXES, pairs)  0.94 us
  transfers between devices with their start and end apart: 7, of which 2 were waited for; matrix products, arithmetic and copies ran while one was open for 0% of the time, Pallas kernels for 21%

profile of v11, /device:TPU:0, one launch (start us, length us, event | category | flops | bytes accessed | tf_op | source)
XLA Modules:
  0.0 40.7 jit_solution(9843469110653164336)
XLA Ops:
  0.6 1.7 %shard_map.50 = (bf16[24,64,256]{2,1,0:T(8,128)(2,1)S(1)}, bf16[24,64,256]{2,1,0:T(8,128)(2,1)S(1)}, f32[2,16,8,256]{3,2,1,0:T(8,128)S(1)}, f32[2,16,8,256]{3,2,...) custom-call(f32[16,64,256]{2,1,0:T(8,128)} %refs_0_.1, ...), custom_call_target="tpu_custom_call" | custom-call | tf_op jit(solution)/shard_map/pallas_call | solution.py:128
  2.4 0.5 %collective-permute-start = (bf16[24,64,256]{2,1,0:T(8,128)(2,1)S(1)}, bf16[24,64,256]{2,1,0:T(8,128)(2,1)S(1)}, u32[]{:S(2)}, u32[]{:S(2)}) collective-permute-start(bf16[24,64,256]{2,1,0:T(8,128)(2,1)S(1)} %get-tuple-element.65), channel_id=1, source_target_pairs={{0,4},{1,5},{2,6},{3,7},{4,0},{5,1},{6,2},{7,3},{8,12},{9,13},{10,... | collective-permute-start | bytes 2359304 | tf_op jit(solution)/shard_map/ppermute | solution.py:197
  2.9 0.7 %collective-permute-start.4 = (bf16[24,64,256]{2,1,0:T(8,128)(2,1)S(1)}, bf16[24,64,256]{2,1,0:T(8,128)(2,1)S(1)}, u32[]{:S(2)}, u32[]{:S(2)}) collective-permute-start(bf16[24,64,256]{2,1,0:T(8,128)(2,1)S(1)} %get-tuple-element.97), channel_id=1, source_target_pairs={{4,8},{5,9},{6,10},{7,11},{8,4},{9,5},{10,6},{11,7},{20,24},{21,25... | collective-permute-start | bytes 2359304 | tf_op jit(solution)/shard_map/ppermute | solution.py:197
  3.6 0.7 %collective-permute-start.1 = (f32[2,16,8,256]{3,2,1,0:T(8,128)S(1)}, f32[2,16,8,256]{3,2,1,0:T(8,128)S(1)}, u32[]{:S(2)}, u32[]{:S(2)}) collective-permute-start(f32[2,16,8,256]{3,2,1,0:T(8,128)S(1)} %get-tuple-element.79), channel_id=1, source_target_pairs={{1,2},{2,1},{5,6},{6,5},{9,10},{10,9},{13,14},{14,13},{17,18},{18,... | collective-permute-start | bytes 786440 | tf_op jit(solution)/shard_map/ppermute | solution.py:197
  4.3 5.5 %collective-permute-start.2 = (f32[2,16,8,256]{3,2,1,0:T(8,128)S(1)}, f32[2,16,8,256]{3,2,1,0:T(8,128)S(1)}, u32[]{:S(2)}, u32[]{:S(2)}) collective-permute-start(f32[2,16,8,256]{3,2,1,0:T(8,128)S(1)} %get-tuple-element.80), channel_id=1, source_target_pairs={{0,1},{1,0},{2,3},{3,2},{4,5},{5,4},{6,7},{7,6},{8,9},{9,8},{10,11... | collective-permute-start | bytes 786440 | tf_op jit(solution)/shard_map/ppermute | solution.py:197
  9.8 2.4 %shard_map.51 = (f32[16,64,256]{2,1,0:T(8,128)S(1)}, f32[16,64,256]{2,1,0:T(8,128)S(1)}, f32[16,64,256]{2,1,0:T(8,128)S(1)}, f32[16,64,256]{2,1,0:T(8,128)S(1)},...) custom-call(f32[16,64,256]{2,1,0:T(8,128)S(1)} %get-tuple-element.61, ...), custom_call_target="tpu_custom_call" | custom-call | flops 31457280 | bytes 6291456 | tf_op jit(solution)/shard_map/pallas_call | solution.py:559
  12.2 0.0 collective-permute-done.w_in
  12.2 3.0 %shard_map.52 = (f32[16,64,256]{2,1,0:T(8,128)S(1)}, f32[16,64,256]{2,1,0:T(8,128)S(1)}, f32[16,64,256]{2,1,0:T(8,128)S(1)}, f32[16,64,256]{2,1,0:T(8,128)S(1)},...) custom-call(f32[16,64,256]{2,1,0:T(8,128)S(1)} %get-tuple-element.61, ...), custom_call_target="tpu_custom_call", output_to_operand_aliasing={{0}: (3, {}), {1}: (4, {}), {2}: (5, {}), {3}: (6, {}), {4}... | custom-call | flops 31457280 | bytes 6291456 | tf_op jit(solution)/shard_map/pallas_call | solution.py:576
  15.2 0.0 collective-permute-done.1.refs_0_
  15.2 0.0 collective-permute-done.2.refs_1_
  15.2 0.1 shard_map.53
  15.3 2.3 %collective-permute-start.3 = (bf16[3,4,16,256]{3,2,1,0:T(8,128)(2,1)S(1)}, bf16[3,4,16,256]{3,2,1,0:T(8,128)(2,1)S(1)}, u32[]{:S(2)}, u32[]{:S(2)}) collective-permute-start(bf16[3,4,16,256]{3,2,1,0:T(8,128)(2,1)S(1)} %get-tuple-element.81), channel_id=1, source_target_pairs={{0,4},{1,5},{2,6},{3,7},{4,0},{5,1},{6,2},{7,3},{8,12},{9,13},{10,... | collective-permute-start | bytes 294920 | tf_op jit(solution)/shard_map/ppermute | solution.py:197
  17.6 0.8 %collective-permute-start.5 = (bf16[3,4,16,256]{3,2,1,0:T(8,128)(2,1)S(1)}, bf16[3,4,16,256]{3,2,1,0:T(8,128)(2,1)S(1)}, u32[]{:S(2)}, u32[]{:S(2)}) collective-permute-start(bf16[3,4,16,256]{3,2,1,0:T(8,128)(2,1)S(1)} %get-tuple-element.98), channel_id=1, source_target_pairs={{4,8},{5,9},{6,10},{7,11},{8,4},{9,5},{10,6},{11,7},{20,24},{21,25... | collective-permute-start | bytes 294920 | tf_op jit(solution)/shard_map/ppermute | solution.py:197
  18.5 0.1 collective-permute-done.3.refs_2_
  18.6 3.0 %shard_map.54 = (f32[16,64,256]{2,1,0:T(8,128)S(1)}, f32[16,64,256]{2,1,0:T(8,128)S(1)}, f32[16,64,256]{2,1,0:T(8,128)S(1)}, f32[16,64,256]{2,1,0:T(8,128)S(1)},...) custom-call(f32[16,64,256]{2,1,0:T(8,128)S(1)} %get-tuple-element.61, ...), custom_call_target="tpu_custom_call", output_to_operand_aliasing={{0}: (7, {}), {1}: (8, {}), {2}: (9, {}), {3}: (10, {}), {4... | custom-call | flops 31457280 | bytes 6291456 | tf_op jit(solution)/shard_map/pallas_call | solution.py:576
  21.6 0.0 collective-permute-done.4.refs_0_
  21.6 0.0 collective-permute-done.5.refs_1_
  21.6 3.7 %shard_map.55 = (f32[16,64,256]{2,1,0:T(8,128)S(1)}, f32[16,64,256]{2,1,0:T(8,128)S(1)}, f32[16,64,256]{2,1,0:T(8,128)S(1)}, f32[16,64,256]{2,1,0:T(8,128)S(1)},...) custom-call(f32[16,64,256]{2,1,0:T(8,128)S(1)} %get-tuple-element.61, ...), custom_call_target="tpu_custom_call", output_to_operand_aliasing={{0}: (4, {}), {1}: (5, {}), {2}: (6, {}), {3}: (7, {}), {4}... | custom-call | flops 31457280 | bytes 6291456 | tf_op jit(solution)/shard_map/pallas_call | solution.py:576
  25.3 2.4 %collective-permute-start.6 = (f32[1,8,128]{2,1,0:T(8,128)S(1)}, f32[1,8,128]{2,1,0:T(8,128)S(1)}, u32[]{:S(2)}, u32[]{:S(2)}) collective-permute-start(f32[1,8,128]{2,1,0:T(8,128)S(1)} %get-tuple-element.111.mine), channel_id=1, source_target_pairs={{0,4},{1,5},{2,6},{3,7},{4,0},{5,1},{6,2},{7,3},{8,12},{9,13},{10,... | collective-permute-start | bytes 12296 | tf_op jit(solution)/shard_map/ppermute | solution.py:197
  27.7 0.8 %collective-permute-done.6.other = f32[1,8,128]{2,1,0:T(8,128)S(1)} collective-permute-done((f32[1,8,128]{2,1,0:T(8,128)S(1)}, f32[1,8,128]{2,1,0:T(8,128)S(1)}, u32[]{:S(2)}, u32[]{:S(2)}) %collective-permute-start.6) | collective-permute-done | bytes 4128 | tf_op jit(solution)/shard_map/ppermute | solution.py:197
  28.5 0.1 shard_map.56
  28.6 9.6 %all_to_all.5.m_ref = f32[8,8,128]{2,1,0:T(8,128)S(1)} all-to-all(f32[8,8,128]{2,1,0:T(8,128)S(1)} %shard_map.56), channel_id=1, replica_groups={{0,1,2,3,8,9,10,11},{4,5,6,7,12,13,14,15},{16,17,18,19,24,25,26,27},{20..., dimensions={0} | all-to-all | bytes 65536 | tf_op jit(solution)/shard_map/all_to_all | solution.py:547
  38.2 2.4 %shard_map.57 = (f32[16,64,256]{2,1,0:T(8,128)}, f32[16,64,256]{2,1,0:T(8,128)}) custom-call(f32[8,8,128]{2,1,0:T(8,128)S(1)} %all_to_all.5.m_ref, f32[16,64,256]{2,1,0:T(8,128)S(1)} %get-tuple-element.61.b_ref, f32[16,64,256]{2,1,0:T(8,128)S(1)} %get-tuple-element.112.refs_0_, f32[16,64,256]{2,1,0:T(8,128)S(1)} %get-tuple-element.113.refs_1_, ...), custom_call_target="tpu_custom_call" | custom-call | tf_op jit(solution)/shard_map/pallas_call | solution.py:668
Async XLA Ops:
  2.4 9.8 %collective-permute-start = (bf16[24,64,256]{2,1,0:T(8,128)(2,1)S(1)}, bf16[24,64,256]{2,1,0:T(8,128)(2,1)S(1)}, u32[]{:S(2)}, u32[]{:S(2)}) collective-permute-start(bf16[24,64,256]{2,1,0:T(8,128)(2,1)S(1)} %get-tuple-element.65), channel_id=1, source_target_pairs={{0,4},{1,5},{2,6},{3,7},{4,0},{5,1},{6,2},{7,3},{8,12},{9,13},{10,... | collective-permute-start | bytes 2359304 | tf_op jit(solution)/shard_map/ppermute | solution.py:197
  2.9 18.7 %collective-permute-start.4 = (bf16[24,64,256]{2,1,0:T(8,128)(2,1)S(1)}, bf16[24,64,256]{2,1,0:T(8,128)(2,1)S(1)}, u32[]{:S(2)}, u32[]{:S(2)}) collective-permute-start(bf16[24,64,256]{2,1,0:T(8,128)(2,1)S(1)} %get-tuple-element.97), channel_id=1, source_target_pairs={{4,8},{5,9},{6,10},{7,11},{8,4},{9,5},{10,6},{11,7},{20,24},{21,25... | collective-permute-start | bytes 2359304 | tf_op jit(solution)/shard_map/ppermute | solution.py:197
  3.6 11.6 %collective-permute-start.1 = (f32[2,16,8,256]{3,2,1,0:T(8,128)S(1)}, f32[2,16,8,256]{3,2,1,0:T(8,128)S(1)}, u32[]{:S(2)}, u32[]{:S(2)}) collective-permute-start(f32[2,16,8,256]{3,2,1,0:T(8,128)S(1)} %get-tuple-element.79), channel_id=1, source_target_pairs={{1,2},{2,1},{5,6},{6,5},{9,10},{10,9},{13,14},{14,13},{17,18},{18,... | collective-permute-start | bytes 786440 | tf_op jit(solution)/shard_map/ppermute | solution.py:197
  4.3 10.9 %collective-permute-start.2 = (f32[2,16,8,256]{3,2,1,0:T(8,128)S(1)}, f32[2,16,8,256]{3,2,1,0:T(8,128)S(1)}, u32[]{:S(2)}, u32[]{:S(2)}) collective-permute-start(f32[2,16,8,256]{3,2,1,0:T(8,128)S(1)} %get-tuple-element.80), channel_id=1, source_target_pairs={{0,1},{1,0},{2,3},{3,2},{4,5},{5,4},{6,7},{7,6},{8,9},{9,8},{10,11... | collective-permute-start | bytes 786440 | tf_op jit(solution)/shard_map/ppermute | solution.py:197
  15.3 3.3 %collective-permute-start.3 = (bf16[3,4,16,256]{3,2,1,0:T(8,128)(2,1)S(1)}, bf16[3,4,16,256]{3,2,1,0:T(8,128)(2,1)S(1)}, u32[]{:S(2)}, u32[]{:S(2)}) collective-permute-start(bf16[3,4,16,256]{3,2,1,0:T(8,128)(2,1)S(1)} %get-tuple-element.81), channel_id=1, source_target_pairs={{0,4},{1,5},{2,6},{3,7},{4,0},{5,1},{6,2},{7,3},{8,12},{9,13},{10,... | collective-permute-start | bytes 294920 | tf_op jit(solution)/shard_map/ppermute | solution.py:197
  17.6 3.9 %collective-permute-start.5 = (bf16[3,4,16,256]{3,2,1,0:T(8,128)(2,1)S(1)}, bf16[3,4,16,256]{3,2,1,0:T(8,128)(2,1)S(1)}, u32[]{:S(2)}, u32[]{:S(2)}) collective-permute-start(bf16[3,4,16,256]{3,2,1,0:T(8,128)(2,1)S(1)} %get-tuple-element.98), channel_id=1, source_target_pairs={{4,8},{5,9},{6,10},{7,11},{8,4},{9,5},{10,6},{11,7},{20,24},{21,25... | collective-permute-start | bytes 294920 | tf_op jit(solution)/shard_map/ppermute | solution.py:197
  25.3 3.2 %collective-permute-start.6 = (f32[1,8,128]{2,1,0:T(8,128)S(1)}, f32[1,8,128]{2,1,0:T(8,128)S(1)}, u32[]{:S(2)}, u32[]{:S(2)}) collective-permute-start(f32[1,8,128]{2,1,0:T(8,128)S(1)} %get-tuple-element.111.mine), channel_id=1, source_target_pairs={{0,4},{1,5},{2,6},{3,7},{4,0},{5,1},{6,2},{7,3},{8,12},{9,13},{10,... | collective-permute-start | bytes 12296 | tf_op jit(solution)/shard_map/ppermute | solution.py:197

commit v12 on v11

--- a/solution.py
+++ b/solution.py
@@ -522,31 +522,6 @@
     return total, error
 
 
-def merge_kernel(mine, other, out_ref):
-    total, error = two_sum(mine[0], other[0])
-    lane = lax.broadcasted_iota(jnp.int32, (8, LANES), 1)
-    low = lax.rem(lane // QUARTER, 2) == 1
-    message = total + jnp.where(low, pltpu.roll(error, QUARTER, 1), 0.0)
-    for k in range(out_ref.shape[0]):
-        out_ref[k] = message
-
-
-def gather(message):
-    wides, narrows = lax.axis_size("wide"), lax.axis_size("narrow")
-    peers = wides // 2 * narrows
-    merged = pl.pallas_call(
-        merge_kernel,
-        out_shape=jax.ShapeDtypeStruct((peers, 8, LANES), jnp.float32),
-        in_specs=[VMEM] * 2,
-        out_specs=VMEM,
-        compiler_params=pltpu.CompilerParams(vmem_limit_bytes=2 * MIB),
-    )(message, swapped(message, 0, None))
-    groups = [
-        [w * narrows + n for w in range(core, wides, 2) for n in range(narrows)] for core in range(2)
-    ]
-    return lax.all_to_all(merged, AXES, 0, 0, axis_index_groups=groups, tiled=True)
-
-
 def state_shapes(b):
     rows, columns, depth = b.shape
     wide, narrow = rows + 2 * STEPS, columns + 2 * STEPS
@@ -677,6 +652,7 @@
 
 
 def on_device(right_side, conduct_half, reaction_half):
+    peers = lax.axis_size("wide") * lax.axis_size("narrow")
     *sent, b, c, r = messages(right_side, conduct_half, reaction_half)
     far, near = swapped(sent[1], 1, None), swapped(sent[0], 0, None)
     narrow_halos = [swapped(sent[2 + k], None, 1 - k) for k in range(2)]
@@ -689,8 +665,8 @@
     received = [*narrow_halos, diagonal[0], *saved]
     state, moments = onward(border_kernel, b, moments, received, state, moments.shape)
     received = [far, diagonal[1]]
-    state, moments = onward(late_kernel, b, moments, received, state, (1, 8, LANES))
-    gathered, fields = gather(moments), state[:STEPS]
+    state, moments = onward(late_kernel, b, moments, received, state, (peers, 8, LANES))
+    gathered, fields = lax.all_to_all(moments, AXES, 0, 0, tiled=True), state[:STEPS]
     solution, residual = combine(gathered, b, fields)
     return (solution, residual)
 

time: 41 us -> 39.7 us (0.968)
  starting transfers between devices: 13 us -> 10.5 us
  blocking collectives: 9.58 us -> 11.6 us
  waiting for transfers between devices: 0.94 us -> 0.11 us
    ppermute x7 -> x6, starting transfers between devices: 13 us -> 10.5 us  [swapped(): return lax.ppermute(array, AXES, pairs)]
    all_to_all x1, blocking collectives: 9.58 us -> 11.6 us  [on_device(): lax.all_to_all(moments, AXES, 0, 0, tiled=True)]
    ppermute x7 -> x6, waiting for transfers between devices: 0.94 us -> 0.11 us  [swapped(): return lax.ppermute(array, AXES, pairs)]
  transfers between devices with their start and end apart: 7 -> 6, of which waited for: 2 -> 1; matrix products, arithmetic and copies ran while one was open for 0% -> 0% of each run, Pallas kernels for 21% -> 21%
where the time goes in v12:
time: 39.7 us; the launch traced here: 39.5 us
  Pallas kernels  16.3 us (41%)
  blocking collectives  11.6 us (29%)
  starting transfers between devices  10.5 us (26%)
  between operations  0.89 us (2%)
    all_to_all x1, blocking collectives, on_device(): lax.all_to_all(moments, AXES, 0, 0, tiled=True)  11.6 us
    ppermute x6, starting transfers between devices, swapped(): return lax.ppermute(array, AXES, pairs)  10.5 us
    pallas_call x3, Pallas kernels, onward(): pl.pallas_call(kernel, out_shape=shapes, in_specs=[VMEM] * (others + coun...  9.71 us
    pallas_call x1, Pallas kernels, inner(): pl.pallas_call(inner_kernel, cost_estimate=pl.CostEstimate(flops=120 * b....  2.4 us
    pallas_call x1, Pallas kernels, combine(): pl.pallas_call(combine_kernel, out_shape=[jax.ShapeDtypeStruct(b.shape, j...  2.38 us
    pallas_call x1, Pallas kernels, messages(): pl.pallas_call(send_kernel, out_shape=outs + [pltpu.VMEM(a.shape, a.dtype...  1.73 us
  transfers between devices with their start and end apart: 6, of which 1 were waited for; matrix products, arithmetic and copies ran while one was open for 0% of the time, Pallas kernels for 21%

profile of v12, /device:TPU:0, one launch (start us, length us, event | category | flops | bytes accessed | tf_op | source)
XLA Modules:
  0.0 39.5 jit_solution(3334038175987099735)
XLA Ops:
  0.6 1.7 %shard_map.50 = (bf16[24,64,256]{2,1,0:T(8,128)(2,1)S(1)}, bf16[24,64,256]{2,1,0:T(8,128)(2,1)S(1)}, f32[2,16,8,256]{3,2,1,0:T(8,128)S(1)}, f32[2,16,8,256]{3,2,...) custom-call(f32[16,64,256]{2,1,0:T(8,128)} %refs_0_.1, ...), custom_call_target="tpu_custom_call" | custom-call | tf_op jit(solution)/shard_map/pallas_call | solution.py:128
  2.4 0.5 %collective-permute-start = (bf16[24,64,256]{2,1,0:T(8,128)(2,1)S(1)}, bf16[24,64,256]{2,1,0:T(8,128)(2,1)S(1)}, u32[]{:S(2)}, u32[]{:S(2)}) collective-permute-start(bf16[24,64,256]{2,1,0:T(8,128)(2,1)S(1)} %get-tuple-element.65), channel_id=1, source_target_pairs={{0,4},{1,5},{2,6},{3,7},{4,0},{5,1},{6,2},{7,3},{8,12},{9,13},{10,... | collective-permute-start | bytes 2359304 | tf_op jit(solution)/shard_map/ppermute | solution.py:197
  2.9 0.7 %collective-permute-start.4 = (bf16[24,64,256]{2,1,0:T(8,128)(2,1)S(1)}, bf16[24,64,256]{2,1,0:T(8,128)(2,1)S(1)}, u32[]{:S(2)}, u32[]{:S(2)}) collective-permute-start(bf16[24,64,256]{2,1,0:T(8,128)(2,1)S(1)} %get-tuple-element.97), channel_id=1, source_target_pairs={{4,8},{5,9},{6,10},{7,11},{8,4},{9,5},{10,6},{11,7},{20,24},{21,25... | collective-permute-start | bytes 2359304 | tf_op jit(solution)/shard_map/ppermute | solution.py:197
  3.6 0.7 %collective-permute-start.1 = (f32[2,16,8,256]{3,2,1,0:T(8,128)S(1)}, f32[2,16,8,256]{3,2,1,0:T(8,128)S(1)}, u32[]{:S(2)}, u32[]{:S(2)}) collective-permute-start(f32[2,16,8,256]{3,2,1,0:T(8,128)S(1)} %get-tuple-element.79), channel_id=1, source_target_pairs={{1,2},{2,1},{5,6},{6,5},{9,10},{10,9},{13,14},{14,13},{17,18},{18,... | collective-permute-start | bytes 786440 | tf_op jit(solution)/shard_map/ppermute | solution.py:197
  4.3 5.5 %collective-permute-start.2 = (f32[2,16,8,256]{3,2,1,0:T(8,128)S(1)}, f32[2,16,8,256]{3,2,1,0:T(8,128)S(1)}, u32[]{:S(2)}, u32[]{:S(2)}) collective-permute-start(f32[2,16,8,256]{3,2,1,0:T(8,128)S(1)} %get-tuple-element.80), channel_id=1, source_target_pairs={{0,1},{1,0},{2,3},{3,2},{4,5},{5,4},{6,7},{7,6},{8,9},{9,8},{10,11... | collective-permute-start | bytes 786440 | tf_op jit(solution)/shard_map/ppermute | solution.py:197
  9.8 2.4 %shard_map.51 = (f32[16,64,256]{2,1,0:T(8,128)S(1)}, f32[16,64,256]{2,1,0:T(8,128)S(1)}, f32[16,64,256]{2,1,0:T(8,128)S(1)}, f32[16,64,256]{2,1,0:T(8,128)S(1)},...) custom-call(f32[16,64,256]{2,1,0:T(8,128)S(1)} %get-tuple-element.61, ...), custom_call_target="tpu_custom_call" | custom-call | flops 31457280 | bytes 6291456 | tf_op jit(solution)/shard_map/pallas_call | solution.py:534
  12.2 0.0 collective-permute-done.w_in
  12.2 3.0 %shard_map.52 = (f32[16,64,256]{2,1,0:T(8,128)S(1)}, f32[16,64,256]{2,1,0:T(8,128)S(1)}, f32[16,64,256]{2,1,0:T(8,128)S(1)}, f32[16,64,256]{2,1,0:T(8,128)S(1)},...) custom-call(f32[16,64,256]{2,1,0:T(8,128)S(1)} %get-tuple-element.61, ...), custom_call_target="tpu_custom_call", output_to_operand_aliasing={{0}: (3, {}), {1}: (4, {}), {2}: (5, {}), {3}: (6, {}), {4}... | custom-call | flops 31457280 | bytes 6291456 | tf_op jit(solution)/shard_map/pallas_call | solution.py:551
  15.2 0.0 collective-permute-done.1.refs_0_
  15.2 0.0 collective-permute-done.2.refs_1_
  15.2 0.1 shard_map.53
  15.3 2.3 %collective-permute-start.3 = (bf16[3,4,16,256]{3,2,1,0:T(8,128)(2,1)S(1)}, bf16[3,4,16,256]{3,2,1,0:T(8,128)(2,1)S(1)}, u32[]{:S(2)}, u32[]{:S(2)}) collective-permute-start(bf16[3,4,16,256]{3,2,1,0:T(8,128)(2,1)S(1)} %get-tuple-element.81), channel_id=1, source_target_pairs={{0,4},{1,5},{2,6},{3,7},{4,0},{5,1},{6,2},{7,3},{8,12},{9,13},{10,... | collective-permute-start | bytes 294920 | tf_op jit(solution)/shard_map/ppermute | solution.py:197
  17.6 0.8 %collective-permute-start.5 = (bf16[3,4,16,256]{3,2,1,0:T(8,128)(2,1)S(1)}, bf16[3,4,16,256]{3,2,1,0:T(8,128)(2,1)S(1)}, u32[]{:S(2)}, u32[]{:S(2)}) collective-permute-start(bf16[3,4,16,256]{3,2,1,0:T(8,128)(2,1)S(1)} %get-tuple-element.98), channel_id=1, source_target_pairs={{4,8},{5,9},{6,10},{7,11},{8,4},{9,5},{10,6},{11,7},{20,24},{21,25... | collective-permute-start | bytes 294920 | tf_op jit(solution)/shard_map/ppermute | solution.py:197
  18.5 0.1 collective-permute-done.3.refs_2_
  18.6 3.0 %shard_map.54 = (f32[16,64,256]{2,1,0:T(8,128)S(1)}, f32[16,64,256]{2,1,0:T(8,128)S(1)}, f32[16,64,256]{2,1,0:T(8,128)S(1)}, f32[16,64,256]{2,1,0:T(8,128)S(1)},...) custom-call(f32[16,64,256]{2,1,0:T(8,128)S(1)} %get-tuple-element.61, ...), custom_call_target="tpu_custom_call", output_to_operand_aliasing={{0}: (7, {}), {1}: (8, {}), {2}: (9, {}), {3}: (10, {}), {4... | custom-call | flops 31457280 | bytes 6291456 | tf_op jit(solution)/shard_map/pallas_call | solution.py:551
  21.6 0.0 collective-permute-done.4.refs_0_
  21.6 0.0 collective-permute-done.5.refs_1_
  21.6 3.7 %shard_map.55 = (f32[16,64,256]{2,1,0:T(8,128)S(1)}, f32[16,64,256]{2,1,0:T(8,128)S(1)}, f32[16,64,256]{2,1,0:T(8,128)S(1)}, f32[16,64,256]{2,1,0:T(8,128)S(1)},...) custom-call(f32[16,64,256]{2,1,0:T(8,128)S(1)} %get-tuple-element.61, ...), custom_call_target="tpu_custom_call", output_to_operand_aliasing={{0}: (4, {}), {1}: (5, {}), {2}: (6, {}), {3}: (7, {}), {4}... | custom-call | flops 31457280 | bytes 6291456 | tf_op jit(solution)/shard_map/pallas_call | solution.py:551
  25.3 11.6 %all_to_all.5.m_ref = f32[16,8,128]{2,1,0:T(8,128)S(1)} all-to-all(f32[16,8,128]{2,1,0:T(8,128)S(1)} %get-tuple-element.111), channel_id=1, replica_groups=mesh['group'=2,'wide'=4,'narrow'=4] {'wide','narrow'}, dimensions={0} | all-to-all | bytes 131072 | tf_op jit(solution)/shard_map/all_to_all | solution.py:669
  36.9 2.4 %shard_map.56 = (f32[16,64,256]{2,1,0:T(8,128)}, f32[16,64,256]{2,1,0:T(8,128)}) custom-call(f32[16,8,128]{2,1,0:T(8,128)S(1)} %all_to_all.5.m_ref, f32[16,64,256]{2,1,0:T(8,128)S(1)} %get-tuple-element.61.b_ref, f32[16,64,256]{2,1,0:T(8,128)S(1)} %get-tuple-element.112.refs_0_, f32[16,64,256]{2,1,0:T(8,128)S(1)} %get-tuple-element.113.refs_1_, ...), custom_call_target="tpu_custom_call" | custom-call | tf_op jit(solution)/shard_map/pallas_call | solution.py:643
Async XLA Ops:
  2.4 9.8 %collective-permute-start = (bf16[24,64,256]{2,1,0:T(8,128)(2,1)S(1)}, bf16[24,64,256]{2,1,0:T(8,128)(2,1)S(1)}, u32[]{:S(2)}, u32[]{:S(2)}) collective-permute-start(bf16[24,64,256]{2,1,0:T(8,128)(2,1)S(1)} %get-tuple-element.65), channel_id=1, source_target_pairs={{0,4},{1,5},{2,6},{3,7},{4,0},{5,1},{6,2},{7,3},{8,12},{9,13},{10,... | collective-permute-start | bytes 2359304 | tf_op jit(solution)/shard_map/ppermute | solution.py:197
  2.9 18.7 %collective-permute-start.4 = (bf16[24,64,256]{2,1,0:T(8,128)(2,1)S(1)}, bf16[24,64,256]{2,1,0:T(8,128)(2,1)S(1)}, u32[]{:S(2)}, u32[]{:S(2)}) collective-permute-start(bf16[24,64,256]{2,1,0:T(8,128)(2,1)S(1)} %get-tuple-element.97), channel_id=1, source_target_pairs={{4,8},{5,9},{6,10},{7,11},{8,4},{9,5},{10,6},{11,7},{20,24},{21,25... | collective-permute-start | bytes 2359304 | tf_op jit(solution)/shard_map/ppermute | solution.py:197
  3.6 11.6 %collective-permute-start.1 = (f32[2,16,8,256]{3,2,1,0:T(8,128)S(1)}, f32[2,16,8,256]{3,2,1,0:T(8,128)S(1)}, u32[]{:S(2)}, u32[]{:S(2)}) collective-permute-start(f32[2,16,8,256]{3,2,1,0:T(8,128)S(1)} %get-tuple-element.79), channel_id=1, source_target_pairs={{1,2},{2,1},{5,6},{6,5},{9,10},{10,9},{13,14},{14,13},{17,18},{18,... | collective-permute-start | bytes 786440 | tf_op jit(solution)/shard_map/ppermute | solution.py:197
  4.3 10.9 %collective-permute-start.2 = (f32[2,16,8,256]{3,2,1,0:T(8,128)S(1)}, f32[2,16,8,256]{3,2,1,0:T(8,128)S(1)}, u32[]{:S(2)}, u32[]{:S(2)}) collective-permute-start(f32[2,16,8,256]{3,2,1,0:T(8,128)S(1)} %get-tuple-element.80), channel_id=1, source_target_pairs={{0,1},{1,0},{2,3},{3,2},{4,5},{5,4},{6,7},{7,6},{8,9},{9,8},{10,11... | collective-permute-start | bytes 786440 | tf_op jit(solution)/shard_map/ppermute | solution.py:197
  15.3 3.3 %collective-permute-start.3 = (bf16[3,4,16,256]{3,2,1,0:T(8,128)(2,1)S(1)}, bf16[3,4,16,256]{3,2,1,0:T(8,128)(2,1)S(1)}, u32[]{:S(2)}, u32[]{:S(2)}) collective-permute-start(bf16[3,4,16,256]{3,2,1,0:T(8,128)(2,1)S(1)} %get-tuple-element.81), channel_id=1, source_target_pairs={{0,4},{1,5},{2,6},{3,7},{4,0},{5,1},{6,2},{7,3},{8,12},{9,13},{10,... | collective-permute-start | bytes 294920 | tf_op jit(solution)/shard_map/ppermute | solution.py:197
  17.6 3.9 %collective-permute-start.5 = (bf16[3,4,16,256]{3,2,1,0:T(8,128)(2,1)S(1)}, bf16[3,4,16,256]{3,2,1,0:T(8,128)(2,1)S(1)}, u32[]{:S(2)}, u32[]{:S(2)}) collective-permute-start(bf16[3,4,16,256]{3,2,1,0:T(8,128)(2,1)S(1)} %get-tuple-element.98), channel_id=1, source_target_pairs={{4,8},{5,9},{6,10},{7,11},{8,4},{9,5},{10,6},{11,7},{20,24},{21,25... | collective-permute-start | bytes 294920 | tf_op jit(solution)/shard_map/ppermute | solution.py:197
